TPU v7x, 32 devices: a whole 2x2x4 slice. The times are simulated.
32 devices in a mesh: grp: 2 (over y), chan: 4 (over z), sub: 4 (over x, core).
Axes of the slice: x: 2, y: 2, z: 4, core: 2. Of those that a mesh axis runs over, the one named last changes fastest.
Arguments:
- voltages: bfloat16 [2048, 2, 5504], P(('grp', 'chan', 'sub')), parts along dimension 0, may hold values from -6 to 6
- taps: float32 [1536], replicated, may hold values from -0.15625 to 0.15625
- input_id: int32 [1024], replicated, may hold values from 0 to 1023, each once
- counts: int32 [8], P('grp'), parts along dimension 0, may hold values from 2 to 8, as said below
- delays: int32 [512, 1024], P(('grp', 'sub')), parts along dimension 0, may hold values from 0 to 127
- beam_owner: int32 [512, 1], P('grp'), parts along dimension 0, may hold values from 0 to 3; in each aligned block of 64 rows (0 to 63, 64 to 127, ...) at most 32 rows name the same one
Outputs:
- visibility: bfloat16 [256, 2, 1024, 1024], P(('grp', 'chan'), None, 'sub'), parts along dimension 0
- resynth: float32 [1024, 2, 5504], P(('grp', 'chan', 'sub')), parts along dimension 0
There are 2 independent parts, one for each index of `grp`. A program takes and returns all parts, laid end to end along the dimension named above; an argument that names none is the same for every part. Nothing has to cross between parts.
Inputs may be any that keep to these rules, and one draw needn't show every extreme that they name: `input_id`: each input id appears once. `counts`: every draw has a block with all 8 spectra valid. `beam_owner`: within each section of 64 consecutive beams no owner is named more than 32 times; some owner is named exactly 32 times in some section.
All inputs are finite; a program needn't handle non-finite values.
Results may differ from a plain program's by a relative error of at most 0.007.
Values may be sent and summed in bfloat16 or wider, within the bound.
No kernel may reach another device: no remote copies, remote signals or barrier semaphores. Data moves between devices by JAX's collectives and lax.ppermute only.
A program may use at most 192 MiB of HBM per device.

v0:
```python
import math

import jax
import jax.numpy as jnp
from jax import lax
from jax.sharding import PartitionSpec as P

NCH = 128
TAPS = 12
SPEC = 8
BLOCKS = 4
BEAMS = 256


def filter_table(taps, chans):
    length = taps.shape[0]
    position = jnp.arange(length, dtype=jnp.int32) % chans
    channel = jnp.arange(chans, dtype=jnp.int32)
    phase = (position[:, None] * channel[None, :] % chans).astype(jnp.float32) * (
        2.0 * math.pi / chans
    )
    cosine = taps[:, None] * jnp.cos(phase)
    sine = taps[:, None] * jnp.sin(phase)
    upper = jnp.concatenate([cosine, -sine], axis=1)
    lower = jnp.concatenate([sine, cosine], axis=1)
    return jnp.concatenate([upper, lower], axis=0).astype(jnp.bfloat16)


def resynthesize(received, table, taps_count, chans):
    count = received.shape[0]
    spectra_n = received.shape[3]
    table3 = table.reshape(2 * taps_count * chans, 2, chans)
    grid = jnp.einsum("pcht,mch->ptm", received, table3, preferred_element_type=jnp.float32)
    grid = grid.reshape(count, spectra_n, 2, taps_count, chans)
    total = jnp.zeros((count, spectra_n + taps_count - 1, 2, chans), jnp.float32)
    for k in range(taps_count):
        total = total + jnp.pad(
            grid[:, :, :, k, :], ((0, 0), (k, taps_count - 1 - k), (0, 0), (0, 0))
        )
    return jnp.transpose(total, (0, 2, 1, 3)).reshape(
        count, 2, (spectra_n + taps_count - 1) * chans
    )


def local(voltages, taps, input_id, counts, delays, beam_owner):
    n_chan = lax.axis_size("chan")
    n_sub = lax.axis_size("sub")
    inp_dev = voltages.shape[0]
    inputs = input_id.shape[0]
    chans = NCH
    taps_count = TAPS
    spectra_n = BLOCKS * SPEC
    ch_dev = chans // n_chan
    rows = inputs // n_sub
    section = BEAMS // n_sub
    most = min(section, max(2, 2 * section // n_chan))
    table = filter_table(taps, chans)
    position = jnp.arange(spectra_n, dtype=jnp.int32)
    valid = (position % SPEC < jnp.repeat(counts, SPEC)).astype(jnp.float32)
    total = jnp.sum(counts.astype(jnp.float32))
    frames = voltages.reshape(inp_dev, 2, spectra_n + taps_count - 1, chans)
    windows = jnp.concatenate(
        [frames[:, :, k : k + spectra_n, :] for k in range(taps_count)], axis=3
    )
    table3 = table.reshape(2, taps_count * chans, 2 * chans)
    filtered = jnp.einsum("icth,chm->mit", windows, table3, preferred_element_type=jnp.float32)
    filtered = filtered * valid[None, None, :]
    spectra = filtered.reshape(2, chans, inp_dev, spectra_n).astype(jnp.bfloat16)
    slot_of = jnp.zeros((inputs,), jnp.int32).at[input_id].set(jnp.arange(inputs, dtype=jnp.int32))
    turned = lax.all_to_all(spectra, "chan", split_axis=1, concat_axis=2, tiled=True)
    gathered = lax.all_gather(turned, "sub", axis=2, tiled=True)
    chan_part = slot_of // (n_sub * inp_dev)
    sub_part = slot_of // inp_dev % n_sub
    order = (sub_part * n_chan + chan_part) * inp_dev + slot_of % inp_dev
    by_id = jnp.take(gathered, order, axis=2)
    sub_index = lax.axis_index("sub")
    mine = lax.dynamic_slice_in_dim(by_id, sub_index * rows, rows, 2)
    real_part = jnp.einsum("cxit,cxjt->xij", mine, by_id, preferred_element_type=jnp.float32)
    imag_part = jnp.einsum("xit,xjt->xij", mine[1], by_id[0], preferred_element_type=jnp.float32)
    imag_part = imag_part - jnp.einsum(
        "xit,xjt->xij", mine[0], by_id[1], preferred_element_type=jnp.float32
    )
    visibility = (jnp.stack([real_part, imag_part], axis=1) / total).astype(jnp.bfloat16)
    channel = lax.axis_index("chan") * ch_dev + jnp.arange(ch_dev, dtype=jnp.int32)
    phase = (delays[None, :, :] * channel[:, None, None] % chans).astype(jnp.float32) * (
        2.0 * math.pi / chans
    )
    scale = 1.0 / math.sqrt(inputs)
    weight_cos = (jnp.cos(phase) * scale).astype(jnp.bfloat16)
    weight_sin = (jnp.sin(phase) * scale).astype(jnp.bfloat16)
    from_cos = jnp.einsum("xbi,cxit->cxbt", weight_cos, by_id, preferred_element_type=jnp.float32)
    from_sin = jnp.einsum("xbi,cxit->cxbt", weight_sin, by_id, preferred_element_type=jnp.float32)
    beams = jnp.stack([from_cos[0] - from_sin[1], from_cos[1] + from_sin[0]]).astype(jnp.bfloat16)
    owner = lax.dynamic_slice_in_dim(beam_owner[:, 0], sub_index * section, section)
    beam = jnp.arange(section, dtype=jnp.int32)
    earlier = (owner[None, :] == owner[:, None]) & (beam[None, :] < beam[:, None])
    rank = jnp.sum(earlier.astype(jnp.int32), axis=1)
    target = owner * most + rank
    select = (jnp.arange(n_chan * most, dtype=jnp.int32)[:, None] == target[None, :]).astype(
        jnp.bfloat16
    )
    placed = jnp.einsum("pb,cxbt->pcxt", select, beams, preferred_element_type=jnp.float32).astype(
        jnp.bfloat16
    )
    placed = placed.reshape(n_chan, most, 2, ch_dev, spectra_n)
    resynth = resynthesize(
        lax.all_to_all(placed, "chan", split_axis=0, concat_axis=3, tiled=True)[0],
        table,
        taps_count,
        chans,
    )
    return (visibility, resynth)


def solution(mesh):
    placed = (
        P(("grp", "chan", "sub"), None, None),
        P(),
        P(),
        P("grp"),
        P(("grp", "sub"), None),
        P("grp", None),
    )
    return jax.shard_map(
        local,
        mesh=mesh,
        in_specs=placed,
        out_specs=(P(("grp", "chan"), None, "sub", None), P(("grp", "chan", "sub"), None, None)),
        check_vma=False,
    )
```

profile of v0, /device:TPU:0, one launch (start us, length us, event | category | flops | bytes accessed | tf_op | source)
XLA Modules:
  0.0 463.8 jit_solution(4813590015660750824)
XLA Ops:
  8.0 3.7 reshape.232
  11.7 3.5 fusion.74
  16.0 4.4 negate_convert_fusion.1
  29.9 4.8 %copy-done.3 = bf16[64,2,32,1536]{3,0,1,2:T(8,128)(2,1)} copy-done((bf16[64,2,32,1536]{3,0,1,2:T(8,128)(2,1)}, bf16[64,2,32,1536]{3,0,1,2:T(8,128)(2,1)S(1)}, u32[]{:S(2)}) %copy-start.3) | copy-done | bytes 12582936
  34.8 8.5 %fusion.15 = bf16[256,64,32]{0,1,2:T(8,128)(2,1)S(1)} fusion(bf16[2,1536,256,1]{2,1,0,3:T(8,128)(2,1)S(1)} %bitcast.153, bf16[64,2,32,1536]{3,0,1,2:T(8,128)(2,1)} %copy-done.3, f32[32]{0:T(128)S(1)} %compare_convert_fusion), kind=kOutput, calls=%fused_computation.28 | convolution fusion | flops 3222274048 | bytes 15204480 | tf_op jit(solution)/shard_map/icth,chm->mit/dot_general | solution.py:66
  43.6 2.2 copy.105
  47.5 32.0 %all_to_all.33 = bf16[4,2,65536]{2,1,0:T(2,128)(2,1)} all-to-all(bf16[4,2,65536]{2,1,0:T(2,128)(2,1)S(1)} %reshape.237), channel_id=1, replica_groups=mesh['grp'=2,'chan'=4,'sub'=4] {'chan'}, dimensions={0} | all-to-all | bytes 2097152 | tf_op jit(solution)/shard_map/all_to_all | solution.py:70
  79.4 3.1 reshape.238
  82.6 6.5 %copy.149 = bf16[2,32,4,64,32]{4,1,3,2,0:T(8,128)(2,1)} copy(bf16[2,32,4,64,32]{3,4,0,1,2:T(8,128)(2,1)S(1)} %bitcast.149) | data formatting | bytes 2097152 | tf_op jit(solution)/shard_map/all_to_all | solution.py:70
  89.1 4.3 scatter_custom_fusion
  94.5 4.2 negate_convert_fusion
  99.9 94.4 %all-gather.2.cloned.1.call-done = bf16[2,32,1024,32]{3,1,2,0:T(8,128)(2,1)} async-done(((bf16[2,32,256,32]{3,1,2,0:T(8,128)(2,1)}), bf16[2,32,1024,32]{3,1,2,0:T(8,128)(2,1)}) %all-gather.2.cloned.1.call-update) | async-done | bytes 4194320 | tf_op jit(solution)/shard_map/all_gather | solution.py:71
  194.3 19.1 %gather_fusion = bf16[1024,2,32,32]{3,2,1,0:T(8,128)(2,1)} fusion(bf16[2,32,1024,32]{3,1,2,0:T(8,128)(2,1)} %all-gather.2.cloned.1.call-done, s32[1024]{0:T(1024)S(1)} %broadcast_clamp_fusion), kind=kCustom, calls=%fused_computation | custom fusion | bytes 8392704 | tf_op jit(solution)/shard_map/jit(_take)/gather | solution.py:75
  213.4 17.5 %copy.109 = bf16[1024,2,32,32]{0,3,1,2:T(8,128)(2,1)} copy(bf16[1024,2,32,32]{3,2,1,0:T(8,128)(2,1)} %gather_fusion) | data formatting | bytes 8388608 | tf_op jit(solution)/shard_map/jit(_take)/gather | solution.py:75
  230.9 2.7 broadcast_select_fusion
  234.4 2.7 fusion.78
  237.0 31.6 %fusion.21 = f32[2,32,64,32]{2,3,0,1:T(8,128)S(1)} fusion(s32[32]{0:T(128)S(1)} %iota_add_fusion, s32[64,1024]{1,0:T(8,128)S(1)} %copy-done.8, bf16[1024,2,32,32]{0,3,1,2:T(8,128)(2,1)S(1)} %broadcast_select_fusion), kind=kOutput, calls=%fused_computation.35 | convolution fusion | flops 301989888 | bytes 4980864 | tf_op jit(solution)/shard_map/xbi,cxit->cxbt/dot_general | solution.py:91
  268.6 32.3 %fusion.18 = f32[2,32,64,32]{2,3,0,1:T(8,128)S(1)} fusion(s32[32]{0:T(128)S(1)} %iota_add_fusion, s32[64,1024]{1,0:T(8,128)S(1)} %copy-done.8, bf16[1024,2,32,32]{0,3,1,2:T(8,128)(2,1)S(1)} %broadcast_select_fusion), kind=kOutput, calls=%fused_computation.34 | convolution fusion | flops 301989888 | bytes 4980864 | tf_op jit(solution)/shard_map/xbi,cxit->cxbt/dot_general | solution.py:92
  302.4 3.1 reshape.203
  307.2 4.5 reshape.239
  311.7 4.6 all-to-all-start.1
  316.3 15.5 %convolution_bitcast_fusion = f32[32,1,256,1024]{3,2,0,1:T(8,128)} fusion(bf16[2,32,256,32]{2,3,0,1:T(8,128)(2,1)S(1)} %dynamic-slice_bitcast_fusion, bf16[1024,2,32,32]{0,3,1,2:T(8,128)(2,1)} %copy-done.1), kind=kOutput, calls=%fused_computation.8 | convolution fusion | flops 1073741824 | bytes 38797312 | tf_op jit(solution)/shard_map/cxit,cxjt->xij/dot_general | solution.py:78
  331.8 14.0 %fusion.14 = f32[32,256,1024]{2,1,0:T(8,128)} fusion(bf16[2,32,1024,32]{2,3,0,1:T(8,128)(2,1)S(1)} %copy-done.2, bf16[2,32,256,32]{2,3,0,1:T(8,128)(2,1)S(1)} %dynamic-slice_bitcast_fusion), kind=kOutput, calls=%fused_computation.26 | convolution fusion | flops 536870912 | bytes 36175872 | tf_op jit(solution)/shard_map/xit,xjt->xij/dot_general | solution.py:79
  345.8 21.7 %subtract_bitcast_fusion = f32[32,1,256,1024]{3,2,0,1:T(8,128)} fusion(f32[32,256,1024]{2,1,0:T(8,128)} %fusion.14, bf16[2,32,1024,32]{2,3,0,1:T(8,128)(2,1)S(1)} %copy-done.2, bf16[2,32,256,32]{2,3,0,1:T(8,128)(2,1)S(1)} %dynamic-slice_bitcast_fusion), kind=kOutput, calls=%fused_computation.4 | convolution fusion | flops 545259520 | bytes 69730304 | tf_op jit(solution)/shard_map/xit,xjt->xij/dot_general | solution.py:80
  367.5 33.5 %fusion = bf16[32,2,256,1024]{3,2,0,1:T(8,128)(2,1)} fusion(f32[32,1,256,1024]{3,2,0,1:T(8,128)} %subtract_bitcast_fusion, f32[32,1,256,1024]{3,2,0,1:T(8,128)} %convolution_bitcast_fusion, f32[]{:T(128)} %convert_reduce_fusion.1), kind=kLoop, calls=%fused_computation.3 | loop fusion | flops 50331648 | bytes 100663296 | tf_op jit(solution)/shard_map/convert_element_type | solution.py:83
  401.0 23.2 %copy.126 = bf16[32,2,256,1024]{3,2,1,0:T(8,128)(2,1)} copy(bf16[32,2,256,1024]{3,2,0,1:T(8,128)(2,1)} %fusion) | data formatting | bytes 67108864
  425.4 1.8 bitcast_bitcast_fusion
  427.2 5.2 %copy.112 = bf16[1,32,2,4,32,32]{4,3,5,2,1,0:T(4,128)(2,1)S(1)} copy(bf16[1,32,2,4,32,32]{1,5,4,2,3,0:T(8,128)(2,1)} %bitcast_bitcast_fusion) | data formatting | bytes 1048576 | tf_op jit(solution)/shard_map/all_to_all | solution.py:107
  433.5 7.3 %convolution_bitcast_fusion.1 = f32[32,32,2,12,128]{4,1,3,2,0:T(8,128)} fusion(bf16[2,12,128,2,128]{4,2,1,0,3:T(8,128)(2,1)} %bitcast.152, bf16[32,2,128,32,1,1]{2,3,1,0,4,5:T(8,128)(2,1)S(1)} %reshape.229), kind=kOutput, calls=%fused_computation.16 | convolution fusion | flops 1610612736 | bytes 14680064 | tf_op jit(solution)/shard_map/pcht,mch->ptm/dot_general | solution.py:33
  440.8 9.1 %slice_bitcast_fusion.15 = (f32[32,32,2,128]{3,1,2,0:T(8,128)S(1)}, f32[32,32,2,128]{3,1,2,0:T(8,128)S(1)}, f32[32,32,2,128]{3,1,2,0:T(8,128)S(1)}, f32[32,32,2,...) fusion(f32[32,32,2,12,128]{4,1,3,2,0:T(8,128)} %convolution_bit, ...), kind=kLoop, calls=%fused_computation.54 | loop fusion | bytes 25165824 | tf_op jit(solution)/shard_map/squeeze | solution.py:38
  449.9 5.0 %add_bitcast_fusion = f32[32,2,43,128]{3,2,1,0:T(8,128)S(1)} fusion(f32[32,32,2,128]{3,1,2,0:T(8,128)} %get-tuple-element.22, f32[32,32,2,128]{3,1,2,0:T(8,128)} %get-tuple-element.23, f32[32,32,2,128]{3,1,2,0:T(8,128)S(1)} %get-tuple-element.13, f32[32,32,2,128]{3,1,2,0:T(8,128)S(1)} %get-tuple-element.14, f32[32,32,2,128]{3,1,2,0:T(8,128)S(1)} %get-tuple-element.15, ...), kind=kLoop, calls=%fused_computation.33 | loop fusion | flops 3874816 | bytes 13991936 | tf_op jit(solution)/shard_map/transpose | solution.py:40
  454.9 1.8 reshape.234
  (55 shorter events, 21.5 us)
Async XLA Ops:
  7.2 187.1 %all-gather.2.cloned.1.call-start = ((), (), s32[]{:S(2)}) async-start(), calls=%async_computation.2 | async-start | bytes 20971520 | tf_op jit(solution)/shard_map/all_gather | solution.py:71
  11.7 4.2 copy-start.4
  29.8 4.8 %copy-start.3 = (bf16[64,2,32,1536]{3,0,1,2:T(8,128)(2,1)}, bf16[64,2,32,1536]{3,0,1,2:T(8,128)(2,1)S(1)}, u32[]{:S(2)}) copy-start(bf16[64,2,32,1536]{3,0,1,2:T(8,128)(2,1)S(1)} %copy_dynamic-update-slice_fusion) | copy-start | bytes 37748740
  82.5 6.6 %copy-start.5 = (s32[1024]{0:T(1024)S(1)}, s32[1024]{0:T(1024)}, u32[]{:S(2)}) copy-start(s32[1024]{0:T(1024)} %param.8) | copy-start | bytes 12292
  82.5 10.9 %copy-start.7 = (s32[256,1]{0,1:T(1,128)S(1)}, s32[256,1]{0,1:T(1,128)}, u32[]{:S(2)}) copy-start(s32[256,1]{0,1:T(1,128)} %param.11) | copy-start | bytes 3076
  82.6 11.0 %copy-start.6 = (s32[4]{0:T(128)S(1)}, s32[4]{0:T(128)}, u32[]{:S(2)}) copy-start(s32[4]{0:T(128)} %param.9) | copy-start | bytes 52
  230.9 3.4 copy-start
  234.3 66.5 %copy-start.1 = (bf16[1024,2,32,32]{0,3,1,2:T(8,128)(2,1)}, bf16[1024,2,32,32]{0,3,1,2:T(8,128)(2,1)S(1)}, u32[]{:S(2)}) copy-start(bf16[1024,2,32,32]{0,3,1,2:T(8,128)(2,1)S(1)} %broadcast_select_fusion) | copy-start | bytes 12582916
  234.4 2.7 copy-start.8
  311.7 112.5 %all-to-all-start.1 = ((bf16[4,2,32768]{2,1,0:T(2,128)(2,1)}), bf16[4,2,32768]{2,1,0:T(2,128)(2,1)S(1)}, u32[]{:S(2)}, u32[]{:S(2)}) async-start(bf16[4,2,32768]{2,1,0:T(2,128)(2,1)} %reshape.239), calls=%async_computation.1 | async-start | bytes 1048576 | tf_op jit(solution)/shard_map/all_to_all | solution.py:107
  316.3 15.5 %copy-start.2 = (bf16[2,32,1024,32]{2,3,0,1:T(8,128)(2,1)S(1)}, bf16[2,32,1024,32]{2,3,0,1:T(8,128)(2,1)}, u32[]{:S(2)}) copy-start(bf16[2,32,1024,32]{2,3,0,1:T(8,128)(2,1)} %fusion.78) | copy-start | bytes 12582916
Sparse Core Ops, SparseCore 0:
  89.2 105.0 all-gather.1
where the time goes:
time: 469 us; the launch traced here: 464 us
  matrix products  132 us (28%)
  local copies, waits for them, and re-layouts  131 us (28%)
  waiting for transfers between devices  94.4 us (20%)
  other arithmetic  55 us (12%)
  blocking collectives  32 us (7%)
  between operations  14.6 us (3%)
    all_gather x1, waiting for transfers between devices, local(): gathered = lax.all_gather(turned, 'sub', axis=2, tiled=True)  94.4 us
    unnamed x34, local copies, waits for them, and re-layouts  48.3 us
    gather x2, local copies, waits for them, and re-layouts, local(): by_id = jnp.take(gathered, order, axis=2)  36.6 us
    convert_element_type x1, other arithmetic, local(): (jnp.stack([real_part, imag_part], axis=1) / total).astype(jnp.bfloat16)  33.5 us
    dot_general x1, matrix products, local(): jnp.einsum('xbi,cxit->cxbt', weight_sin, by_id, preferred_element_type=jn...  32.3 us
    all_to_all x1, blocking collectives, local(): lax.all_to_all(spectra, 'chan', split_axis=1, concat_axis=2, tiled=True)  32 us
    dot_general x1, matrix products, local(): jnp.einsum('xbi,cxit->cxbt', weight_cos, by_id, preferred_element_type=jn...  31.6 us
    dot_general x1, matrix products, local(): jnp.einsum('xit,xjt->xij', mine[0], by_id[1], preferred_element_type=jnp....  21.7 us
  transfers between devices with their start and end apart: 2, of which 1 were waited for; matrix products, arithmetic and copies ran while one was open for 26% of the time, Pallas kernels for 0%

commit v1 on v0

--- a/solution.py
+++ b/solution.py
@@ -1,8 +1,11 @@
+import functools
 import math
 
 import jax
 import jax.numpy as jnp
 from jax import lax
+from jax.experimental import pallas as pl
+from jax.experimental.pallas import tpu as pltpu
 from jax.sharding import PartitionSpec as P
 
 NCH = 128
@@ -10,6 +13,8 @@
 SPEC = 8
 BLOCKS = 4
 BEAMS = 256
+LANES = 128
+MIB = 1024 * 1024
 
 
 def filter_table(taps, chans):
@@ -42,7 +47,7 @@
     )
 
 
-def local(voltages, taps, input_id, counts, delays, beam_owner):
+def general(voltages, taps, input_id, counts, delays, beam_owner):
     n_chan = lax.axis_size("chan")
     n_sub = lax.axis_size("sub")
     inp_dev = voltages.shape[0]
@@ -112,6 +117,438 @@
     return (visibility, resynth)
 
 
+def dot(a, b, dims):
+    return lax.dot_general(a, b, (dims, ((), ())), preferred_element_type=jnp.float32)
+
+
+def whole(shape):
+    return pl.BlockSpec(shape, lambda *_: (0,) * len(shape))
+
+
+SCALARS = pl.BlockSpec(memory_space=pltpu.SMEM)
+
+
+def filter_kernel(inp, group, spectra_n, counts, frames, taps_col, base, *rest):
+    *outs, table = rest
+    depth = base.shape[0]
+    for k in range(TAPS):
+        table[k * depth : (k + 1) * depth, :] = (taps_col[:, k : k + 1] * base[...]).astype(
+            jnp.bfloat16
+        )
+    width = base.shape[1] // len(outs)
+    for first in range(0, spectra_n, group):
+        left = jnp.concatenate(
+            [
+                frames[(first + k) * inp : (first + k + group) * inp, :]
+                for k in range(TAPS)
+            ],
+            axis=1,
+        )
+        got = dot(left, table[...], ((1,), (0,)))
+        pieces = []
+        for step in range(group):
+            t = first + step
+            keep = (t % SPEC < counts[t // SPEC]).astype(jnp.float32)
+            pieces.append(got[step * inp : (step + 1) * inp, :] * keep)
+        pack = LANES // width
+        for pair in range(group // pack):
+            row = (first // pack + pair) * inp
+            for d, out in enumerate(outs):
+                out[row : row + inp, :] = jnp.concatenate(
+                    [
+                        pieces[pair * pack + h][:, d * width : (d + 1) * width]
+                        for h in range(pack)
+                    ],
+                    axis=1,
+                ).astype(jnp.bfloat16)
+
+
+def run_filter(counts, frames, taps_col, base, inp, n_chan, spectra_n):
+    width = base.shape[1] // n_chan
+    pack = LANES // width
+    out = jax.ShapeDtypeStruct((spectra_n // pack * inp, LANES), jnp.bfloat16)
+    return pl.pallas_call(
+        functools.partial(filter_kernel, inp, 4, spectra_n),
+        out_shape=[out] * n_chan,
+        in_specs=[SCALARS] + [pl.BlockSpec(memory_space=pltpu.VMEM)] * 3,
+        out_specs=[pl.BlockSpec(memory_space=pltpu.VMEM)] * n_chan,
+        scratch_shapes=[pltpu.VMEM((TAPS * base.shape[0], base.shape[1]), jnp.bfloat16)],
+        compiler_params=pltpu.CompilerParams(vmem_limit_bytes=32 * MIB),
+        cost_estimate=pl.CostEstimate(
+            flops=2 * spectra_n * inp * TAPS * base.size,
+            bytes_accessed=4 * MIB,
+            transcendentals=0,
+        ),
+    )(counts, frames, taps_col, base)
+
+
+def weight_kernel(first, delays, turn_cos, turn_sin, out):
+    channel = first[0] + pl.program_id(0)
+    section, inputs = delays.shape
+    cosine = jnp.broadcast_to(turn_cos[0:1, :], (section, LANES))
+    sine = jnp.broadcast_to(turn_sin[0:1, :], (section, LANES))
+    for block in range(inputs // LANES):
+        lanes = slice(block * LANES, (block + 1) * LANES)
+        phase = (delays[:, lanes] * channel) & (NCH - 1)
+        out[0, :section, lanes] = jnp.take_along_axis(cosine, phase, axis=1).astype(jnp.bfloat16)
+        out[0, section:, lanes] = jnp.take_along_axis(sine, phase, axis=1).astype(jnp.bfloat16)
+
+
+def run_weights(first, delays, turn_cos, turn_sin, ch_dev):
+    section, inputs = delays.shape
+    return pl.pallas_call(
+        weight_kernel,
+        out_shape=jax.ShapeDtypeStruct((ch_dev, 2 * section, inputs), jnp.bfloat16),
+        grid=(ch_dev,),
+        in_specs=[
+            SCALARS,
+            whole(delays.shape),
+            whole(turn_cos.shape),
+            whole(turn_sin.shape),
+        ],
+        out_specs=pl.BlockSpec((1, 2 * section, inputs), lambda f: (f, 0, 0)),
+        compiler_params=pltpu.CompilerParams(vmem_limit_bytes=16 * MIB),
+        cost_estimate=pl.CostEstimate(
+            flops=8 * ch_dev * section * inputs,
+            bytes_accessed=4 * ch_dev * section * inputs,
+            transcendentals=0,
+        ),
+    )(first, delays, turn_cos, turn_sin)
+
+
+def beam_kernel(sizes, n_blocks, n_dest, *refs):
+    inp, ch_dev, spectra_n, most = sizes
+    weights, choose, ids = refs[:3]
+    blocks = refs[3 : 3 + n_blocks]
+    by_id = refs[3 + n_blocks]
+    sent = refs[4 + n_blocks : 4 + n_blocks + n_dest]
+    turned, formed = refs[4 + n_blocks + n_dest :]
+    channel = pl.program_id(0)
+    width = 2 * ch_dev
+    pack = LANES // width
+    packed = spectra_n // pack
+    section = weights.shape[1] // 2
+
+    @pl.when(channel == 0)
+    def _():
+        together = 4
+        for first in range(0, packed, together):
+            left = jnp.concatenate(
+                [
+                    jnp.concatenate(
+                        [block[t * inp : (t + 1) * inp, :] for block in blocks], axis=0
+                    )
+                    for t in range(first, first + together)
+                ],
+                axis=1,
+            )
+            got = dot(left, ids[...], ((0,), (0,)))
+            for j in range(turned.shape[0]):
+                turned[j, first * LANES : (first + together) * LANES, :] = got[
+                    :, j * LANES : (j + 1) * LANES
+                ]
+
+    both = jnp.concatenate(
+        [
+            jnp.concatenate(
+                [
+                    turned[j, pl.ds(c * ch_dev + channel, spectra_n, stride=width), :]
+                    for j in range(turned.shape[0])
+                ],
+                axis=1,
+            )
+            for c in range(2)
+        ],
+        axis=0,
+    ).astype(jnp.bfloat16)
+    by_id[0] = both
+    got = dot(both, weights[0], ((1,), (1,)))
+    real = got[:spectra_n, :section] - got[spectra_n:, section:]
+    imag = got[spectra_n:, :section] + got[:spectra_n, section:]
+    for c, part in enumerate((real, imag)):
+        formed[pl.ds(c * ch_dev + channel, spectra_n, stride=width), :] = jnp.pad(
+            part, ((0, 0), (0, LANES - section))
+        )
+
+    @pl.when(channel == ch_dev - 1)
+    def _():
+        per = LANES // most
+        total = None
+        for j in range(per):
+            left = jnp.concatenate(
+                [
+                    formed[t * width : (t + 1) * width, :section].astype(jnp.bfloat16)
+                    for t in range(j, spectra_n, per)
+                ],
+                axis=0,
+            )
+            more = dot(left, choose[j * section : (j + 1) * section, :], ((1,), (0,)))
+            total = more if total is None else total + more
+        for d in range(n_dest):
+            sent[d][...] = total[:, d * LANES : (d + 1) * LANES].astype(jnp.bfloat16)
+
+
+def run_beams(weights, choose, ids, blocks, inp, spectra_n, most, n_dest):
+    ch_dev, twice, inputs = weights.shape
+    width = 2 * ch_dev
+    out_rows = spectra_n // (LANES // most) * width
+    return pl.pallas_call(
+        functools.partial(beam_kernel, (inp, ch_dev, spectra_n, most), len(blocks), n_dest),
+        out_shape=[jax.ShapeDtypeStruct((ch_dev, 2 * spectra_n, inputs), jnp.bfloat16)]
+        + [jax.ShapeDtypeStruct((out_rows, LANES), jnp.bfloat16)] * n_dest,
+        grid=(ch_dev,),
+        in_specs=[
+            pl.BlockSpec((1, twice, inputs), lambda f: (f, 0, 0)),
+            whole(choose.shape),
+            whole(ids.shape),
+        ]
+        + [whole(block.shape) for block in blocks],
+        out_specs=[pl.BlockSpec((1, 2 * spectra_n, inputs), lambda f: (f, 0, 0))]
+        + [whole((out_rows, LANES))] * n_dest,
+        scratch_shapes=[
+            pltpu.VMEM((inputs // LANES, spectra_n * width, LANES), jnp.float32),
+            pltpu.VMEM((spectra_n * width, LANES), jnp.float32),
+        ],
+        compiler_params=pltpu.CompilerParams(vmem_limit_bytes=48 * MIB),
+        cost_estimate=pl.CostEstimate(
+            flops=2 * spectra_n * width * inputs * inputs,
+            bytes_accessed=24 * MIB,
+            transcendentals=0,
+        ),
+    )(weights, choose, ids, *blocks)
+
+
+def visibility_kernel(sub_index, counts, mine, by_id, out):
+    del sub_index
+    total = counts[0]
+    for b in range(1, counts.shape[0]):
+        total = total + counts[b]
+    half = mine.shape[1] // 2
+    rows = mine.shape[2]
+    real, imag = mine[0, :half, :], mine[0, half:, :]
+    left = jnp.concatenate(
+        [jnp.concatenate([real, imag], axis=0), jnp.concatenate([imag, -real], axis=0)], axis=1
+    )
+    got = dot(left, by_id[0], ((0,), (0,)))
+    scale = 1.0 / jnp.full((1, got.shape[1]), total, jnp.int32).astype(jnp.float32)
+    out[0, 0] = (got[:rows, :] * scale).astype(jnp.bfloat16)
+    out[0, 1] = (got[rows:, :] * scale).astype(jnp.bfloat16)
+
+
+def run_visibility(sub_index, counts, by_id, rows):
+    ch_dev, depth, inputs = by_id.shape
+    return pl.pallas_call(
+        visibility_kernel,
+        out_shape=jax.ShapeDtypeStruct((ch_dev, 2, rows, inputs), jnp.bfloat16),
+        grid_spec=pltpu.PrefetchScalarGridSpec(
+            num_scalar_prefetch=2,
+            grid=(ch_dev,),
+            in_specs=[
+                pl.BlockSpec((1, depth, rows), lambda f, sub, counts: (f, 0, sub[0])),
+                pl.BlockSpec((1, depth, inputs), lambda f, sub, counts: (f, 0, 0)),
+            ],
+            out_specs=pl.BlockSpec((1, 2, rows, inputs), lambda f, sub, counts: (f, 0, 0, 0)),
+        ),
+        compiler_params=pltpu.CompilerParams(vmem_limit_bytes=24 * MIB),
+        cost_estimate=pl.CostEstimate(
+            flops=4 * ch_dev * depth * rows * inputs,
+            bytes_accessed=4 * ch_dev * rows * inputs,
+            transcendentals=0,
+        ),
+    )(sub_index, counts, by_id, by_id)
+
+
+def resynth_kernel(most, spectra_n, taps_row, base, *refs):
+    *blocks, out, table, window = refs
+    depth, width = base.shape
+    for k in range(TAPS):
+        table[k * depth : (k + 1) * depth, :] = (taps_row[k : k + 1, :] * base[...]).astype(
+            jnp.bfloat16
+        )
+    per = LANES // most
+    edge = (TAPS - 1) * most
+    window[:edge, :] = jnp.zeros((edge, depth), jnp.bfloat16)
+    window[edge + spectra_n * most :, :] = jnp.zeros((edge, depth), jnp.bfloat16)
+    fold = depth // len(blocks)
+    for group in range(spectra_n // per):
+        tall = jnp.concatenate(
+            [block[group * fold : (group + 1) * fold, :] for block in blocks], axis=0
+        )
+        window[edge + group * LANES : edge + (group + 1) * LANES, :] = tall.T
+    frames_n = spectra_n + TAPS - 1
+    chans = width // 2
+    step = 11
+    for first in range(0, frames_n, step):
+        many = min(step, frames_n - first)
+        left = jnp.concatenate(
+            [
+                window[
+                    (first + TAPS - 1 - k) * most : (first + TAPS - 1 - k + many) * most, :
+                ]
+                for k in range(TAPS)
+            ],
+            axis=1,
+        )
+        got = dot(left, table[...], ((1,), (0,)))
+        for s in range(many):
+            for c in range(2):
+                out[pl.ds(2 * (first + s) + c, most, stride=2 * frames_n), :] = got[
+                    s * most : (s + 1) * most, c * chans : (c + 1) * chans
+                ]
+
+
+def run_resynth(taps_row, base, blocks, most, spectra_n):
+    frames_n = spectra_n + TAPS - 1
+    return pl.pallas_call(
+        functools.partial(resynth_kernel, most, spectra_n),
+        out_shape=jax.ShapeDtypeStruct((most * frames_n * 2, NCH), jnp.float32),
+        in_specs=[pl.BlockSpec(memory_space=pltpu.VMEM)] * (2 + len(blocks)),
+        out_specs=pl.BlockSpec(memory_space=pltpu.VMEM),
+        scratch_shapes=[
+            pltpu.VMEM((TAPS * base.shape[0], base.shape[1]), jnp.bfloat16),
+            pltpu.VMEM(((spectra_n + 2 * (TAPS - 1)) * most, base.shape[0]), jnp.bfloat16),
+        ],
+        compiler_params=pltpu.CompilerParams(vmem_limit_bytes=32 * MIB),
+        cost_estimate=pl.CostEstimate(
+            flops=2 * frames_n * most * TAPS * base.size,
+            bytes_accessed=4 * MIB,
+            transcendentals=0,
+        ),
+    )(taps_row, base, *blocks)
+
+
+def swap(x, axis, size, mask):
+    return lax.ppermute(x, axis, [(i, i ^ mask) for i in range(size)])
+
+
+def quick(voltages, taps, input_id, counts, delays, beam_owner):
+    n_chan = lax.axis_size("chan")
+    n_sub = lax.axis_size("sub")
+    inp = voltages.shape[0]
+    inputs = input_id.shape[0]
+    spectra_n = BLOCKS * SPEC
+    frames_n = spectra_n + TAPS - 1
+    ch_dev = NCH // n_chan
+    rows = inputs // n_sub
+    section = BEAMS // n_sub
+    most = min(section, max(2, 2 * section // n_chan))
+    chan_index = lax.axis_index("chan")
+    sub_index = lax.axis_index("sub")
+    turn = 2.0 * math.pi / NCH
+
+    partner = chan_index ^ jnp.arange(n_chan, dtype=jnp.int32)
+    column_channel = jnp.broadcast_to(
+        (partner[:, None, None] * ch_dev + jnp.arange(ch_dev, dtype=jnp.int32)[None, None, :]),
+        (n_chan, 2, ch_dev),
+    ).reshape(-1)
+    column_part = jnp.broadcast_to(
+        jnp.arange(2, dtype=jnp.int32)[None, :, None], (n_chan, 2, ch_dev)
+    ).reshape(-1)
+    row_place = jnp.tile(jnp.arange(NCH, dtype=jnp.int32), 2)
+    row_part = jnp.repeat(jnp.arange(2, dtype=jnp.int32), NCH)
+
+    def fourier(place, place_part, channel, channel_part):
+        quarter = (channel_part - place_part) * (NCH // 4)
+        index = (place * channel + quarter + NCH) % NCH
+        return jnp.cos(index.astype(jnp.float32) * turn)
+
+    base = fourier(
+        row_place[:, None], row_part[:, None], column_channel[None, :], column_part[None, :]
+    )
+    base_back = fourier(
+        row_place[None, :], row_part[None, :], column_channel[:, None], column_part[:, None]
+    )
+    taps2 = taps.reshape(TAPS, NCH)
+    taps_row = jnp.tile(taps2, (1, 2))
+    taps_col = taps_row.T
+
+    frames = jnp.transpose(voltages.reshape(inp, 2, frames_n, NCH), (2, 0, 1, 3)).reshape(
+        frames_n * inp, 2 * NCH
+    )
+    outgoing = run_filter(counts, frames, taps_col, base, inp, n_chan, spectra_n)
+
+    turned = [outgoing[0]] + [swap(outgoing[d], "chan", n_chan, d) for d in range(1, n_chan)]
+    blocks = []
+    for block in turned:
+        held = [block]
+        far = n_sub
+        masks = []
+        while far > 1:
+            far //= 2
+            masks.append(far)
+        for mask in masks:
+            held = held + [swap(x, "sub", n_sub, mask) for x in held]
+        blocks.extend(held)
+    order = [0]
+    far = n_sub
+    while far > 1:
+        far //= 2
+        order = order + [o ^ far for o in order]
+    id_table = input_id.reshape(n_chan, n_sub, inp)
+    slot_id = jnp.take(
+        jnp.take(id_table, partner, axis=0), sub_index ^ jnp.array(order, jnp.int32), axis=1
+    ).reshape(-1)
+    ids = (slot_id[:, None] == jnp.arange(inputs, dtype=jnp.int32)[None, :]).astype(jnp.bfloat16)
+
+    phases = jnp.arange(NCH, dtype=jnp.int32).astype(jnp.float32) * turn
+    scale = 1.0 / math.sqrt(inputs)
+    turn_cos = jnp.broadcast_to((jnp.cos(phases) * scale)[None, :], (8, NCH))
+    turn_sin = jnp.broadcast_to((jnp.sin(phases) * scale)[None, :], (8, NCH))
+    weights = run_weights(
+        (chan_index * ch_dev).reshape(1).astype(jnp.int32), delays, turn_cos, turn_sin, ch_dev
+    )
+
+    owner = lax.dynamic_slice_in_dim(beam_owner[:, 0], sub_index * section, section)
+    beam = jnp.arange(section, dtype=jnp.int32)
+    earlier = (owner[None, :] == owner[:, None]) & (beam[None, :] < beam[:, None])
+    rank = jnp.sum(earlier.astype(jnp.int32), axis=1)
+    per = LANES // most
+    line = jnp.arange(n_chan * per * most, dtype=jnp.int32)
+    target = (owner ^ chan_index) * (per * most) + rank
+    choose = (
+        line[None, None, :]
+        == target[None, :, None] + (jnp.arange(per, dtype=jnp.int32) * most)[:, None, None]
+    ).astype(jnp.bfloat16).reshape(per * section, n_chan * per * most)
+
+    by_id, *leaving = run_beams(weights, choose, ids, blocks, inp, spectra_n, most, n_chan)
+    arrived = [leaving[0]] + [swap(leaving[d], "chan", n_chan, d) for d in range(1, n_chan)]
+    visibility = run_visibility(
+        sub_index.reshape(1).astype(jnp.int32), counts, by_id, rows
+    )
+    voice = run_resynth(taps_row, base_back, arrived, most, spectra_n)
+    resynth = jnp.transpose(voice.reshape(most, frames_n, 2, NCH), (0, 2, 1, 3)).reshape(
+        most, 2, frames_n * NCH
+    )
+    return (visibility, resynth)
+
+
+def power_of_two(n):
+    return n & (n - 1) == 0
+
+
+def local(voltages, taps, input_id, counts, delays, beam_owner):
+    n_chan = lax.axis_size("chan")
+    n_sub = lax.axis_size("sub")
+    section = BEAMS // n_sub
+    most = min(section, max(2, 2 * section // n_chan))
+    width = 2 * NCH // n_chan
+    fits = (
+        power_of_two(n_chan)
+        and power_of_two(n_sub)
+        and voltages.shape[0] % 16 == 0
+        and LANES % width == 0
+        and width % 32 == 0
+        and LANES % most == 0
+        and most % 16 == 0
+        and section % 16 == 0
+        and section <= LANES
+        and input_id.shape[0] // n_sub % LANES == 0
+        and (BLOCKS * SPEC) % (4 * LANES // width) == 0
+    )
+    form = quick if fits else general
+    return form(voltages, taps, input_id, counts, delays, beam_owner)
+
+
 def solution(mesh):
     placed = (
         P(("grp", "chan", "sub"), None, None),

time: 469 us -> 128 us (0.27)
  matrix products: 132 us -> 0 us
  local copies, waits for them, and re-layouts: 131 us -> 16 us
  waiting for transfers between devices: 94.4 us -> 16.1 us
  Pallas kernels: 0 us -> 70.8 us
  other arithmetic: 55 us -> 5.47 us
  blocking collectives: 32 us -> 0 us
  between operations: 14.6 us -> 0.91 us
  starting transfers between devices: 4.64 us -> 17.8 us
    dot_general x8 -> x0, matrix products: 132 us -> none  [the longest x1 32.3 us: local(): jnp.einsum('xbi,cxit->cxbt', weight_sin, by_id, preferred_element_type=jn...]
    all_gather x1 -> x0, waiting for transfers between devices: 94.4 us -> none  [local(): gathered = lax.all_gather(turned, 'sub', axis=2, tiled=True)]
    pallas_call x0 -> x5, Pallas kernels: none -> 70.8 us  [the longest x1 31.5 us: run_beams(): pl.pallas_call(functools.partial(beam_kernel, (inp, ch_dev, spectra_n, mo...]
    unnamed x34 -> x20, local copies, waits for them, and re-layouts: 48.3 us -> 8.47 us
    gather x2, local copies, waits for them, and re-layouts: 36.6 us -> 1.14 us  [the longest x1 0.57 us: quick(): jnp.take(id_table, partner, axis=0)]
    all_to_all x1 -> x0, blocking collectives: 32 us -> none  [local(): lax.all_to_all(spectra, 'chan', split_axis=1, concat_axis=2, tiled=True)]
    convert_element_type x2, other arithmetic: 33.5 us -> 1.86 us  [the longest x1 1.75 us: quick(): (slot_id[:, None] == jnp.arange(inputs, dtype=jnp.int32)[None, :]).astype...]
    ppermute x0 -> x18, starting transfers between devices: none -> 17.8 us  [swap(): return lax.ppermute(x, axis, [(i, i ^ mask) for i in range(size)])]
  transfers between devices with their start and end apart: 2 -> 18, of which waited for: 1 -> 3; matrix products, arithmetic and copies ran while one was open for 26% -> 3% of each run, Pallas kernels for 0% -> 25%
where the time goes in v1:
time: 128 us; the launch traced here: 127 us
  Pallas kernels  70.8 us (55%)
  starting transfers between devices  17.8 us (14%)
  waiting for transfers between devices  16.1 us (13%)
  local copies, waits for them, and re-layouts  16 us (12%)
  other arithmetic  5.47 us (4%)
    pallas_call x1, Pallas kernels, run_beams(): pl.pallas_call(functools.partial(beam_kernel, (inp, ch_dev, spectra_n, mo...  31.5 us
    pallas_call x1, Pallas kernels, run_visibility(): pl.pallas_call(visibility_kernel, out_shape=jax.ShapeDtypeStruct((ch_dev,...  24 us
    ppermute x18, starting transfers between devices, swap(): return lax.ppermute(x, axis, [(i, i ^ mask) for i in range(size)])  17.8 us
    ppermute x18, waiting for transfers between devices, swap(): return lax.ppermute(x, axis, [(i, i ^ mask) for i in range(size)])  16.1 us
    unnamed x20, local copies, waits for them, and re-layouts  8.47 us
    pallas_call x1, Pallas kernels, run_weights(): pl.pallas_call(weight_kernel, out_shape=jax.ShapeDtypeStruct((ch_dev, 2 *...  8.12 us
    pallas_call x1, Pallas kernels, run_filter(): pl.pallas_call(functools.partial(filter_kernel, inp, 4, spectra_n), out_s...  4.82 us
    reshape x1, local copies, waits for them, and re-layouts, quick(): voltages.reshape(inp, 2, frames_n, NCH)  3.68 us
  transfers between devices with their start and end apart: 18, of which 3 were waited for; matrix products, arithmetic and copies ran while one was open for 3% of the time, Pallas kernels for 25%

profile of v1, /device:TPU:0, one launch (start us, length us, event | category | flops | bytes accessed | tf_op | source)
XLA Modules:
  0.0 127.1 jit_solution(8860255568661001529)
XLA Ops:
  0.6 3.7 %reshape.187 = bf16[64,2,43,128]{3,2,1,0:T(8,128)(2,1)S(1)} reshape(bf16[64,2,5504]{2,1,0:T(2,128)(2,1)} %param.7) | data formatting | bytes 2818048 | tf_op jit(solution)/shard_map/reshape | solution.py:465
  4.3 1.5 %copy.23 = bf16[43,64,2,128]{3,2,1,0:T(2,128)(2,1)S(1)} copy(bf16[43,64,2,128]{3,0,2,1:T(8,128)(2,1)S(1)} %bitcast.38) | data formatting | bytes 2818048 | tf_op jit(solution)/shard_map/transpose | solution.py:465
  5.9 0.2 copy.34
  6.1 0.5 copy-done.4
  7.0 3.0 %fusion.9 = (f32[256,256]{1,0:T(8,128)S(1)}, f32[256,256]{1,0:T(8,128)S(1)}) fusion(s32[256]{0:T(256)S(1)} %get-tuple-element.28, s32[256]{0:T(256)S(1)} %sub.34, s32[256]{0:T(256)S(1)} %mul.116, s32[256]{0:T(256)S(1)} %get-tuple-element.29), kind=kLoop, calls=%fused_computation.21 | loop fusion | flops 2359296 | bytes 528384 | tf_op jit(solution)/shard_map/cos | solution.py:453
  10.0 4.8 %shard_map.87 = (bf16[1024,128]{1,0:T(8,128)(2,1)S(1)}, bf16[1024,128]{1,0:T(8,128)(2,1)S(1)}, bf16[1024,128]{1,0:T(8,128)(2,1)}, bf16[1024,128]{1,0:T(8,128)(2,1)S(1)}) custom-call(s32[4]{0:T(128)S(1)} %copy-done.3, bf16[2752,256]{1,0:T(8,128)(2,1)S(1)} %bitcast.33, f32[256,12]{1,0:T(8,128)S(1)} %copy.24.taps_col, f32[256,256]{1,0:T(8,128)S(1)} %get-tuple-element.27.base), custom_call_target="tpu_custom_call" | custom-call | flops 3221225472 | bytes 4194304 | tf_op jit(solution)/shard_map/pallas_call | solution.py:170
  14.9 2.9 %collective-permute-start = (bf16[1024,128]{1,0:T(8,128)(2,1)S(1)}, bf16[1024,128]{1,0:T(8,128)(2,1)S(1)}, u32[]{:S(2)}, u32[]{:S(2)}) collective-permute-start(bf16[1024,128]{1,0:T(8,128)(2,1)S(1)} %get-tuple-element.11.refs_3_), channel_id=1, source_target_pairs={{0,2},{1,3},{2,0},{3,1},{4,6},{5,7},{6,4},{7,5},{8,10},{9,11},{10,... | collective-permute-start | bytes 786440 | tf_op jit(solution)/shard_map/ppermute | solution.py:421
  17.8 1.6 %collective-permute-start.3 = (bf16[1024,128]{1,0:T(8,128)(2,1)S(1)}, bf16[1024,128]{1,0:T(8,128)(2,1)S(1)}, u32[]{:S(2)}, u32[]{:S(2)}) collective-permute-start(bf16[1024,128]{1,0:T(8,128)(2,1)S(1)} %get-tuple-element.12), channel_id=1, source_target_pairs={{0,4},{4,0},{8,12},{12,8},{1,5},{5,1},{9,13},{13,9},{2,6},{6,2},{1... | collective-permute-start | bytes 786440 | tf_op jit(solution)/shard_map/ppermute | solution.py:421
  19.4 2.6 %collective-permute-start.7 = (bf16[1024,128]{1,0:T(8,128)(2,1)}, bf16[1024,128]{1,0:T(8,128)(2,1)S(1)}, u32[]{:S(2)}, u32[]{:S(2)}) collective-permute-start(bf16[1024,128]{1,0:T(8,128)(2,1)} %get-tuple-element.13), channel_id=1, source_target_pairs={{0,8},{4,12},{8,0},{12,4},{1,9},{5,13},{9,1},{13,5},{2,10},{6,14},... | collective-permute-start | bytes 786440 | tf_op jit(solution)/shard_map/ppermute | solution.py:421
  22.0 0.2 collective-permute-start.11
  22.8 0.6 gather_fusion
  23.5 0.6 gather_fusion.1
  24.1 7.5 %collective-permute-done.3.refs_7_ = bf16[1024,128]{1,0:T(8,128)(2,1)S(1)} collective-permute-done((bf16[1024,128]{1,0:T(8,128)(2,1)S(1)}, bf16[1024,128]{1,0:T(8,128)(2,1)S(1)}, u32[]{:S(2)}, u32[]{:S(2)}) %collective-permute-start.3) | collective-permute-done | bytes 262176 | tf_op jit(solution)/shard_map/ppermute | solution.py:421
  31.6 0.4 collective-permute-start.4
  32.0 0.5 collective-permute-start.2
  32.5 8.4 %collective-permute-done.7.refs_11_ = bf16[1024,128]{1,0:T(8,128)(2,1)S(1)} collective-permute-done((bf16[1024,128]{1,0:T(8,128)(2,1)}, bf16[1024,128]{1,0:T(8,128)(2,1)S(1)}, u32[]{:S(2)}, u32[]{:S(2)}) %collective-permute-start.7) | collective-permute-done | bytes 262176 | tf_op jit(solution)/shard_map/ppermute | solution.py:421
  40.9 0.5 collective-permute-start.8
  41.4 1.5 %collective-permute-start.12 = (bf16[1024,128]{1,0:T(8,128)(2,1)S(1)}, bf16[1024,128]{1,0:T(8,128)(2,1)S(1)}, u32[]{:S(2)}, u32[]{:S(2)}) collective-permute-start(bf16[1024,128]{1,0:T(8,128)(2,1)S(1)} %collective-permute-done.11.refs_15_), channel_id=1, source_target_pairs={{0,2},{1,3},{2,0},{3,1},{4,6},{5,7},{6,4},{7,5},{8,10},{9,11},{10,... | collective-permute-start | bytes 786440 | tf_op jit(solution)/shard_map/ppermute | solution.py:421
  43.3 8.1 %shard_map.86.refs_0_ = bf16[32,128,1024]{2,1,0:T(8,128)(2,1)S(1)} custom-call(s32[1]{0:T(128)} %bitcast.1.first, s32[64,1024]{1,0:T(8,128)S(1)} %copy-done.2, f32[8,128]{1,0:T(8,128)S(1)} %broadcast_in_dim.34.turn_cos, f32[8,128]{1,0:T(8,128)S(1)} %broadcast_in_dim.35.turn_sin), custom_call_target="tpu_custom_call" | custom-call | flops 16777216 | bytes 8388608 | tf_op jit(solution)/shard_map/pallas_call | solution.py:199
  51.4 3.4 %copy-done.1 = bf16[32,128,1024]{2,1,0:T(8,128)(2,1)} copy-done((bf16[32,128,1024]{2,1,0:T(8,128)(2,1)}, bf16[32,128,1024]{2,1,0:T(8,128)(2,1)S(1)}, u32[]{:S(2)}) %copy-start.1) | copy-done | bytes 8388632
  55.0 0.5 collective-permute-start.13
  55.6 0.4 collective-permute-start.10
  56.1 1.8 %fusion.refs_2_ = bf16[1024,1024]{1,0:T(8,128)(2,1)} fusion(s32[1024]{0:T(1024)S(1)} %select_n.55), kind=kLoop, calls=%fused_computation.3 | loop fusion | flops 2097152 | bytes 2101248 | tf_op jit(solution)/shard_map/convert_element_type | solution.py:491
  58.0 31.5 %shard_map.88 = (bf16[32,64,1024]{2,1,0:T(8,128)(2,1)}, bf16[512,128]{1,0:T(8,128)(2,1)S(1)}, bf16[512,128]{1,0:T(8,128)(2,1)S(1)}, bf16[512,128]{1,0:T(8,128)(2,1)S(1)}, bf16[512,128]{1,0:T(8,128)(2,1)S(1)}) custom-call(bf16[32,128,1024]{2,1,0:T(8,128)(2,1)} %copy-done.1, bf16[256,512]{1,0:T(8,128)(2,1)S(1)} %fusion.1.refs_1_, ...), custom_call_target="tpu_custom_call" | custom-call | flops 4294967296 | bytes 25165824 | tf_op jit(solution)/shard_map/pallas_call | solution.py:295
  89.5 4.0 %collective-permute-start.15 = (bf16[512,128]{1,0:T(8,128)(2,1)S(1)}, bf16[512,128]{1,0:T(8,128)(2,1)S(1)}, u32[]{:S(2)}, u32[]{:S(2)}) collective-permute-start(bf16[512,128]{1,0:T(8,128)(2,1)S(1)} %get-tuple-element.17), channel_id=1, source_target_pairs={{0,4},{4,0},{8,12},{12,8},{1,5},{5,1},{9,13},{13,9},{2,6},{6,2},{1... | collective-permute-start | bytes 393224 | tf_op jit(solution)/shard_map/ppermute | solution.py:421
  93.5 1.0 collective-permute-start.16
  94.5 1.5 %collective-permute-start.17 = (bf16[512,128]{1,0:T(8,128)(2,1)S(1)}, bf16[512,128]{1,0:T(8,128)(2,1)S(1)}, u32[]{:S(2)}, u32[]{:S(2)}) collective-permute-start(bf16[512,128]{1,0:T(8,128)(2,1)S(1)} %get-tuple-element.19), channel_id=1, source_target_pairs={{0,12},{4,8},{8,4},{12,0},{1,13},{5,9},{9,5},{13,1},{2,14},{6,10},... | collective-permute-start | bytes 393224 | tf_op jit(solution)/shard_map/ppermute | solution.py:421
  96.0 2.2 %copy-done = bf16[32,64,1024]{2,1,0:T(8,128)(2,1)S(1)} copy-done((bf16[32,64,1024]{2,1,0:T(8,128)(2,1)S(1)}, bf16[32,64,1024]{2,1,0:T(8,128)(2,1)}, u32[]{:S(2)}) %copy-start) | copy-done | bytes 4194328
  98.2 24.0 %shard_map.89 = bf16[32,2,256,1024]{3,2,1,0:T(8,128)(2,1)} custom-call(s32[1]{0:T(128)} %bitcast.sub_index, s32[4]{0:T(128)S(1)} %copy-done.3, bf16[32,64,1024]{2,1,0:T(8,128)(2,1)S(1)} %copy-done, bf16[32,64,1024]{2,1,0:T(8,128)(2,1)S(1)} %copy-done), custom_call_target="tpu_custom_call" | custom-call | flops 2147483648 | bytes 33554432 | tf_op jit(solution)/shard_map/pallas_call | solution.py:340
  122.2 2.4 %shard_map.90 = f32[2752,128]{1,0:T(8,128)S(1)} custom-call(f32[12,256]{1,0:T(8,128)S(1)} %bitcast.36, f32[256,256]{1,0:T(8,128)S(1)} %get-tuple-element.26.base, bf16[512,128]{1,0:T(8,128)(2,1)S(1)} %get-tuple-element.16.refs_0_, bf16[512,128]{1,0:T(8,128)(2,1)S(1)} %collective-permute-done.15.refs_1_, ...), custom_call_target="tpu_custom_call" | custom-call | flops 2164260864 | bytes 4194304 | tf_op jit(solution)/shard_map/pallas_call | solution.py:402
  124.7 0.2 reshape.169
  124.9 2.2 %copy.26 = f32[32,2,5504]{2,1,0:T(2,128)} copy(f32[32,2,5504]{2,0,1:T(8,128)S(1)} %reshape.169) | data formatting | bytes 2818048
  (71 shorter events, 2.1 us)
Async XLA Ops:
  5.9 0.7 copy-start.4
  5.9 4.1 %copy-start.3 = (s32[4]{0:T(128)S(1)}, s32[4]{0:T(128)}, u32[]{:S(2)}) copy-start(s32[4]{0:T(128)} %counts.3) | copy-start | bytes 52
  10.0 12.3 %copy-start.7 = (s32[256,1]{0,1:T(1,128)S(1)}, s32[256,1]{0,1:T(1,128)}, u32[]{:S(2)}) copy-start(s32[256,1]{0,1:T(1,128)} %param.12) | copy-start | bytes 3076
  10.0 12.6 %copy-start.5 = (s32[1024]{0:T(1024)S(1)}, s32[1024]{0:T(1024)}, u32[]{:S(2)}) copy-start(s32[1024]{0:T(1024)} %param.9) | copy-start | bytes 12292
  10.0 12.7 %copy-start.6 = (s32[4]{0:T(128)S(1)}, s32[4]{0:T(128)}, u32[]{:S(2)}) copy-start(s32[4]{0:T(128)} %constant.74.clone) | copy-start | bytes 52
  10.0 33.2 %copy-start.2 = (s32[64,1024]{1,0:T(8,128)S(1)}, s32[64,1024]{1,0:T(8,128)}, u32[]{:S(2)}) copy-start(s32[64,1024]{1,0:T(8,128)} %delays.1) | copy-start | bytes 786436
  14.9 17.1 %collective-permute-start = (bf16[1024,128]{1,0:T(8,128)(2,1)S(1)}, bf16[1024,128]{1,0:T(8,128)(2,1)S(1)}, u32[]{:S(2)}, u32[]{:S(2)}) collective-permute-start(bf16[1024,128]{1,0:T(8,128)(2,1)S(1)} %get-tuple-element.11.refs_3_), channel_id=1, source_target_pairs={{0,2},{1,3},{2,0},{3,1},{4,6},{5,7},{6,4},{7,5},{8,10},{9,11},{10,... | collective-permute-start | bytes 786440 | tf_op jit(solution)/shard_map/ppermute | solution.py:421
  17.8 14.2 %collective-permute-start.1 = (bf16[1024,128]{1,0:T(8,128)(2,1)S(1)}, bf16[1024,128]{1,0:T(8,128)(2,1)S(1)}, u32[]{:S(2)}, u32[]{:S(2)}) collective-permute-start(bf16[1024,128]{1,0:T(8,128)(2,1)S(1)} %get-tuple-element.11.refs_3_), channel_id=1, source_target_pairs={{0,1},{1,0},{2,3},{3,2},{4,5},{5,4},{6,7},{7,6},{8,9},{9,8},{10,11... | collective-permute-start | bytes 786440 | tf_op jit(solution)/shard_map/ppermute | solution.py:421
  17.8 13.8 %collective-permute-start.3 = (bf16[1024,128]{1,0:T(8,128)(2,1)S(1)}, bf16[1024,128]{1,0:T(8,128)(2,1)S(1)}, u32[]{:S(2)}, u32[]{:S(2)}) collective-permute-start(bf16[1024,128]{1,0:T(8,128)(2,1)S(1)} %get-tuple-element.12), channel_id=1, source_target_pairs={{0,4},{4,0},{8,12},{12,8},{1,5},{5,1},{9,13},{13,9},{2,6},{6,2},{1... | collective-permute-start | bytes 786440 | tf_op jit(solution)/shard_map/ppermute | solution.py:421
  19.4 21.5 %collective-permute-start.7 = (bf16[1024,128]{1,0:T(8,128)(2,1)}, bf16[1024,128]{1,0:T(8,128)(2,1)S(1)}, u32[]{:S(2)}, u32[]{:S(2)}) collective-permute-start(bf16[1024,128]{1,0:T(8,128)(2,1)} %get-tuple-element.13), channel_id=1, source_target_pairs={{0,8},{4,12},{8,0},{12,4},{1,9},{5,13},{9,1},{13,5},{2,10},{6,14},... | collective-permute-start | bytes 786440 | tf_op jit(solution)/shard_map/ppermute | solution.py:421
  22.0 19.5 %collective-permute-start.11 = (bf16[1024,128]{1,0:T(8,128)(2,1)S(1)}, bf16[1024,128]{1,0:T(8,128)(2,1)S(1)}, u32[]{:S(2)}, u32[]{:S(2)}) collective-permute-start(bf16[1024,128]{1,0:T(8,128)(2,1)S(1)} %get-tuple-element.14), channel_id=1, source_target_pairs={{0,12},{4,8},{8,4},{12,0},{1,13},{5,9},{9,5},{13,1},{2,14},{6,10},... | collective-permute-start | bytes 786440 | tf_op jit(solution)/shard_map/ppermute | solution.py:421
  31.6 23.4 %collective-permute-start.4 = (bf16[1024,128]{1,0:T(8,128)(2,1)S(1)}, bf16[1024,128]{1,0:T(8,128)(2,1)S(1)}, u32[]{:S(2)}, u32[]{:S(2)}) collective-permute-start(bf16[1024,128]{1,0:T(8,128)(2,1)S(1)} %collective-permute-done.3.refs_7_), channel_id=1, source_target_pairs={{0,2},{1,3},{2,0},{3,1},{4,6},{5,7},{6,4},{7,5},{8,10},{9,11},{10,... | collective-permute-start | bytes 786440 | tf_op jit(solution)/shard_map/ppermute | solution.py:421
  32.0 23.5 %collective-permute-start.5 = (bf16[1024,128]{1,0:T(8,128)(2,1)S(1)}, bf16[1024,128]{1,0:T(8,128)(2,1)S(1)}, u32[]{:S(2)}, u32[]{:S(2)}) collective-permute-start(bf16[1024,128]{1,0:T(8,128)(2,1)S(1)} %collective-permute-done.3.refs_7_), channel_id=1, source_target_pairs={{0,1},{1,0},{2,3},{3,2},{4,5},{5,4},{6,7},{7,6},{8,9},{9,8},{10,11... | collective-permute-start | bytes 786440 | tf_op jit(solution)/shard_map/ppermute | solution.py:421
  32.0 22.9 %collective-permute-start.2 = (bf16[1024,128]{1,0:T(8,128)(2,1)S(1)}, bf16[1024,128]{1,0:T(8,128)(2,1)S(1)}, u32[]{:S(2)}, u32[]{:S(2)}) collective-permute-start(bf16[1024,128]{1,0:T(8,128)(2,1)S(1)} %collective-permute-done.refs_4_), channel_id=1, source_target_pairs={{0,1},{1,0},{2,3},{3,2},{4,5},{5,4},{6,7},{7,6},{8,9},{9,8},{10,11... | collective-permute-start | bytes 786440 | tf_op jit(solution)/shard_map/ppermute | solution.py:421
  40.9 14.7 %collective-permute-start.8 = (bf16[1024,128]{1,0:T(8,128)(2,1)S(1)}, bf16[1024,128]{1,0:T(8,128)(2,1)}, u32[]{:S(2)}, u32[]{:S(2)}) collective-permute-start(bf16[1024,128]{1,0:T(8,128)(2,1)S(1)} %collective-permute-done.7.refs_11_), channel_id=1, source_target_pairs={{0,2},{1,3},{2,0},{3,1},{4,6},{5,7},{6,4},{7,5},{8,10},{9,11},{10,... | collective-permute-start | bytes 786440 | tf_op jit(solution)/shard_map/ppermute | solution.py:421
  41.4 14.6 %collective-permute-start.12 = (bf16[1024,128]{1,0:T(8,128)(2,1)S(1)}, bf16[1024,128]{1,0:T(8,128)(2,1)S(1)}, u32[]{:S(2)}, u32[]{:S(2)}) collective-permute-start(bf16[1024,128]{1,0:T(8,128)(2,1)S(1)} %collective-permute-done.11.refs_15_), channel_id=1, source_target_pairs={{0,2},{1,3},{2,0},{3,1},{4,6},{5,7},{6,4},{7,5},{8,10},{9,11},{10,... | collective-permute-start | bytes 786440 | tf_op jit(solution)/shard_map/ppermute | solution.py:421
  51.4 3.4 %copy-start.1 = (bf16[32,128,1024]{2,1,0:T(8,128)(2,1)}, bf16[32,128,1024]{2,1,0:T(8,128)(2,1)S(1)}, u32[]{:S(2)}) copy-start(bf16[32,128,1024]{2,1,0:T(8,128)(2,1)S(1)} %shard_map.86.refs_0_) | copy-start | bytes 25165828
  54.9 2.9 %collective-permute-start.9 = (bf16[1024,128]{1,0:T(8,128)(2,1)S(1)}, bf16[1024,128]{1,0:T(8,128)(2,1)S(1)}, u32[]{:S(2)}, u32[]{:S(2)}) collective-permute-start(bf16[1024,128]{1,0:T(8,128)(2,1)S(1)} %collective-permute-done.7.refs_11_), channel_id=1, source_target_pairs={{0,1},{1,0},{2,3},{3,2},{4,5},{5,4},{6,7},{7,6},{8,9},{9,8},{10,11... | collective-permute-start | bytes 786440 | tf_op jit(solution)/shard_map/ppermute | solution.py:421
  55.0 2.9 %collective-permute-start.13 = (bf16[1024,128]{1,0:T(8,128)(2,1)S(1)}, bf16[1024,128]{1,0:T(8,128)(2,1)S(1)}, u32[]{:S(2)}, u32[]{:S(2)}) collective-permute-start(bf16[1024,128]{1,0:T(8,128)(2,1)S(1)} %collective-permute-done.11.refs_15_), channel_id=1, source_target_pairs={{0,1},{1,0},{2,3},{3,2},{4,5},{5,4},{6,7},{7,6},{8,9},{9,8},{10,11... | collective-permute-start | bytes 786440 | tf_op jit(solution)/shard_map/ppermute | solution.py:421
  55.5 2.4 %collective-permute-start.6 = (bf16[1024,128]{1,0:T(8,128)(2,1)S(1)}, bf16[1024,128]{1,0:T(8,128)(2,1)S(1)}, u32[]{:S(2)}, u32[]{:S(2)}) collective-permute-start(bf16[1024,128]{1,0:T(8,128)(2,1)S(1)} %collective-permute-done.4.refs_8_), channel_id=1, source_target_pairs={{0,1},{1,0},{2,3},{3,2},{4,5},{5,4},{6,7},{7,6},{8,9},{9,8},{10,11... | collective-permute-start | bytes 786440 | tf_op jit(solution)/shard_map/ppermute | solution.py:421
  55.6 2.4 %collective-permute-start.10 = (bf16[1024,128]{1,0:T(8,128)(2,1)}, bf16[1024,128]{1,0:T(8,128)(2,1)S(1)}, u32[]{:S(2)}, u32[]{:S(2)}) collective-permute-start(bf16[1024,128]{1,0:T(8,128)(2,1)} %collective-permute-done.8.refs_12_), channel_id=1, source_target_pairs={{0,1},{1,0},{2,3},{3,2},{4,5},{5,4},{6,7},{7,6},{8,9},{9,8},{10,11... | collective-permute-start | bytes 786440 | tf_op jit(solution)/shard_map/ppermute | solution.py:421
  56.0 2.0 %collective-permute-start.14 = (bf16[1024,128]{1,0:T(8,128)(2,1)S(1)}, bf16[1024,128]{1,0:T(8,128)(2,1)S(1)}, u32[]{:S(2)}, u32[]{:S(2)}) collective-permute-start(bf16[1024,128]{1,0:T(8,128)(2,1)S(1)} %collective-permute-done.12.refs_16_), channel_id=1, source_target_pairs={{0,1},{1,0},{2,3},{3,2},{4,5},{5,4},{6,7},{7,6},{8,9},{9,8},{10,11... | collective-permute-start | bytes 786440 | tf_op jit(solution)/shard_map/ppermute | solution.py:421
  89.5 32.6 %collective-permute-start.15 = (bf16[512,128]{1,0:T(8,128)(2,1)S(1)}, bf16[512,128]{1,0:T(8,128)(2,1)S(1)}, u32[]{:S(2)}, u32[]{:S(2)}) collective-permute-start(bf16[512,128]{1,0:T(8,128)(2,1)S(1)} %get-tuple-element.17), channel_id=1, source_target_pairs={{0,4},{4,0},{8,12},{12,8},{1,5},{5,1},{9,13},{13,9},{2,6},{6,2},{1... | collective-permute-start | bytes 393224 | tf_op jit(solution)/shard_map/ppermute | solution.py:421
  93.5 28.6 %collective-permute-start.16 = (bf16[512,128]{1,0:T(8,128)(2,1)S(1)}, bf16[512,128]{1,0:T(8,128)(2,1)S(1)}, u32[]{:S(2)}, u32[]{:S(2)}) collective-permute-start(bf16[512,128]{1,0:T(8,128)(2,1)S(1)} %get-tuple-element.18), channel_id=1, source_target_pairs={{0,8},{4,12},{8,0},{12,4},{1,9},{5,13},{9,1},{13,5},{2,10},{6,14},... | collective-permute-start | bytes 393224 | tf_op jit(solution)/shard_map/ppermute | solution.py:421
  94.5 27.6 %collective-permute-start.17 = (bf16[512,128]{1,0:T(8,128)(2,1)S(1)}, bf16[512,128]{1,0:T(8,128)(2,1)S(1)}, u32[]{:S(2)}, u32[]{:S(2)}) collective-permute-start(bf16[512,128]{1,0:T(8,128)(2,1)S(1)} %get-tuple-element.19), channel_id=1, source_target_pairs={{0,12},{4,8},{8,4},{12,0},{1,13},{5,9},{9,5},{13,1},{2,14},{6,10},... | collective-permute-start | bytes 393224 | tf_op jit(solution)/shard_map/ppermute | solution.py:421
  96.0 2.2 %copy-start = (bf16[32,64,1024]{2,1,0:T(8,128)(2,1)S(1)}, bf16[32,64,1024]{2,1,0:T(8,128)(2,1)}, u32[]{:S(2)}) copy-start(bf16[32,64,1024]{2,1,0:T(8,128)(2,1)} %get-tuple-element.15.mine.by_id) | copy-start | bytes 12582916

commit v2 on v1

--- a/solution.py
+++ b/solution.py
@@ -5,6 +5,7 @@
 import jax.numpy as jnp
 from jax import lax
 from jax.experimental import pallas as pl
+from jax.experimental.layout import Layout, with_layout_constraint
 from jax.experimental.pallas import tpu as pltpu
 from jax.sharding import PartitionSpec as P
 
@@ -128,14 +129,44 @@
 SCALARS = pl.BlockSpec(memory_space=pltpu.SMEM)
 
 
-def filter_kernel(inp, group, spectra_n, counts, frames, taps_col, base, *rest):
-    *outs, table = rest
-    depth = base.shape[0]
+def nested(flat, pieces):
+    flat = list(flat)
+    out = []
+    for many in pieces:
+        out.append(flat[:many])
+        flat = flat[many:]
+    return out
+
+
+def turned_by(turn_row, index):
+    table = jnp.broadcast_to(turn_row, (index.shape[0], LANES))
+    return jnp.concatenate(
+        [
+            jnp.take_along_axis(table, index[:, j : j + LANES], axis=1)
+            for j in range(0, index.shape[1], LANES)
+        ],
+        axis=1,
+    )
+
+
+def filter_kernel(inp, group, spectra_n, pieces, counts, voltages, taps_col, turn_cos, index, *rest):
+    *flat, table, wide, frames = rest
+    outs = nested(flat, pieces)
+    depth = index.shape[0]
+    frames_n = spectra_n + TAPS - 1
+    base = turned_by(turn_cos[0:1, :], index[...])
     for k in range(TAPS):
-        table[k * depth : (k + 1) * depth, :] = (taps_col[:, k : k + 1] * base[...]).astype(
+        table[k * depth : (k + 1) * depth, :] = (taps_col[:, k : k + 1] * base).astype(
             jnp.bfloat16
         )
-    width = base.shape[1] // len(outs)
+    wide[...] = voltages[...].astype(jnp.float32)
+    for s in range(frames_n):
+        for c in range(2):
+            frames[s * inp : (s + 1) * inp, c * NCH : (c + 1) * NCH] = wide[
+                pl.ds(2 * s + c, inp, stride=2 * frames_n), :
+            ].astype(jnp.bfloat16)
+    width = index.shape[1] // len(outs)
+    pack = LANES // width
     for first in range(0, spectra_n, group):
         left = jnp.concatenate(
             [
@@ -145,68 +176,84 @@
             axis=1,
         )
         got = dot(left, table[...], ((1,), (0,)))
-        pieces = []
+        kept = []
         for step in range(group):
             t = first + step
             keep = (t % SPEC < counts[t // SPEC]).astype(jnp.float32)
-            pieces.append(got[step * inp : (step + 1) * inp, :] * keep)
-        pack = LANES // width
+            kept.append(got[step * inp : (step + 1) * inp, :] * keep)
         for pair in range(group // pack):
             row = (first // pack + pair) * inp
-            for d, out in enumerate(outs):
-                out[row : row + inp, :] = jnp.concatenate(
+            for d, parts in enumerate(outs):
+                out = parts[row // parts[0].shape[0]]
+                line = row % out.shape[0]
+                out[line : line + inp, :] = jnp.concatenate(
                     [
-                        pieces[pair * pack + h][:, d * width : (d + 1) * width]
+                        kept[pair * pack + h][:, d * width : (d + 1) * width]
                         for h in range(pack)
                     ],
                     axis=1,
                 ).astype(jnp.bfloat16)
 
 
-def run_filter(counts, frames, taps_col, base, inp, n_chan, spectra_n):
-    width = base.shape[1] // n_chan
-    pack = LANES // width
-    out = jax.ShapeDtypeStruct((spectra_n // pack * inp, LANES), jnp.bfloat16)
-    return pl.pallas_call(
-        functools.partial(filter_kernel, inp, 4, spectra_n),
-        out_shape=[out] * n_chan,
-        in_specs=[SCALARS] + [pl.BlockSpec(memory_space=pltpu.VMEM)] * 3,
-        out_specs=[pl.BlockSpec(memory_space=pltpu.VMEM)] * n_chan,
-        scratch_shapes=[pltpu.VMEM((TAPS * base.shape[0], base.shape[1]), jnp.bfloat16)],
+def run_filter(counts, voltages, taps_col, turn_cos, index, inp, pieces, spectra_n):
+    depth, columns = index.shape
+    pack = LANES * len(pieces) // columns
+    flat = pl.pallas_call(
+        functools.partial(filter_kernel, inp, 4, spectra_n, pieces),
+        out_shape=[
+            jax.ShapeDtypeStruct((spectra_n // pack * inp // many, LANES), jnp.bfloat16)
+            for many in pieces
+            for _ in range(many)
+        ],
+        in_specs=[SCALARS] + [pl.BlockSpec(memory_space=pltpu.VMEM)] * 4,
+        out_specs=[pl.BlockSpec(memory_space=pltpu.VMEM)] * sum(pieces),
+        scratch_shapes=[
+            pltpu.VMEM((TAPS * depth, columns), jnp.bfloat16),
+            pltpu.VMEM(voltages.shape, jnp.float32),
+            pltpu.VMEM((voltages.shape[0] // 2, 2 * NCH), jnp.bfloat16),
+        ],
         compiler_params=pltpu.CompilerParams(vmem_limit_bytes=32 * MIB),
         cost_estimate=pl.CostEstimate(
-            flops=2 * spectra_n * inp * TAPS * base.size,
+            flops=2 * spectra_n * inp * TAPS * depth * columns,
             bytes_accessed=4 * MIB,
             transcendentals=0,
         ),
-    )(counts, frames, taps_col, base)
+    )(counts, voltages, taps_col, turn_cos, index)
+    return nested(flat, pieces)
 
 
 def weight_kernel(first, delays, turn_cos, turn_sin, out):
-    channel = first[0] + pl.program_id(0)
+    some = out.shape[0]
     section, inputs = delays.shape
     cosine = jnp.broadcast_to(turn_cos[0:1, :], (section, LANES))
     sine = jnp.broadcast_to(turn_sin[0:1, :], (section, LANES))
-    for block in range(inputs // LANES):
-        lanes = slice(block * LANES, (block + 1) * LANES)
-        phase = (delays[:, lanes] * channel) & (NCH - 1)
-        out[0, :section, lanes] = jnp.take_along_axis(cosine, phase, axis=1).astype(jnp.bfloat16)
-        out[0, section:, lanes] = jnp.take_along_axis(sine, phase, axis=1).astype(jnp.bfloat16)
+    for part in range(some):
+        channel = first[0] + pl.program_id(0) * some + part
+        for block in range(inputs // LANES):
+            lanes = slice(block * LANES, (block + 1) * LANES)
+            phase = (delays[:, lanes] * channel) & (NCH - 1)
+            out[part, :section, lanes] = jnp.take_along_axis(cosine, phase, axis=1).astype(
+                jnp.bfloat16
+            )
+            out[part, section:, lanes] = jnp.take_along_axis(sine, phase, axis=1).astype(
+                jnp.bfloat16
+            )
 
 
 def run_weights(first, delays, turn_cos, turn_sin, ch_dev):
     section, inputs = delays.shape
+    some = math.gcd(4, ch_dev)
     return pl.pallas_call(
         weight_kernel,
         out_shape=jax.ShapeDtypeStruct((ch_dev, 2 * section, inputs), jnp.bfloat16),
-        grid=(ch_dev,),
+        grid=(ch_dev // some,),
         in_specs=[
             SCALARS,
             whole(delays.shape),
             whole(turn_cos.shape),
             whole(turn_sin.shape),
         ],
-        out_specs=pl.BlockSpec((1, 2 * section, inputs), lambda f: (f, 0, 0)),
+        out_specs=pl.BlockSpec((some, 2 * section, inputs), lambda f: (f, 0, 0)),
         compiler_params=pltpu.CompilerParams(vmem_limit_bytes=16 * MIB),
         cost_estimate=pl.CostEstimate(
             flops=8 * ch_dev * section * inputs,
@@ -216,140 +263,181 @@
     )(first, delays, turn_cos, turn_sin)
 
 
-def beam_kernel(sizes, n_blocks, n_dest, *refs):
+def beam_kernel(sizes, pieces, n_dest, weights, choose, ids, *refs):
     inp, ch_dev, spectra_n, most = sizes
-    weights, choose, ids = refs[:3]
-    blocks = refs[3 : 3 + n_blocks]
-    by_id = refs[3 + n_blocks]
-    sent = refs[4 + n_blocks : 4 + n_blocks + n_dest]
-    turned, formed = refs[4 + n_blocks + n_dest :]
-    channel = pl.program_id(0)
+    blocks, refs = nested(refs[: sum(pieces)], pieces), refs[sum(pieces) :]
+    by_id, sent = refs[0], refs[1 : 1 + n_dest]
+    turned, formed, ordered, out_sem = refs[1 + n_dest :]
     width = 2 * ch_dev
-    pack = LANES // width
-    packed = spectra_n // pack
+    pitch = width + 8
+    packed = spectra_n * width // LANES
     section = weights.shape[1] // 2
-
-    @pl.when(channel == 0)
-    def _():
-        together = 4
-        for first in range(0, packed, together):
-            left = jnp.concatenate(
+    n_parts = out_sem.shape[0]
+    part = ch_dev // n_parts
+
+    def store(p):
+        lines = pl.ds(p * part, part)
+        return pltpu.make_async_copy(ordered.at[lines], by_id.at[lines], out_sem.at[p])
+
+    together = 4
+    for first in range(0, packed, together):
+        left = jnp.concatenate(
+            [
+                jnp.concatenate(
+                    [
+                        parts[t * len(parts) // packed][
+                            t * inp % parts[0].shape[0] : t * inp % parts[0].shape[0] + inp, :
+                        ]
+                        for parts in blocks
+                    ],
+                    axis=0,
+                )
+                for t in range(first, first + together)
+            ],
+            axis=1,
+        )
+        got = dot(left, ids[...], ((0,), (0,)))
+        for j in range(turned.shape[0]):
+            for row in range(0, together * LANES, width):
+                place = (first * LANES + row) // width * pitch
+                turned[j, place : place + width, :] = got[
+                    row : row + width, j * LANES : (j + 1) * LANES
+                ]
+
+    for p in range(n_parts):
+        for channel in range(p * part, (p + 1) * part):
+            both = jnp.concatenate(
                 [
                     jnp.concatenate(
-                        [block[t * inp : (t + 1) * inp, :] for block in blocks], axis=0
+                        [
+                            turned[j, pl.ds(c * ch_dev + channel, spectra_n, stride=pitch), :]
+                            for j in range(turned.shape[0])
+                        ],
+                        axis=1,
                     )
-                    for t in range(first, first + together)
-                ],
-                axis=1,
-            )
-            got = dot(left, ids[...], ((0,), (0,)))
-            for j in range(turned.shape[0]):
-                turned[j, first * LANES : (first + together) * LANES, :] = got[
-                    :, j * LANES : (j + 1) * LANES
-                ]
-
-    both = jnp.concatenate(
-        [
-            jnp.concatenate(
-                [
-                    turned[j, pl.ds(c * ch_dev + channel, spectra_n, stride=width), :]
-                    for j in range(turned.shape[0])
-                ],
-                axis=1,
-            )
-            for c in range(2)
-        ],
-        axis=0,
-    ).astype(jnp.bfloat16)
-    by_id[0] = both
-    got = dot(both, weights[0], ((1,), (1,)))
-    real = got[:spectra_n, :section] - got[spectra_n:, section:]
-    imag = got[spectra_n:, :section] + got[:spectra_n, section:]
-    for c, part in enumerate((real, imag)):
-        formed[pl.ds(c * ch_dev + channel, spectra_n, stride=width), :] = jnp.pad(
-            part, ((0, 0), (0, LANES - section))
-        )
-
-    @pl.when(channel == ch_dev - 1)
-    def _():
-        per = LANES // most
-        total = None
-        for j in range(per):
-            left = jnp.concatenate(
-                [
-                    formed[t * width : (t + 1) * width, :section].astype(jnp.bfloat16)
-                    for t in range(j, spectra_n, per)
+                    for c in range(2)
                 ],
                 axis=0,
-            )
-            more = dot(left, choose[j * section : (j + 1) * section, :], ((1,), (0,)))
-            total = more if total is None else total + more
-        for d in range(n_dest):
-            sent[d][...] = total[:, d * LANES : (d + 1) * LANES].astype(jnp.bfloat16)
+            ).astype(jnp.bfloat16)
+            ordered[channel] = both
+            got = dot(both, weights[channel], ((1,), (1,)))
+            real = got[:spectra_n, :section] - got[spectra_n:, section:]
+            imag = got[spectra_n:, :section] + got[:spectra_n, section:]
+            for c, value in enumerate((real, imag)):
+                formed[pl.ds(c * ch_dev + channel, spectra_n, stride=pitch), :] = jnp.pad(
+                    value, ((0, 0), (0, LANES - section))
+                )
+        store(p).start()
+
+    per = LANES // most
+    total = None
+    for j in range(per):
+        left = jnp.concatenate(
+            [
+                formed[t * pitch : t * pitch + width, :section].astype(jnp.bfloat16)
+                for t in range(j, spectra_n, per)
+            ],
+            axis=0,
+        )
+        more = dot(left, choose[j * section : (j + 1) * section, :], ((1,), (0,)))
+        total = more if total is None else total + more
+    for d in range(n_dest):
+        sent[d][...] = total[:, d * LANES : (d + 1) * LANES].astype(jnp.bfloat16)
+    for p in range(n_parts):
+        store(p).wait()
 
 
 def run_beams(weights, choose, ids, blocks, inp, spectra_n, most, n_dest):
     ch_dev, twice, inputs = weights.shape
     width = 2 * ch_dev
     out_rows = spectra_n // (LANES // most) * width
+    n_parts = math.gcd(8, ch_dev)
+    vmem = pl.BlockSpec(memory_space=pltpu.VMEM)
+    anywhere = pl.BlockSpec(memory_space=pltpu.HBM)
     return pl.pallas_call(
-        functools.partial(beam_kernel, (inp, ch_dev, spectra_n, most), len(blocks), n_dest),
+        functools.partial(
+            beam_kernel, (inp, ch_dev, spectra_n, most), [len(parts) for parts in blocks], n_dest
+        ),
         out_shape=[jax.ShapeDtypeStruct((ch_dev, 2 * spectra_n, inputs), jnp.bfloat16)]
         + [jax.ShapeDtypeStruct((out_rows, LANES), jnp.bfloat16)] * n_dest,
-        grid=(ch_dev,),
-        in_specs=[
-            pl.BlockSpec((1, twice, inputs), lambda f: (f, 0, 0)),
-            whole(choose.shape),
-            whole(ids.shape),
-        ]
-        + [whole(block.shape) for block in blocks],
-        out_specs=[pl.BlockSpec((1, 2 * spectra_n, inputs), lambda f: (f, 0, 0))]
-        + [whole((out_rows, LANES))] * n_dest,
+        in_specs=[vmem, vmem, vmem] + [vmem] * sum(len(parts) for parts in blocks),
+        out_specs=[anywhere] + [vmem] * n_dest,
         scratch_shapes=[
-            pltpu.VMEM((inputs // LANES, spectra_n * width, LANES), jnp.float32),
-            pltpu.VMEM((spectra_n * width, LANES), jnp.float32),
+            pltpu.VMEM((inputs // LANES, spectra_n * (width + 8), LANES), jnp.float32),
+            pltpu.VMEM((spectra_n * (width + 8), LANES), jnp.float32),
+            pltpu.VMEM((ch_dev, 2 * spectra_n, inputs), jnp.bfloat16),
+            pltpu.SemaphoreType.DMA((n_parts,)),
         ],
-        compiler_params=pltpu.CompilerParams(vmem_limit_bytes=48 * MIB),
+        compiler_params=pltpu.CompilerParams(vmem_limit_bytes=36 * MIB),
         cost_estimate=pl.CostEstimate(
             flops=2 * spectra_n * width * inputs * inputs,
             bytes_accessed=24 * MIB,
             transcendentals=0,
         ),
-    )(weights, choose, ids, *blocks)
-
-
-def visibility_kernel(sub_index, counts, mine, by_id, out):
+    )(weights, choose, ids, *[part for parts in blocks for part in parts])
+
+
+def visibility_kernel(sub_index, counts, mine, by_id, out, held, sem):
     del sub_index
+    some, depth, rows = mine.shape
+    half = depth // 2
+    step = pl.program_id(0)
     total = counts[0]
     for b in range(1, counts.shape[0]):
         total = total + counts[b]
-    half = mine.shape[1] // 2
-    rows = mine.shape[2]
-    real, imag = mine[0, :half, :], mine[0, half:, :]
-    left = jnp.concatenate(
-        [jnp.concatenate([real, imag], axis=0), jnp.concatenate([imag, -real], axis=0)], axis=1
-    )
-    got = dot(left, by_id[0], ((0,), (0,)))
-    scale = 1.0 / jnp.full((1, got.shape[1]), total, jnp.int32).astype(jnp.float32)
-    out[0, 0] = (got[:rows, :] * scale).astype(jnp.bfloat16)
-    out[0, 1] = (got[rows:, :] * scale).astype(jnp.bfloat16)
+    scale = 1.0 / jnp.full((1, by_id.shape[2]), total, jnp.int32).astype(jnp.float32)
+
+    def store(part, at):
+        slot = at % 2 * some + part
+        return pltpu.make_async_copy(held.at[slot], out.at[at * some + part], sem.at[slot])
+
+    @pl.when(step > 1)
+    def _():
+        for part in range(some):
+            store(part, step - 2).wait()
+
+    for part in range(some):
+        real, imag = mine[part, :half, :], mine[part, half:, :]
+        left = jnp.concatenate(
+            [jnp.concatenate([real, imag], axis=0), jnp.concatenate([imag, -real], axis=0)],
+            axis=1,
+        )
+        got = dot(left, by_id[part], ((0,), (0,)))
+        slot = step % 2 * some + part
+        held[slot, 0] = (got[:rows, :] * scale).astype(jnp.bfloat16)
+        held[slot, 1] = (got[rows:, :] * scale).astype(jnp.bfloat16)
+        store(part, step).start()
+
+    @pl.when(step == pl.num_programs(0) - 1)
+    def _():
+        for before in (1, 0):
+
+            @pl.when(step >= before)
+            def _():
+                for part in range(some):
+                    store(part, step - before).wait()
 
 
 def run_visibility(sub_index, counts, by_id, rows):
     ch_dev, depth, inputs = by_id.shape
+    some = math.gcd(4, ch_dev)
     return pl.pallas_call(
         visibility_kernel,
         out_shape=jax.ShapeDtypeStruct((ch_dev, 2, rows, inputs), jnp.bfloat16),
         grid_spec=pltpu.PrefetchScalarGridSpec(
             num_scalar_prefetch=2,
-            grid=(ch_dev,),
+            grid=(ch_dev // some,),
             in_specs=[
-                pl.BlockSpec((1, depth, rows), lambda f, sub, counts: (f, 0, sub[0])),
-                pl.BlockSpec((1, depth, inputs), lambda f, sub, counts: (f, 0, 0)),
+                pl.BlockSpec((some, depth, rows), lambda f, sub, counts: (f, 0, sub[0])),
+                pl.BlockSpec((some, depth, inputs), lambda f, sub, counts: (f, 0, 0)),
             ],
-            out_specs=pl.BlockSpec((1, 2, rows, inputs), lambda f, sub, counts: (f, 0, 0, 0)),
-        ),
-        compiler_params=pltpu.CompilerParams(vmem_limit_bytes=24 * MIB),
+            out_specs=pl.BlockSpec(memory_space=pltpu.HBM),
+            scratch_shapes=[
+                pltpu.VMEM((2 * some, 2, rows, inputs), jnp.bfloat16),
+                pltpu.SemaphoreType.DMA((2 * some,)),
+            ],
+        ),
+        compiler_params=pltpu.CompilerParams(vmem_limit_bytes=60 * MIB),
         cost_estimate=pl.CostEstimate(
             flops=4 * ch_dev * depth * rows * inputs,
             bytes_accessed=4 * ch_dev * rows * inputs,
@@ -358,11 +446,12 @@
     )(sub_index, counts, by_id, by_id)
 
 
-def resynth_kernel(most, spectra_n, taps_row, base, *refs):
+def resynth_kernel(most, spectra_n, taps_row, turn_cos, index, *refs):
     *blocks, out, table, window = refs
-    depth, width = base.shape
+    depth, width = index.shape
+    base = turned_by(turn_cos[0:1, :], index[...])
     for k in range(TAPS):
-        table[k * depth : (k + 1) * depth, :] = (taps_row[k : k + 1, :] * base[...]).astype(
+        table[k * depth : (k + 1) * depth, :] = (taps_row[k : k + 1, :] * base).astype(
             jnp.bfloat16
         )
     per = LANES // most
@@ -397,24 +486,24 @@
                 ]
 
 
-def run_resynth(taps_row, base, blocks, most, spectra_n):
+def run_resynth(taps_row, turn_cos, index, blocks, most, spectra_n):
     frames_n = spectra_n + TAPS - 1
     return pl.pallas_call(
         functools.partial(resynth_kernel, most, spectra_n),
         out_shape=jax.ShapeDtypeStruct((most * frames_n * 2, NCH), jnp.float32),
-        in_specs=[pl.BlockSpec(memory_space=pltpu.VMEM)] * (2 + len(blocks)),
+        in_specs=[pl.BlockSpec(memory_space=pltpu.VMEM)] * (3 + len(blocks)),
         out_specs=pl.BlockSpec(memory_space=pltpu.VMEM),
         scratch_shapes=[
-            pltpu.VMEM((TAPS * base.shape[0], base.shape[1]), jnp.bfloat16),
-            pltpu.VMEM(((spectra_n + 2 * (TAPS - 1)) * most, base.shape[0]), jnp.bfloat16),
+            pltpu.VMEM((TAPS * index.shape[0], index.shape[1]), jnp.bfloat16),
+            pltpu.VMEM(((spectra_n + 2 * (TAPS - 1)) * most, index.shape[0]), jnp.bfloat16),
         ],
         compiler_params=pltpu.CompilerParams(vmem_limit_bytes=32 * MIB),
         cost_estimate=pl.CostEstimate(
-            flops=2 * frames_n * most * TAPS * base.size,
+            flops=2 * frames_n * most * TAPS * index.size,
             bytes_accessed=4 * MIB,
             transcendentals=0,
         ),
-    )(taps_row, base, *blocks)
+    )(taps_row, turn_cos, index, *blocks)
 
 
 def swap(x, axis, size, mask):
@@ -447,56 +536,69 @@
     row_place = jnp.tile(jnp.arange(NCH, dtype=jnp.int32), 2)
     row_part = jnp.repeat(jnp.arange(2, dtype=jnp.int32), NCH)
 
-    def fourier(place, place_part, channel, channel_part):
+    def table_index(place, place_part, channel, channel_part):
         quarter = (channel_part - place_part) * (NCH // 4)
-        index = (place * channel + quarter + NCH) % NCH
-        return jnp.cos(index.astype(jnp.float32) * turn)
-
-    base = fourier(
+        return (place * channel + quarter) & (NCH - 1)
+
+    index = table_index(
         row_place[:, None], row_part[:, None], column_channel[None, :], column_part[None, :]
     )
-    base_back = fourier(
+    index_back = table_index(
         row_place[None, :], row_part[None, :], column_channel[:, None], column_part[:, None]
     )
-    taps2 = taps.reshape(TAPS, NCH)
-    taps_row = jnp.tile(taps2, (1, 2))
+    phases = jnp.arange(NCH, dtype=jnp.int32).astype(jnp.float32) * turn
+    turn_cos = jnp.broadcast_to(jnp.cos(phases)[None, :], (8, NCH))
+    turn_sin = jnp.broadcast_to(jnp.sin(phases)[None, :], (8, NCH))
+    taps_row = jnp.tile(taps.reshape(TAPS, NCH), (1, 2))
     taps_col = taps_row.T
 
-    frames = jnp.transpose(voltages.reshape(inp, 2, frames_n, NCH), (2, 0, 1, 3)).reshape(
-        frames_n * inp, 2 * NCH
-    )
-    outgoing = run_filter(counts, frames, taps_col, base, inp, n_chan, spectra_n)
-
-    turned = [outgoing[0]] + [swap(outgoing[d], "chan", n_chan, d) for d in range(1, n_chan)]
-    blocks = []
-    for block in turned:
-        held = [block]
-        far = n_sub
-        masks = []
-        while far > 1:
-            far //= 2
-            masks.append(far)
-        for mask in masks:
-            held = held + [swap(x, "sub", n_sub, mask) for x in held]
-        blocks.extend(held)
+    lines = jnp.transpose(
+        with_layout_constraint(
+            voltages.reshape(inp, 2, frames_n, NCH),
+            Layout(major_to_minor=(0, 2, 1, 3)),
+        ),
+        (0, 2, 1, 3),
+    ).reshape(2 * inp * frames_n, NCH)
+    pieces = [1] * n_chan
+    if spectra_n * ch_dev * 2 // LANES % 2 == 0:
+        pieces[-1] = 1
+    outgoing = run_filter(counts, lines, taps_col, turn_cos, index, inp, pieces, spectra_n)
+    turned = [outgoing[0]] + [
+        [swap(x, "chan", n_chan, d) for x in outgoing[d]] for d in range(1, n_chan)
+    ]
+
+    masks = []
     order = [0]
     far = n_sub
     while far > 1:
         far //= 2
+        masks.append(far)
         order = order + [o ^ far for o in order]
     id_table = input_id.reshape(n_chan, n_sub, inp)
-    slot_id = jnp.take(
-        jnp.take(id_table, partner, axis=0), sub_index ^ jnp.array(order, jnp.int32), axis=1
+    slot_id = jnp.stack(
+        [
+            lax.dynamic_slice(id_table, (chan_index ^ d, sub_index ^ o, 0), (1, 1, inp))
+            for d in range(n_chan)
+            for o in order
+        ]
     ).reshape(-1)
+    scale = 1.0 / math.sqrt(inputs)
+    weights = run_weights(
+        (chan_index * ch_dev).reshape(1).astype(jnp.int32),
+        delays,
+        turn_cos * scale,
+        turn_sin * scale,
+        ch_dev,
+    )
+    turned[1][0], weights = lax.optimization_barrier((turned[1][0], weights))
+    turned[0][0], slot_id = lax.optimization_barrier((turned[0][0], slot_id))
     ids = (slot_id[:, None] == jnp.arange(inputs, dtype=jnp.int32)[None, :]).astype(jnp.bfloat16)
-
-    phases = jnp.arange(NCH, dtype=jnp.int32).astype(jnp.float32) * turn
-    scale = 1.0 / math.sqrt(inputs)
-    turn_cos = jnp.broadcast_to((jnp.cos(phases) * scale)[None, :], (8, NCH))
-    turn_sin = jnp.broadcast_to((jnp.sin(phases) * scale)[None, :], (8, NCH))
-    weights = run_weights(
-        (chan_index * ch_dev).reshape(1).astype(jnp.int32), delays, turn_cos, turn_sin, ch_dev
-    )
+    blocks = []
+    for parts in turned:
+        held = [parts]
+        for mask in masks:
+            held = held + [[swap(x, "sub", n_sub, mask) for x in those] for those in held]
+        blocks.extend(held)
 
     owner = lax.dynamic_slice_in_dim(beam_owner[:, 0], sub_index * section, section)
     beam = jnp.arange(section, dtype=jnp.int32)
@@ -515,10 +617,11 @@
     visibility = run_visibility(
         sub_index.reshape(1).astype(jnp.int32), counts, by_id, rows
     )
-    voice = run_resynth(taps_row, base_back, arrived, most, spectra_n)
-    resynth = jnp.transpose(voice.reshape(most, frames_n, 2, NCH), (0, 2, 1, 3)).reshape(
-        most, 2, frames_n * NCH
-    )
+    voice = run_resynth(taps_row, turn_cos, index_back, arrived, most, spectra_n)
+    resynth = with_layout_constraint(
+        jnp.transpose(voice.reshape(most, frames_n, 2, NCH), (0, 2, 1, 3)),
+        Layout(major_to_minor=(0, 2, 1, 3)),
+    ).reshape(most, 2, frames_n * NCH)
     return (visibility, resynth)
 
 

time: 128 us -> 88.3 us (0.69)
  Pallas kernels: 70.8 us -> 42.9 us
  local copies, waits for them, and re-layouts: 16 us -> 10.3 us
  other arithmetic: 5.47 us -> 1.85 us
  starting transfers between devices: 17.8 us -> 15.4 us
    pallas_call x1, Pallas kernels: 31.5 us -> 13.7 us  [run_beams(): pl.pallas_call(functools.partial(beam_kernel, (inp, ch_dev, spectra_n, mo...]
    pallas_call x1, Pallas kernels: 24 us -> 14.4 us  [run_visibility(): pl.pallas_call(visibility_kernel, out_shape=jax.ShapeDtypeStruct((ch_dev,...]
    reshape x3 -> x1, local copies, waits for them, and re-layouts: 4.01 us -> 0.07 us  [quick(): slot_id = jnp.stack([lax.dynamic_slice(id_table, (chan_index ^ d, sub_ind...]
    cos x1, other arithmetic: 2.99 us -> 0.04 us  [quick(): turn_cos = jnp.broadcast_to(jnp.cos(phases)[None, :], (8, NCH))]
    ppermute x18, starting transfers between devices: 17.8 us -> 15.4 us  [swap(): return lax.ppermute(x, axis, [(i, i ^ mask) for i in range(size)])]
    pallas_call x1, Pallas kernels: 8.12 us -> 6.54 us  [run_weights(): pl.pallas_call(weight_kernel, out_shape=jax.ShapeDtypeStruct((ch_dev, 2 *...]
    transpose x1 -> x0, local copies, waits for them, and re-layouts: 1.53 us -> none  [quick(): jnp.transpose(voltages.reshape(inp, 2, frames_n, NCH), (2, 0, 1, 3))]
    convert_element_type x1, other arithmetic: 1.75 us -> 0.4 us  [quick(): (slot_id[:, None] == jnp.arange(inputs, dtype=jnp.int32)[None, :]).astype...]
  transfers between devices with their start and end apart: 18 -> 18, of which waited for: 3 -> 4; matrix products, arithmetic and copies ran while one was open for 3% -> 1% of each run, Pallas kernels for 25% -> 24%
where the time goes in v2:
time: 88.3 us; the launch traced here: 87.8 us
  Pallas kernels  42.9 us (49%)
  waiting for transfers between devices  16.4 us (19%)
  starting transfers between devices  15.4 us (17%)
  local copies, waits for them, and re-layouts  10.3 us (12%)
  other arithmetic  1.85 us (2%)
  between operations  1 us (1%)
    ppermute x18, waiting for transfers between devices, swap(): return lax.ppermute(x, axis, [(i, i ^ mask) for i in range(size)])  16.4 us
    ppermute x18, starting transfers between devices, swap(): return lax.ppermute(x, axis, [(i, i ^ mask) for i in range(size)])  15.4 us
    pallas_call x1, Pallas kernels, run_visibility(): pl.pallas_call(visibility_kernel, out_shape=jax.ShapeDtypeStruct((ch_dev,...  14.4 us
    pallas_call x1, Pallas kernels, run_beams(): pl.pallas_call(functools.partial(beam_kernel, (inp, ch_dev, spectra_n, mo...  13.7 us
    unnamed x29, local copies, waits for them, and re-layouts  7.61 us
    pallas_call x1, Pallas kernels, run_weights(): pl.pallas_call(weight_kernel, out_shape=jax.ShapeDtypeStruct((ch_dev, 2 *...  6.54 us
    pallas_call x1, Pallas kernels, run_filter(): pl.pallas_call(functools.partial(filter_kernel, inp, 4, spectra_n, pieces...  4.54 us
    pallas_call x1, Pallas kernels, run_resynth(): pl.pallas_call(functools.partial(resynth_kernel, most, spectra_n), out_sh...  3.66 us
  transfers between devices with their start and end apart: 18, of which 4 were waited for; matrix products, arithmetic and copies ran while one was open for 1% of the time, Pallas kernels for 24%

profile of v2, /device:TPU:0, one launch (start us, length us, event | category | flops | bytes accessed | tf_op | source)
XLA Modules:
  0.0 87.8 jit_solution(18416713896595527426)
XLA Ops:
  0.7 0.7 tile.19
  1.5 0.1 copy.9.taps_col
  1.8 0.8 reshape.130
  2.9 0.5 broadcast.101
  3.4 0.7 reduce.7
  4.2 0.2 add_and_fusion
  4.4 0.6 copy-done.3
  5.1 1.3 %copy-done.4 = bf16[64,2,5504]{2,1,0:T(2,128)(2,1)S(1)} copy-done((bf16[64,2,5504]{2,1,0:T(2,128)(2,1)S(1)}, bf16[64,2,5504]{2,1,0:T(2,128)(2,1)}, u32[]{:S(2)}) %copy-start.4) | copy-done | bytes 1409048
  6.4 4.5 %shard_map.77 = (bf16[1024,128]{1,0:T(8,128)(2,1)S(1)}, bf16[1024,128]{1,0:T(8,128)(2,1)S(1)}, bf16[1024,128]{1,0:T(8,128)(2,1)S(1)}, bf16[1024,128]{1,0:T(8,128)(2,1)S(1)}) custom-call(s32[4]{0:T(128)S(1)} %copy-done.3, bf16[5504,128]{1,0:T(8,128)(2,1)S(1)} %bitcast.92, f32[256,12]{1,0:T(8,128)S(1)} %copy.9.taps_col, ...), custom_call_target="tpu_custom_call" | custom-call | flops 3221225472 | bytes 4194304 | tf_op jit(solution)/shard_map/pallas_call | solution.py:201
  11.0 3.0 %collective-permute-start.1 = (bf16[1024,128]{1,0:T(8,128)(2,1)S(1)}, bf16[1024,128]{1,0:T(8,128)(2,1)S(1)}, u32[]{:S(2)}, u32[]{:S(2)}) collective-permute-start(bf16[1024,128]{1,0:T(8,128)(2,1)S(1)} %get-tuple-element.19.refs_0_), channel_id=1, source_target_pairs={{0,2},{1,3},{2,0},{3,1},{4,6},{5,7},{6,4},{7,5},{8,10},{9,11},{10,... | collective-permute-start | bytes 786440 | tf_op jit(solution)/shard_map/ppermute | solution.py:510
  14.0 1.6 %collective-permute-start = (bf16[1024,128]{1,0:T(8,128)(2,1)S(1)}, bf16[1024,128]{1,0:T(8,128)(2,1)S(1)}, u32[]{:S(2)}, u32[]{:S(2)}) collective-permute-start(bf16[1024,128]{1,0:T(8,128)(2,1)S(1)} %get-tuple-element.15), channel_id=1, source_target_pairs={{0,4},{4,0},{8,12},{12,8},{1,5},{5,1},{9,13},{13,9},{2,6},{6,2},{1... | collective-permute-start | bytes 786440 | tf_op jit(solution)/shard_map/ppermute | solution.py:510
  15.6 2.6 %collective-permute-start.7 = (bf16[1024,128]{1,0:T(8,128)(2,1)S(1)}, bf16[1024,128]{1,0:T(8,128)(2,1)S(1)}, u32[]{:S(2)}, u32[]{:S(2)}) collective-permute-start(bf16[1024,128]{1,0:T(8,128)(2,1)S(1)} %get-tuple-element.21), channel_id=1, source_target_pairs={{0,8},{4,12},{8,0},{12,4},{1,9},{5,13},{9,1},{13,5},{2,10},{6,14},... | collective-permute-start | bytes 786440 | tf_op jit(solution)/shard_map/ppermute | solution.py:510
  18.1 0.2 collective-permute-start.11
  18.5 0.2 convert_reduce_fusion
  18.7 6.5 %shard_map.78.weights = bf16[32,128,1024]{2,1,0:T(8,128)(2,1)S(1)} custom-call(s32[1]{0:T(128)} %bitcast.8.first, s32[64,1024]{1,0:T(8,128)S(1)} %copy-done.2, f32[8,128]{1,0:T(8,128)S(1)} %broadcast_in_dim.22.turn_cos, f32[8,128]{1,0:T(8,128)S(1)} %broadcast_in_dim.23.turn_sin), custom_call_target="tpu_custom_call" | custom-call | flops 16777216 | bytes 8388608 | tf_op jit(solution)/shard_map/pallas_call | solution.py:246
  25.3 3.4 %copy-done.1 = bf16[32,128,1024]{2,1,0:T(8,128)(2,1)} copy-done((bf16[32,128,1024]{2,1,0:T(8,128)(2,1)}, bf16[32,128,1024]{2,1,0:T(8,128)(2,1)S(1)}, u32[]{:S(2)}) %copy-start.1) | copy-done | bytes 8388632
  28.8 0.4 collective-permute-start.4
  29.2 0.5 collective-permute-start.3
  29.7 7.2 %collective-permute-done.7.refs_8_ = bf16[1024,128]{1,0:T(8,128)(2,1)S(1)} collective-permute-done((bf16[1024,128]{1,0:T(8,128)(2,1)S(1)}, bf16[1024,128]{1,0:T(8,128)(2,1)S(1)}, u32[]{:S(2)}, u32[]{:S(2)}) %collective-permute-start.7) | collective-permute-done | bytes 262176 | tf_op jit(solution)/shard_map/ppermute | solution.py:510
  36.9 0.5 collective-permute-start.8
  37.4 1.5 %collective-permute-start.12 = (bf16[1024,128]{1,0:T(8,128)(2,1)S(1)}, bf16[1024,128]{1,0:T(8,128)(2,1)S(1)}, u32[]{:S(2)}, u32[]{:S(2)}) collective-permute-start(bf16[1024,128]{1,0:T(8,128)(2,1)S(1)} %collective-permute-done.11.refs_12_), channel_id=1, source_target_pairs={{0,2},{1,3},{2,0},{3,1},{4,6},{5,7},{6,4},{7,5},{8,10},{9,11},{10,... | collective-permute-start | bytes 786440 | tf_op jit(solution)/shard_map/ppermute | solution.py:510
  39.4 0.5 collective-permute-start.13
  40.0 5.3 %collective-permute-done.8.refs_9_ = bf16[1024,128]{1,0:T(8,128)(2,1)S(1)} collective-permute-done((bf16[1024,128]{1,0:T(8,128)(2,1)S(1)}, bf16[1024,128]{1,0:T(8,128)(2,1)S(1)}, u32[]{:S(2)}, u32[]{:S(2)}) %collective-permute-start.8) | collective-permute-done | bytes 262176 | tf_op jit(solution)/shard_map/ppermute | solution.py:510
  45.2 2.8 %collective-permute-done.12.refs_13_ = bf16[1024,128]{1,0:T(8,128)(2,1)S(1)} collective-permute-done((bf16[1024,128]{1,0:T(8,128)(2,1)S(1)}, bf16[1024,128]{1,0:T(8,128)(2,1)S(1)}, u32[]{:S(2)}, u32[]{:S(2)}) %collective-permute-start.12) | collective-permute-done | bytes 262176 | tf_op jit(solution)/shard_map/ppermute | solution.py:510
  48.0 0.4 fusion.ids
  48.5 1.1 %collective-permute-done.14.refs_15_ = bf16[1024,128]{1,0:T(8,128)(2,1)S(1)} collective-permute-done((bf16[1024,128]{1,0:T(8,128)(2,1)S(1)}, bf16[1024,128]{1,0:T(8,128)(2,1)S(1)}, u32[]{:S(2)}, u32[]{:S(2)}) %collective-permute-start.14) | collective-permute-done | bytes 262176 | tf_op jit(solution)/shard_map/ppermute | solution.py:510
  49.6 13.7 %shard_map.79 = (bf16[32,64,1024]{2,1,0:T(8,128)(2,1)S(1)}, bf16[512,128]{1,0:T(8,128)(2,1)S(1)}, bf16[512,128]{1,0:T(8,128)(2,1)S(1)}, bf16[512,128]{1,0:T(8,128)(2,1)S(1)}, bf16[512,128]{1,0:T(8,128)(2,1)S(1)}) custom-call(bf16[32,128,1024]{2,1,0:T(8,128)(2,1)} %copy-done.1, bf16[256,512]{1,0:T(8,128)(2,1)S(1)} %fusion.1.choose, ...), custom_call_target="tpu_custom_call" | custom-call | flops 4294967296 | bytes 25165824 | tf_op jit(solution)/shard_map/pallas_call | solution.py:357
  63.3 1.9 %copy-done = bf16[32,64,1024]{2,1,0:T(8,128)(2,1)} copy-done((bf16[32,64,1024]{2,1,0:T(8,128)(2,1)}, bf16[32,64,1024]{2,1,0:T(8,128)(2,1)S(1)}, u32[]{:S(2)}) %copy-start) | copy-done | bytes 4194328
  65.3 1.9 %collective-permute-start.15 = (bf16[512,128]{1,0:T(8,128)(2,1)S(1)}, bf16[512,128]{1,0:T(8,128)(2,1)S(1)}, u32[]{:S(2)}, u32[]{:S(2)}) collective-permute-start(bf16[512,128]{1,0:T(8,128)(2,1)S(1)} %get-tuple-element.25), channel_id=1, source_target_pairs={{0,4},{4,0},{8,12},{12,8},{1,5},{5,1},{9,13},{13,9},{2,6},{6,2},{1... | collective-permute-start | bytes 393224 | tf_op jit(solution)/shard_map/ppermute | solution.py:510
  67.2 2.5 %collective-permute-start.16 = (bf16[512,128]{1,0:T(8,128)(2,1)S(1)}, bf16[512,128]{1,0:T(8,128)(2,1)S(1)}, u32[]{:S(2)}, u32[]{:S(2)}) collective-permute-start(bf16[512,128]{1,0:T(8,128)(2,1)S(1)} %get-tuple-element.26), channel_id=1, source_target_pairs={{0,8},{4,12},{8,0},{12,4},{1,9},{5,13},{9,1},{13,5},{2,10},{6,14},... | collective-permute-start | bytes 393224 | tf_op jit(solution)/shard_map/ppermute | solution.py:510
  69.7 14.4 %shard_map.80 = bf16[32,2,256,1024]{3,2,1,0:T(8,128)(2,1)} custom-call(s32[1]{0:T(128)} %bitcast.sub_index, s32[4]{0:T(128)} %counts.3, bf16[32,64,1024]{2,1,0:T(8,128)(2,1)} %copy-done, bf16[32,64,1024]{2,1,0:T(8,128)(2,1)} %copy-done), custom_call_target="tpu_custom_call" | custom-call | flops 2147483648 | bytes 33554432 | tf_op jit(solution)/shard_map/pallas_call | solution.py:424
  84.1 3.7 %shard_map.81 = f32[2752,128]{1,0:T(8,128)} custom-call(f32[12,256]{1,0:T(8,128)S(1)} %bitcast.91, f32[8,128]{1,0:T(8,128)S(1)} %broadcast_in_dim.18.turn_cos, s32[256,256]{1,0:T(8,128)S(1)} %get-tuple-element.28.index, bf16[512,128]{1,0:T(8,128)(2,1)S(1)} %get-tuple-element.24.refs_0_, bf16[512,128]{1,0:T(8,128)(2,1)S(1)} %collective-permute-done.15.refs_1_, ...), custom_call_target="tpu_custom_call" | custom-call | flops 2164260864 | bytes 4194304 | tf_op jit(solution)/shard_map/pallas_call | solution.py:491
  (70 shorter events, 1.5 us)
Async XLA Ops:
  4.4 0.7 copy-start.3
  5.1 1.4 %copy-start.4 = (bf16[64,2,5504]{2,1,0:T(2,128)(2,1)S(1)}, bf16[64,2,5504]{2,1,0:T(2,128)(2,1)}, u32[]{:S(2)}) copy-start(bf16[64,2,5504]{2,1,0:T(2,128)(2,1)} %param.6) | copy-start | bytes 4227076
  6.4 12.0 %copy-start.5 = (s32[256,1]{0,1:T(1,128)S(1)}, s32[256,1]{0,1:T(1,128)}, u32[]{:S(2)}) copy-start(s32[256,1]{0,1:T(1,128)} %param.11) | copy-start | bytes 3076
  6.4 12.3 %copy-start.2 = (s32[64,1024]{1,0:T(8,128)S(1)}, s32[64,1024]{1,0:T(8,128)}, u32[]{:S(2)}) copy-start(s32[64,1024]{1,0:T(8,128)} %delays.1) | copy-start | bytes 786436
  11.0 18.2 %collective-permute-start.1 = (bf16[1024,128]{1,0:T(8,128)(2,1)S(1)}, bf16[1024,128]{1,0:T(8,128)(2,1)S(1)}, u32[]{:S(2)}, u32[]{:S(2)}) collective-permute-start(bf16[1024,128]{1,0:T(8,128)(2,1)S(1)} %get-tuple-element.19.refs_0_), channel_id=1, source_target_pairs={{0,2},{1,3},{2,0},{3,1},{4,6},{5,7},{6,4},{7,5},{8,10},{9,11},{10,... | collective-permute-start | bytes 786440 | tf_op jit(solution)/shard_map/ppermute | solution.py:510
  14.0 15.2 %collective-permute-start.2 = (bf16[1024,128]{1,0:T(8,128)(2,1)S(1)}, bf16[1024,128]{1,0:T(8,128)(2,1)S(1)}, u32[]{:S(2)}, u32[]{:S(2)}) collective-permute-start(bf16[1024,128]{1,0:T(8,128)(2,1)S(1)} %get-tuple-element.19.refs_0_), channel_id=1, source_target_pairs={{0,1},{1,0},{2,3},{3,2},{4,5},{5,4},{6,7},{7,6},{8,9},{9,8},{10,11... | collective-permute-start | bytes 786440 | tf_op jit(solution)/shard_map/ppermute | solution.py:510
  14.0 14.8 %collective-permute-start = (bf16[1024,128]{1,0:T(8,128)(2,1)S(1)}, bf16[1024,128]{1,0:T(8,128)(2,1)S(1)}, u32[]{:S(2)}, u32[]{:S(2)}) collective-permute-start(bf16[1024,128]{1,0:T(8,128)(2,1)S(1)} %get-tuple-element.15), channel_id=1, source_target_pairs={{0,4},{4,0},{8,12},{12,8},{1,5},{5,1},{9,13},{13,9},{2,6},{6,2},{1... | collective-permute-start | bytes 786440 | tf_op jit(solution)/shard_map/ppermute | solution.py:510
  15.6 21.3 %collective-permute-start.7 = (bf16[1024,128]{1,0:T(8,128)(2,1)S(1)}, bf16[1024,128]{1,0:T(8,128)(2,1)S(1)}, u32[]{:S(2)}, u32[]{:S(2)}) collective-permute-start(bf16[1024,128]{1,0:T(8,128)(2,1)S(1)} %get-tuple-element.21), channel_id=1, source_target_pairs={{0,8},{4,12},{8,0},{12,4},{1,9},{5,13},{9,1},{13,5},{2,10},{6,14},... | collective-permute-start | bytes 786440 | tf_op jit(solution)/shard_map/ppermute | solution.py:510
  18.1 19.3 %collective-permute-start.11 = (bf16[1024,128]{1,0:T(8,128)(2,1)S(1)}, bf16[1024,128]{1,0:T(8,128)(2,1)S(1)}, u32[]{:S(2)}, u32[]{:S(2)}) collective-permute-start(bf16[1024,128]{1,0:T(8,128)(2,1)S(1)} %get-tuple-element.22), channel_id=1, source_target_pairs={{0,12},{4,8},{8,4},{12,0},{1,13},{5,9},{9,5},{13,1},{2,14},{6,10},... | collective-permute-start | bytes 786440 | tf_op jit(solution)/shard_map/ppermute | solution.py:510
  25.3 3.4 %copy-start.1 = (bf16[32,128,1024]{2,1,0:T(8,128)(2,1)}, bf16[32,128,1024]{2,1,0:T(8,128)(2,1)S(1)}, u32[]{:S(2)}) copy-start(bf16[32,128,1024]{2,1,0:T(8,128)(2,1)S(1)} %shard_map.78.weights) | copy-start | bytes 25165828
  28.8 10.6 %collective-permute-start.4 = (bf16[1024,128]{1,0:T(8,128)(2,1)S(1)}, bf16[1024,128]{1,0:T(8,128)(2,1)S(1)}, u32[]{:S(2)}, u32[]{:S(2)}) collective-permute-start(bf16[1024,128]{1,0:T(8,128)(2,1)S(1)} %collective-permute-done.refs_4_), channel_id=1, source_target_pairs={{0,2},{1,3},{2,0},{3,1},{4,6},{5,7},{6,4},{7,5},{8,10},{9,11},{10,... | collective-permute-start | bytes 786440 | tf_op jit(solution)/shard_map/ppermute | solution.py:510
  29.2 10.7 %collective-permute-start.5 = (bf16[1024,128]{1,0:T(8,128)(2,1)S(1)}, bf16[1024,128]{1,0:T(8,128)(2,1)S(1)}, u32[]{:S(2)}, u32[]{:S(2)}) collective-permute-start(bf16[1024,128]{1,0:T(8,128)(2,1)S(1)} %collective-permute-done.refs_4_), channel_id=1, source_target_pairs={{0,1},{1,0},{2,3},{3,2},{4,5},{5,4},{6,7},{7,6},{8,9},{9,8},{10,11... | collective-permute-start | bytes 786440 | tf_op jit(solution)/shard_map/ppermute | solution.py:510
  29.2 10.1 %collective-permute-start.3 = (bf16[1024,128]{1,0:T(8,128)(2,1)S(1)}, bf16[1024,128]{1,0:T(8,128)(2,1)S(1)}, u32[]{:S(2)}, u32[]{:S(2)}) collective-permute-start(bf16[1024,128]{1,0:T(8,128)(2,1)S(1)} %collective-permute-done.1.refs_1_), channel_id=1, source_target_pairs={{0,1},{1,0},{2,3},{3,2},{4,5},{5,4},{6,7},{7,6},{8,9},{9,8},{10,11... | collective-permute-start | bytes 786440 | tf_op jit(solution)/shard_map/ppermute | solution.py:510
  36.9 8.4 %collective-permute-start.8 = (bf16[1024,128]{1,0:T(8,128)(2,1)S(1)}, bf16[1024,128]{1,0:T(8,128)(2,1)S(1)}, u32[]{:S(2)}, u32[]{:S(2)}) collective-permute-start(bf16[1024,128]{1,0:T(8,128)(2,1)S(1)} %collective-permute-done.7.refs_8_), channel_id=1, source_target_pairs={{0,2},{1,3},{2,0},{3,1},{4,6},{5,7},{6,4},{7,5},{8,10},{9,11},{10,... | collective-permute-start | bytes 786440 | tf_op jit(solution)/shard_map/ppermute | solution.py:510
  37.4 10.6 %collective-permute-start.12 = (bf16[1024,128]{1,0:T(8,128)(2,1)S(1)}, bf16[1024,128]{1,0:T(8,128)(2,1)S(1)}, u32[]{:S(2)}, u32[]{:S(2)}) collective-permute-start(bf16[1024,128]{1,0:T(8,128)(2,1)S(1)} %collective-permute-done.11.refs_12_), channel_id=1, source_target_pairs={{0,2},{1,3},{2,0},{3,1},{4,6},{5,7},{6,4},{7,5},{8,10},{9,11},{10,... | collective-permute-start | bytes 786440 | tf_op jit(solution)/shard_map/ppermute | solution.py:510
  39.3 9.2 %collective-permute-start.9 = (bf16[1024,128]{1,0:T(8,128)(2,1)S(1)}, bf16[1024,128]{1,0:T(8,128)(2,1)S(1)}, u32[]{:S(2)}, u32[]{:S(2)}) collective-permute-start(bf16[1024,128]{1,0:T(8,128)(2,1)S(1)} %collective-permute-done.7.refs_8_), channel_id=1, source_target_pairs={{0,1},{1,0},{2,3},{3,2},{4,5},{5,4},{6,7},{7,6},{8,9},{9,8},{10,11... | collective-permute-start | bytes 786440 | tf_op jit(solution)/shard_map/ppermute | solution.py:510
  39.4 9.1 %collective-permute-start.13 = (bf16[1024,128]{1,0:T(8,128)(2,1)S(1)}, bf16[1024,128]{1,0:T(8,128)(2,1)S(1)}, u32[]{:S(2)}, u32[]{:S(2)}) collective-permute-start(bf16[1024,128]{1,0:T(8,128)(2,1)S(1)} %collective-permute-done.11.refs_12_), channel_id=1, source_target_pairs={{0,1},{1,0},{2,3},{3,2},{4,5},{5,4},{6,7},{7,6},{8,9},{9,8},{10,11... | collective-permute-start | bytes 786440 | tf_op jit(solution)/shard_map/ppermute | solution.py:510
  39.9 8.6 %collective-permute-start.6 = (bf16[1024,128]{1,0:T(8,128)(2,1)S(1)}, bf16[1024,128]{1,0:T(8,128)(2,1)S(1)}, u32[]{:S(2)}, u32[]{:S(2)}) collective-permute-start(bf16[1024,128]{1,0:T(8,128)(2,1)S(1)} %collective-permute-done.4.refs_5_), channel_id=1, source_target_pairs={{0,1},{1,0},{2,3},{3,2},{4,5},{5,4},{6,7},{7,6},{8,9},{9,8},{10,11... | collective-permute-start | bytes 786440 | tf_op jit(solution)/shard_map/ppermute | solution.py:510
  45.2 3.3 %collective-permute-start.10 = (bf16[1024,128]{1,0:T(8,128)(2,1)S(1)}, bf16[1024,128]{1,0:T(8,128)(2,1)S(1)}, u32[]{:S(2)}, u32[]{:S(2)}) collective-permute-start(bf16[1024,128]{1,0:T(8,128)(2,1)S(1)} %collective-permute-done.8.refs_9_), channel_id=1, source_target_pairs={{0,1},{1,0},{2,3},{3,2},{4,5},{5,4},{6,7},{7,6},{8,9},{9,8},{10,11... | collective-permute-start | bytes 786440 | tf_op jit(solution)/shard_map/ppermute | solution.py:510
  48.0 1.5 %collective-permute-start.14 = (bf16[1024,128]{1,0:T(8,128)(2,1)S(1)}, bf16[1024,128]{1,0:T(8,128)(2,1)S(1)}, u32[]{:S(2)}, u32[]{:S(2)}) collective-permute-start(bf16[1024,128]{1,0:T(8,128)(2,1)S(1)} %collective-permute-done.12.refs_13_), channel_id=1, source_target_pairs={{0,1},{1,0},{2,3},{3,2},{4,5},{5,4},{6,7},{7,6},{8,9},{9,8},{10,11... | collective-permute-start | bytes 786440 | tf_op jit(solution)/shard_map/ppermute | solution.py:510
  63.3 2.0 %copy-start = (bf16[32,64,1024]{2,1,0:T(8,128)(2,1)}, bf16[32,64,1024]{2,1,0:T(8,128)(2,1)S(1)}, u32[]{:S(2)}) copy-start(bf16[32,64,1024]{2,1,0:T(8,128)(2,1)S(1)} %get-tuple-element.23.mine.by_id) | copy-start | bytes 12582916
  65.3 18.8 %collective-permute-start.15 = (bf16[512,128]{1,0:T(8,128)(2,1)S(1)}, bf16[512,128]{1,0:T(8,128)(2,1)S(1)}, u32[]{:S(2)}, u32[]{:S(2)}) collective-permute-start(bf16[512,128]{1,0:T(8,128)(2,1)S(1)} %get-tuple-element.25), channel_id=1, source_target_pairs={{0,4},{4,0},{8,12},{12,8},{1,5},{5,1},{9,13},{13,9},{2,6},{6,2},{1... | collective-permute-start | bytes 393224 | tf_op jit(solution)/shard_map/ppermute | solution.py:510
  67.2 16.9 %collective-permute-start.16 = (bf16[512,128]{1,0:T(8,128)(2,1)S(1)}, bf16[512,128]{1,0:T(8,128)(2,1)S(1)}, u32[]{:S(2)}, u32[]{:S(2)}) collective-permute-start(bf16[512,128]{1,0:T(8,128)(2,1)S(1)} %get-tuple-element.26), channel_id=1, source_target_pairs={{0,8},{4,12},{8,0},{12,4},{1,9},{5,13},{9,1},{13,5},{2,10},{6,14},... | collective-permute-start | bytes 393224 | tf_op jit(solution)/shard_map/ppermute | solution.py:510
  69.7 14.5 %collective-permute-start.17 = (bf16[512,128]{1,0:T(8,128)(2,1)S(1)}, bf16[512,128]{1,0:T(8,128)(2,1)S(1)}, u32[]{:S(2)}, u32[]{:S(2)}) collective-permute-start(bf16[512,128]{1,0:T(8,128)(2,1)S(1)} %get-tuple-element.27), channel_id=1, source_target_pairs={{0,12},{4,8},{8,4},{12,0},{1,13},{5,9},{9,5},{13,1},{2,14},{6,10},... | collective-permute-start | bytes 393224 | tf_op jit(solution)/shard_map/ppermute | solution.py:510

commit v3 on v2

--- a/solution.py
+++ b/solution.py
@@ -16,6 +16,8 @@
 BEAMS = 256
 LANES = 128
 MIB = 1024 * 1024
+HALVES = 1
+VIS_LIMIT = 58
 
 
 def filter_table(taps, chans):
@@ -149,14 +151,16 @@
     )
 
 
-def filter_kernel(inp, group, spectra_n, pieces, counts, voltages, taps_col, turn_cos, index, *rest):
+def filter_kernel(inp, group, spectra_n, pieces, counts, voltages, taps, turn_cos, index, *rest):
     *flat, table, wide, frames = rest
     outs = nested(flat, pieces)
     depth = index.shape[0]
     frames_n = spectra_n + TAPS - 1
     base = turned_by(turn_cos[0:1, :], index[...])
+    tall = jnp.concatenate([taps[...], jnp.zeros((-TAPS % 8, NCH), jnp.float32)], axis=0).T
+    tall = jnp.concatenate([tall, tall], axis=0)
     for k in range(TAPS):
-        table[k * depth : (k + 1) * depth, :] = (taps_col[:, k : k + 1] * base).astype(
+        table[k * depth : (k + 1) * depth, :] = (tall[:, k : k + 1] * base).astype(
             jnp.bfloat16
         )
     wide[...] = voltages[...].astype(jnp.float32)
@@ -195,7 +199,7 @@
                 ).astype(jnp.bfloat16)
 
 
-def run_filter(counts, voltages, taps_col, turn_cos, index, inp, pieces, spectra_n):
+def run_filter(counts, voltages, taps, turn_cos, index, inp, pieces, spectra_n):
     depth, columns = index.shape
     pack = LANES * len(pieces) // columns
     flat = pl.pallas_call(
@@ -212,66 +216,45 @@
             pltpu.VMEM(voltages.shape, jnp.float32),
             pltpu.VMEM((voltages.shape[0] // 2, 2 * NCH), jnp.bfloat16),
         ],
-        compiler_params=pltpu.CompilerParams(vmem_limit_bytes=32 * MIB),
+        compiler_params=pltpu.CompilerParams(vmem_limit_bytes=36 * MIB),
         cost_estimate=pl.CostEstimate(
             flops=2 * spectra_n * inp * TAPS * depth * columns,
             bytes_accessed=4 * MIB,
             transcendentals=0,
         ),
-    )(counts, voltages, taps_col, turn_cos, index)
+    )(counts, voltages, taps, turn_cos, index)
     return nested(flat, pieces)
 
 
-def weight_kernel(first, delays, turn_cos, turn_sin, out):
-    some = out.shape[0]
-    section, inputs = delays.shape
-    cosine = jnp.broadcast_to(turn_cos[0:1, :], (section, LANES))
-    sine = jnp.broadcast_to(turn_sin[0:1, :], (section, LANES))
-    for part in range(some):
-        channel = first[0] + pl.program_id(0) * some + part
-        for block in range(inputs // LANES):
-            lanes = slice(block * LANES, (block + 1) * LANES)
-            phase = (delays[:, lanes] * channel) & (NCH - 1)
-            out[part, :section, lanes] = jnp.take_along_axis(cosine, phase, axis=1).astype(
-                jnp.bfloat16
-            )
-            out[part, section:, lanes] = jnp.take_along_axis(sine, phase, axis=1).astype(
-                jnp.bfloat16
-            )
-
-
-def run_weights(first, delays, turn_cos, turn_sin, ch_dev):
-    section, inputs = delays.shape
-    some = math.gcd(4, ch_dev)
-    return pl.pallas_call(
-        weight_kernel,
-        out_shape=jax.ShapeDtypeStruct((ch_dev, 2 * section, inputs), jnp.bfloat16),
-        grid=(ch_dev // some,),
-        in_specs=[
-            SCALARS,
-            whole(delays.shape),
-            whole(turn_cos.shape),
-            whole(turn_sin.shape),
-        ],
-        out_specs=pl.BlockSpec((some, 2 * section, inputs), lambda f: (f, 0, 0)),
-        compiler_params=pltpu.CompilerParams(vmem_limit_bytes=16 * MIB),
-        cost_estimate=pl.CostEstimate(
-            flops=8 * ch_dev * section * inputs,
-            bytes_accessed=4 * ch_dev * section * inputs,
-            transcendentals=0,
-        ),
-    )(first, delays, turn_cos, turn_sin)
-
-
-def beam_kernel(sizes, pieces, n_dest, weights, choose, ids, *refs):
+def id_matrix(order, place, input_id, ids):
+    inputs = ids.shape[0]
+    inp = input_id.shape[1]
+    n_sub = len(order)
+    line = lax.broadcasted_iota(jnp.int32, (inputs, LANES), 0)
+    slots = [(d, o) for d in range(input_id.shape[0] // n_sub) for o in order]
+    together = LANES // inp
+    for block in range(inputs // LANES):
+        carried = jnp.concatenate(
+            [
+                input_id[pl.ds((place[1] ^ d) * n_sub + (place[2] ^ o), 1), :]
+                for d, o in slots[block * together : (block + 1) * together]
+            ],
+            axis=1,
+        )
+        ids[:, block * LANES : (block + 1) * LANES] = jnp.where(
+            jnp.broadcast_to(carried, line.shape) == line, 1.0, 0.0
+        ).astype(jnp.bfloat16)
+
+
+def beam_kernel(sizes, order, pieces, n_dest, place, delays, turn_cos, input_id, choose, *refs):
     inp, ch_dev, spectra_n, most = sizes
     blocks, refs = nested(refs[: sum(pieces)], pieces), refs[sum(pieces) :]
     by_id, sent = refs[0], refs[1 : 1 + n_dest]
-    turned, formed, ordered, out_sem = refs[1 + n_dest :]
+    turned, formed, ordered, ids, out_sem = refs[1 + n_dest :]
     width = 2 * ch_dev
     pitch = width + 8
     packed = spectra_n * width // LANES
-    section = weights.shape[1] // 2
+    section, inputs = delays.shape
     n_parts = out_sem.shape[0]
     part = ch_dev // n_parts
 
@@ -279,6 +262,26 @@
         lines = pl.ds(p * part, part)
         return pltpu.make_async_copy(ordered.at[lines], by_id.at[lines], out_sem.at[p])
 
+    cosine = jnp.broadcast_to(turn_cos[0:1, :] * (1.0 / math.sqrt(inputs)), (section, LANES))
+    sine = jnp.concatenate([cosine[:, -NCH // 4 :], cosine[:, : -NCH // 4]], axis=1)
+
+    def weights(channel):
+        phase = (delays[...] * (place[0] + channel)) & (NCH - 1)
+        return jnp.concatenate(
+            [
+                jnp.concatenate(
+                    [
+                        jnp.take_along_axis(wave, phase[:, j : j + LANES], axis=1)
+                        for j in range(0, inputs, LANES)
+                    ],
+                    axis=1,
+                )
+                for wave in (cosine, sine)
+            ],
+            axis=0,
+        ).astype(jnp.bfloat16)
+
+    id_matrix(order, place, input_id, ids)
     together = 4
     for first in range(0, packed, together):
         left = jnp.concatenate(
@@ -296,11 +299,11 @@
             ],
             axis=1,
         )
-        got = dot(left, ids[...], ((0,), (0,)))
+        got = dot(left, ids[...], ((0,), (1,)))
         for j in range(turned.shape[0]):
             for row in range(0, together * LANES, width):
-                place = (first * LANES + row) // width * pitch
-                turned[j, place : place + width, :] = got[
+                spot = (first * LANES + row) // width * pitch
+                turned[j, spot : spot + width, :] = got[
                     row : row + width, j * LANES : (j + 1) * LANES
                 ]
 
@@ -320,7 +323,7 @@
                 axis=0,
             ).astype(jnp.bfloat16)
             ordered[channel] = both
-            got = dot(both, weights[channel], ((1,), (1,)))
+            got = dot(both, weights(channel), ((1,), (1,)))
             real = got[:spectra_n, :section] - got[spectra_n:, section:]
             imag = got[spectra_n:, :section] + got[:spectra_n, section:]
             for c, value in enumerate((real, imag)):
@@ -347,8 +350,9 @@
         store(p).wait()
 
 
-def run_beams(weights, choose, ids, blocks, inp, spectra_n, most, n_dest):
-    ch_dev, twice, inputs = weights.shape
+def run_beams(place, delays, turn_cos, input_id, choose, order, blocks, ch_dev, spectra_n, most, n_dest):
+    section, inputs = delays.shape
+    inp = input_id.shape[1]
     width = 2 * ch_dev
     out_rows = spectra_n // (LANES // most) * width
     n_parts = math.gcd(8, ch_dev)
@@ -356,28 +360,34 @@
     anywhere = pl.BlockSpec(memory_space=pltpu.HBM)
     return pl.pallas_call(
         functools.partial(
-            beam_kernel, (inp, ch_dev, spectra_n, most), [len(parts) for parts in blocks], n_dest
+            beam_kernel,
+            (inp, ch_dev, spectra_n, most),
+            order,
+            [len(parts) for parts in blocks],
+            n_dest,
         ),
         out_shape=[jax.ShapeDtypeStruct((ch_dev, 2 * spectra_n, inputs), jnp.bfloat16)]
         + [jax.ShapeDtypeStruct((out_rows, LANES), jnp.bfloat16)] * n_dest,
-        in_specs=[vmem, vmem, vmem] + [vmem] * sum(len(parts) for parts in blocks),
+        in_specs=[SCALARS] + [vmem] * 4 + [vmem] * sum(len(parts) for parts in blocks),
         out_specs=[anywhere] + [vmem] * n_dest,
         scratch_shapes=[
             pltpu.VMEM((inputs // LANES, spectra_n * (width + 8), LANES), jnp.float32),
             pltpu.VMEM((spectra_n * (width + 8), LANES), jnp.float32),
             pltpu.VMEM((ch_dev, 2 * spectra_n, inputs), jnp.bfloat16),
+            pltpu.VMEM((inputs, inputs), jnp.bfloat16),
             pltpu.SemaphoreType.DMA((n_parts,)),
         ],
-        compiler_params=pltpu.CompilerParams(vmem_limit_bytes=36 * MIB),
+        compiler_params=pltpu.CompilerParams(vmem_limit_bytes=46 * MIB),
         cost_estimate=pl.CostEstimate(
             flops=2 * spectra_n * width * inputs * inputs,
             bytes_accessed=24 * MIB,
             transcendentals=0,
         ),
-    )(weights, choose, ids, *[part for parts in blocks for part in parts])
-
-
-def visibility_kernel(sub_index, counts, mine, by_id, out, held, sem):
+    )(place, delays, turn_cos, input_id, choose, *[part for parts in blocks for part in parts])
+
+
+def visibility_kernel(first, sub_index, counts, mine, by_id, *rest):
+    *_, out, held, sem = rest
     del sub_index
     some, depth, rows = mine.shape
     half = depth // 2
@@ -389,7 +399,7 @@
 
     def store(part, at):
         slot = at % 2 * some + part
-        return pltpu.make_async_copy(held.at[slot], out.at[at * some + part], sem.at[slot])
+        return pltpu.make_async_copy(held.at[slot], out.at[first + at * some + part], sem.at[slot])
 
     @pl.when(step > 1)
     def _():
@@ -418,40 +428,49 @@
                     store(part, step - before).wait()
 
 
-def run_visibility(sub_index, counts, by_id, rows):
-    ch_dev, depth, inputs = by_id.shape
-    some = math.gcd(4, ch_dev)
+def run_visibility(sub_index, counts, by_id, skip, many, first, shape, before):
+    depth, inputs = by_id.shape[1:]
+    rows = shape[2]
+    some = math.gcd(4, many)
+    chained = [] if before is None else [before]
     return pl.pallas_call(
-        visibility_kernel,
-        out_shape=jax.ShapeDtypeStruct((ch_dev, 2, rows, inputs), jnp.bfloat16),
+        functools.partial(visibility_kernel, first),
+        out_shape=jax.ShapeDtypeStruct(shape, jnp.bfloat16),
         grid_spec=pltpu.PrefetchScalarGridSpec(
             num_scalar_prefetch=2,
-            grid=(ch_dev // some,),
+            grid=(many // some,),
             in_specs=[
-                pl.BlockSpec((some, depth, rows), lambda f, sub, counts: (f, 0, sub[0])),
-                pl.BlockSpec((some, depth, inputs), lambda f, sub, counts: (f, 0, 0)),
-            ],
+                pl.BlockSpec(
+                    (some, depth, rows), lambda f, sub, counts: (f + skip // some, 0, sub[0])
+                ),
+                pl.BlockSpec(
+                    (some, depth, inputs), lambda f, sub, counts: (f + skip // some, 0, 0)
+                ),
+            ]
+            + [pl.BlockSpec(memory_space=pl.ANY) for _ in chained],
             out_specs=pl.BlockSpec(memory_space=pltpu.HBM),
             scratch_shapes=[
                 pltpu.VMEM((2 * some, 2, rows, inputs), jnp.bfloat16),
                 pltpu.SemaphoreType.DMA((2 * some,)),
             ],
         ),
-        compiler_params=pltpu.CompilerParams(vmem_limit_bytes=60 * MIB),
+        input_output_aliases={4: 0} if chained else {},
+        compiler_params=pltpu.CompilerParams(vmem_limit_bytes=VIS_LIMIT * MIB),
         cost_estimate=pl.CostEstimate(
-            flops=4 * ch_dev * depth * rows * inputs,
-            bytes_accessed=4 * ch_dev * rows * inputs,
+            flops=4 * many * depth * rows * inputs,
+            bytes_accessed=4 * many * rows * inputs,
             transcendentals=0,
         ),
-    )(sub_index, counts, by_id, by_id)
-
-
-def resynth_kernel(most, spectra_n, taps_row, turn_cos, index, *refs):
+    )(sub_index, counts, by_id, by_id, *chained)
+
+
+def resynth_kernel(most, spectra_n, taps, turn_cos, index, *refs):
     *blocks, out, table, window = refs
     depth, width = index.shape
     base = turned_by(turn_cos[0:1, :], index[...])
+    wide = jnp.concatenate([taps[...], taps[...]], axis=1)
     for k in range(TAPS):
-        table[k * depth : (k + 1) * depth, :] = (taps_row[k : k + 1, :] * base).astype(
+        table[k * depth : (k + 1) * depth, :] = (wide[k : k + 1, :] * base).astype(
             jnp.bfloat16
         )
     per = LANES // most
@@ -486,7 +505,7 @@
                 ]
 
 
-def run_resynth(taps_row, turn_cos, index, blocks, most, spectra_n):
+def run_resynth(taps, turn_cos, index, blocks, most, spectra_n):
     frames_n = spectra_n + TAPS - 1
     return pl.pallas_call(
         functools.partial(resynth_kernel, most, spectra_n),
@@ -497,13 +516,13 @@
             pltpu.VMEM((TAPS * index.shape[0], index.shape[1]), jnp.bfloat16),
             pltpu.VMEM(((spectra_n + 2 * (TAPS - 1)) * most, index.shape[0]), jnp.bfloat16),
         ],
-        compiler_params=pltpu.CompilerParams(vmem_limit_bytes=32 * MIB),
+        compiler_params=pltpu.CompilerParams(vmem_limit_bytes=36 * MIB),
         cost_estimate=pl.CostEstimate(
             flops=2 * frames_n * most * TAPS * index.size,
             bytes_accessed=4 * MIB,
             transcendentals=0,
         ),
-    )(taps_row, turn_cos, index, *blocks)
+    )(taps, turn_cos, index, *blocks)
 
 
 def swap(x, axis, size, mask):
@@ -526,13 +545,14 @@
     turn = 2.0 * math.pi / NCH
 
     partner = chan_index ^ jnp.arange(n_chan, dtype=jnp.int32)
-    column_channel = jnp.broadcast_to(
-        (partner[:, None, None] * ch_dev + jnp.arange(ch_dev, dtype=jnp.int32)[None, None, :]),
-        (n_chan, 2, ch_dev),
+    ch_half = ch_dev // HALVES
+    shape = (n_chan, HALVES, 2, ch_half)
+    column_channel = (
+        partner[:, None, None, None] * ch_dev
+        + lax.broadcasted_iota(jnp.int32, shape, 1) * ch_half
+        + lax.broadcasted_iota(jnp.int32, shape, 3)
     ).reshape(-1)
-    column_part = jnp.broadcast_to(
-        jnp.arange(2, dtype=jnp.int32)[None, :, None], (n_chan, 2, ch_dev)
-    ).reshape(-1)
+    column_part = lax.broadcasted_iota(jnp.int32, shape, 2).reshape(-1)
     row_place = jnp.tile(jnp.arange(NCH, dtype=jnp.int32), 2)
     row_part = jnp.repeat(jnp.arange(2, dtype=jnp.int32), NCH)
 
@@ -548,9 +568,7 @@
     )
     phases = jnp.arange(NCH, dtype=jnp.int32).astype(jnp.float32) * turn
     turn_cos = jnp.broadcast_to(jnp.cos(phases)[None, :], (8, NCH))
-    turn_sin = jnp.broadcast_to(jnp.sin(phases)[None, :], (8, NCH))
-    taps_row = jnp.tile(taps.reshape(TAPS, NCH), (1, 2))
-    taps_col = taps_row.T
+    taps2 = taps.reshape(TAPS, NCH)
 
     lines = jnp.transpose(
         with_layout_constraint(
@@ -559,13 +577,10 @@
         ),
         (0, 2, 1, 3),
     ).reshape(2 * inp * frames_n, NCH)
-    pieces = [1] * n_chan
-    if spectra_n * ch_dev * 2 // LANES % 2 == 0:
-        pieces[-1] = 1
-    outgoing = run_filter(counts, lines, taps_col, turn_cos, index, inp, pieces, spectra_n)
-    turned = [outgoing[0]] + [
-        [swap(x, "chan", n_chan, d) for x in outgoing[d]] for d in range(1, n_chan)
-    ]
+    outgoing = run_filter(
+        counts, lines, taps2, turn_cos, index, inp, [1] * (n_chan * HALVES), spectra_n
+    )
+    leaving = [[outgoing[d * HALVES + h][0] for d in range(n_chan)] for h in range(HALVES)]
 
     masks = []
     order = [0]
@@ -574,32 +589,6 @@
         far //= 2
         masks.append(far)
         order = order + [o ^ far for o in order]
-    id_table = input_id.reshape(n_chan, n_sub, inp)
-    slot_id = jnp.stack(
-        [
-            lax.dynamic_slice(id_table, (chan_index ^ d, sub_index ^ o, 0), (1, 1, inp))
-            for d in range(n_chan)
-            for o in order
-        ]
-    ).reshape(-1)
-    scale = 1.0 / math.sqrt(inputs)
-    weights = run_weights(
-        (chan_index * ch_dev).reshape(1).astype(jnp.int32),
-        delays,
-        turn_cos * scale,
-        turn_sin * scale,
-        ch_dev,
-    )
-    turned[1][0], weights = lax.optimization_barrier((turned[1][0], weights))
-    turned[0][0], slot_id = lax.optimization_barrier((turned[0][0], slot_id))
-    ids = (slot_id[:, None] == jnp.arange(inputs, dtype=jnp.int32)[None, :]).astype(jnp.bfloat16)
-    blocks = []
-    for parts in turned:
-        held = [parts]
-        for mask in masks:
-            held = held + [[swap(x, "sub", n_sub, mask) for x in those] for those in held]
-        blocks.extend(held)
-
     owner = lax.dynamic_slice_in_dim(beam_owner[:, 0], sub_index * section, section)
     beam = jnp.arange(section, dtype=jnp.int32)
     earlier = (owner[None, :] == owner[:, None]) & (beam[None, :] < beam[:, None])
@@ -612,12 +601,40 @@
         == target[None, :, None] + (jnp.arange(per, dtype=jnp.int32) * most)[:, None, None]
     ).astype(jnp.bfloat16).reshape(per * section, n_chan * per * most)
 
-    by_id, *leaving = run_beams(weights, choose, ids, blocks, inp, spectra_n, most, n_chan)
-    arrived = [leaving[0]] + [swap(leaving[d], "chan", n_chan, d) for d in range(1, n_chan)]
-    visibility = run_visibility(
-        sub_index.reshape(1).astype(jnp.int32), counts, by_id, rows
-    )
-    voice = run_resynth(taps_row, turn_cos, index_back, arrived, most, spectra_n)
+    id_rows = input_id.reshape(n_chan * n_sub, inp)
+
+    def to_owners(h, d):
+        return swap(leaving[h][d], "chan", n_chan, d)
+
+    def to_all(block):
+        held = [block]
+        for mask in masks:
+            held = held + [swap(x, "sub", n_sub, mask) for x in held]
+        return [[x] for x in held]
+
+    place = jnp.stack([chan_index * ch_dev, chan_index, sub_index]).astype(jnp.int32)
+
+    def beams_of(arrived):
+        blocks = [part for block in arrived for part in to_all(block)]
+        return run_beams(
+            place, delays, turn_cos, id_rows, choose, order, blocks, ch_half, spectra_n, most, n_chan
+        )
+
+    def formed_to_owners(sent):
+        return [sent[0]] + [swap(sent[d], "chan", n_chan, d) for d in range(1, n_chan)]
+
+    whole_shape = (ch_dev, 2, rows, inputs)
+    sub_at = sub_index.reshape(1).astype(jnp.int32)
+    partners = range(1, n_chan)
+
+    turned = [leaving[0][0]] + [to_owners(0, d) for d in partners]
+    turned[1], choose, id_rows, place = lax.optimization_barrier(
+        (turned[1], choose, id_rows, place)
+    )
+    by_id, *sent = beams_of(turned)
+    back = formed_to_owners(sent)
+    visibility = run_visibility(sub_at, counts, by_id, 0, ch_dev, 0, whole_shape, None)
+    voice = run_resynth(taps2, turn_cos, index_back, back, most, spectra_n)
     resynth = with_layout_constraint(
         jnp.transpose(voice.reshape(most, frames_n, 2, NCH), (0, 2, 1, 3)),
         Layout(major_to_minor=(0, 2, 1, 3)),
@@ -634,13 +651,18 @@
     n_sub = lax.axis_size("sub")
     section = BEAMS // n_sub
     most = min(section, max(2, 2 * section // n_chan))
-    width = 2 * NCH // n_chan
+    width = 2 * NCH // n_chan // HALVES
     fits = (
         power_of_two(n_chan)
+        and n_chan >= 4
         and power_of_two(n_sub)
         and voltages.shape[0] % 16 == 0
+        and LANES % voltages.shape[0] == 0
         and LANES % width == 0
-        and width % 32 == 0
+        and width % 16 == 0
+        and width * HALVES == 2 * NCH // n_chan
+        and width % 8 == 0
+        and width // 2 % 8 == 0
         and LANES % most == 0
         and most % 16 == 0
         and section % 16 == 0

time: 88.3 us -> 81.5 us (0.923)
  waiting for transfers between devices: 16.4 us -> 26.9 us
  Pallas kernels: 42.9 us -> 34.1 us
  local copies, waits for them, and re-layouts: 10.3 us -> 3.29 us
  other arithmetic: 1.85 us -> 0.79 us
    ppermute x18, waiting for transfers between devices: 16.4 us -> 26.9 us  [swap(): return lax.ppermute(x, axis, [(i, i ^ mask) for i in range(size)])]
    pallas_call x2 -> x1, Pallas kernels: 21 us -> 14.6 us  [run_visibility(): pl.pallas_call(functools.partial(visibility_kernel, first), out_shape=jax...]
    unnamed x29 -> x14, local copies, waits for them, and re-layouts: 7.61 us -> 2.71 us
    pallas_call x1, Pallas kernels: 13.7 us -> 11.3 us  [run_beams(): pl.pallas_call(functools.partial(beam_kernel, (inp, ch_dev, spectra_n, mo...]
    another operation x3 -> x0, local copies, waits for them, and re-layouts: 1.24 us -> none  [the longest x1 0.7 us: quick(): taps_row = jnp.tile(taps.reshape(TAPS, NCH), (1, 2))]
  transfers between devices with their start and end apart: 18 -> 18, of which waited for: 4 -> 5; matrix products, arithmetic and copies ran while one was open for 1% -> 1% of each run, Pallas kernels for 24% -> 18%
where the time goes in v3:
time: 81.5 us; the launch traced here: 81.1 us
  Pallas kernels  34.1 us (42%)
  waiting for transfers between devices  26.9 us (33%)
  starting transfers between devices  15.3 us (19%)
  local copies, waits for them, and re-layouts  3.29 us (4%)
    ppermute x18, waiting for transfers between devices, swap(): return lax.ppermute(x, axis, [(i, i ^ mask) for i in range(size)])  26.9 us
    ppermute x18, starting transfers between devices, swap(): return lax.ppermute(x, axis, [(i, i ^ mask) for i in range(size)])  15.3 us
    pallas_call x1, Pallas kernels, run_visibility(): pl.pallas_call(functools.partial(visibility_kernel, first), out_shape=jax...  14.6 us
    pallas_call x1, Pallas kernels, run_beams(): pl.pallas_call(functools.partial(beam_kernel, (inp, ch_dev, spectra_n, mo...  11.3 us
    pallas_call x1, Pallas kernels, run_filter(): pl.pallas_call(functools.partial(filter_kernel, inp, 4, spectra_n, pieces...  4.55 us
    pallas_call x1, Pallas kernels, run_resynth(): pl.pallas_call(functools.partial(resynth_kernel, most, spectra_n), out_sh...  3.66 us
    unnamed x14, local copies, waits for them, and re-layouts  2.71 us
  transfers between devices with their start and end apart: 18, of which 5 were waited for; matrix products, arithmetic and copies ran while one was open for 1% of the time, Pallas kernels for 18%

profile of v3, /device:TPU:0, one launch (start us, length us, event | category | flops | bytes accessed | tf_op | source)
XLA Modules:
  0.0 81.1 jit_solution(4909334677350632290)
XLA Ops:
  0.7 0.1 sub.34
  0.9 0.1 add.61
  0.9 0.2 add_and_fusion
  1.2 0.6 copy-done
  1.8 1.3 %copy-done.1 = bf16[64,2,5504]{2,1,0:T(2,128)(2,1)S(1)} copy-done((bf16[64,2,5504]{2,1,0:T(2,128)(2,1)S(1)}, bf16[64,2,5504]{2,1,0:T(2,128)(2,1)}, u32[]{:S(2)}) %copy-start.1) | copy-done | bytes 1409048
  3.2 0.7 copy-done.3
  3.9 4.6 %shard_map.77 = (bf16[1024,128]{1,0:T(8,128)(2,1)S(1)}, bf16[1024,128]{1,0:T(8,128)(2,1)S(1)}, bf16[1024,128]{1,0:T(8,128)(2,1)S(1)}, bf16[1024,128]{1,0:T(8,128)(2,1)S(1)}) custom-call(s32[4]{0:T(128)S(1)} %copy-done, bf16[5504,128]{1,0:T(8,128)(2,1)S(1)} %bitcast.22, f32[12,128]{1,0:T(8,128)S(1)} %bitcast.23, f32[8,128]{1,0:T(8,128)S(1)} %broadcast_in_dim.10.turn_cos, ...), custom_call_target="tpu_custom_call" | custom-call | flops 3221225472 | bytes 4194304 | tf_op jit(solution)/shard_map/pallas_call | solution.py:205
  8.4 3.0 %collective-permute-start.1 = (bf16[1024,128]{1,0:T(8,128)(2,1)S(1)}, bf16[1024,128]{1,0:T(8,128)(2,1)S(1)}, u32[]{:S(2)}, u32[]{:S(2)}) collective-permute-start(bf16[1024,128]{1,0:T(8,128)(2,1)S(1)} %get-tuple-element.19.refs_0_), channel_id=1, source_target_pairs={{0,2},{1,3},{2,0},{3,1},{4,6},{5,7},{6,4},{7,5},{8,10},{9,11},{10,... | collective-permute-start | bytes 786440 | tf_op jit(solution)/shard_map/ppermute | solution.py:529
  11.5 1.6 %collective-permute-start = (bf16[1024,128]{1,0:T(8,128)(2,1)S(1)}, bf16[1024,128]{1,0:T(8,128)(2,1)S(1)}, u32[]{:S(2)}, u32[]{:S(2)}) collective-permute-start(bf16[1024,128]{1,0:T(8,128)(2,1)S(1)} %get-tuple-element.15), channel_id=1, source_target_pairs={{0,4},{4,0},{8,12},{12,8},{1,5},{5,1},{9,13},{13,9},{2,6},{6,2},{1... | collective-permute-start | bytes 786440 | tf_op jit(solution)/shard_map/ppermute | solution.py:529
  13.0 2.6 %collective-permute-start.7 = (bf16[1024,128]{1,0:T(8,128)(2,1)S(1)}, bf16[1024,128]{1,0:T(8,128)(2,1)S(1)}, u32[]{:S(2)}, u32[]{:S(2)}) collective-permute-start(bf16[1024,128]{1,0:T(8,128)(2,1)S(1)} %get-tuple-element.21), channel_id=1, source_target_pairs={{0,8},{4,12},{8,0},{12,4},{1,9},{5,13},{9,1},{13,5},{2,10},{6,14},... | collective-permute-start | bytes 786440 | tf_op jit(solution)/shard_map/ppermute | solution.py:529
  15.6 0.2 collective-permute-start.11
  15.9 0.2 convert_reduce_fusion
  16.1 0.1 multiply_add_fusion
  16.2 0.1 pad_add_fusion.place
  16.3 0.1 add.66
  16.4 0.1 add.68
  16.6 0.1 fusion.choose
  16.7 8.7 %collective-permute-done.refs_4_ = bf16[1024,128]{1,0:T(8,128)(2,1)S(1)} collective-permute-done((bf16[1024,128]{1,0:T(8,128)(2,1)S(1)}, bf16[1024,128]{1,0:T(8,128)(2,1)S(1)}, u32[]{:S(2)}, u32[]{:S(2)}) %collective-permute-start) | collective-permute-done | bytes 262176 | tf_op jit(solution)/shard_map/ppermute | solution.py:529
  25.4 0.4 collective-permute-start.4
  25.8 0.2 collective-permute-start.5
  26.0 8.4 %collective-permute-done.7.refs_8_ = bf16[1024,128]{1,0:T(8,128)(2,1)S(1)} collective-permute-done((bf16[1024,128]{1,0:T(8,128)(2,1)S(1)}, bf16[1024,128]{1,0:T(8,128)(2,1)S(1)}, u32[]{:S(2)}, u32[]{:S(2)}) %collective-permute-start.7) | collective-permute-done | bytes 262176 | tf_op jit(solution)/shard_map/ppermute | solution.py:529
  34.4 0.5 collective-permute-start.8
  34.9 1.5 %collective-permute-start.12 = (bf16[1024,128]{1,0:T(8,128)(2,1)S(1)}, bf16[1024,128]{1,0:T(8,128)(2,1)S(1)}, u32[]{:S(2)}, u32[]{:S(2)}) collective-permute-start(bf16[1024,128]{1,0:T(8,128)(2,1)S(1)} %collective-permute-done.11.refs_12_), channel_id=1, source_target_pairs={{0,2},{1,3},{2,0},{3,1},{4,6},{5,7},{6,4},{7,5},{8,10},{9,11},{10,... | collective-permute-start | bytes 786440 | tf_op jit(solution)/shard_map/ppermute | solution.py:529
  36.4 0.5 collective-permute-start.13
  37.0 5.6 %collective-permute-done.8.refs_9_ = bf16[1024,128]{1,0:T(8,128)(2,1)S(1)} collective-permute-done((bf16[1024,128]{1,0:T(8,128)(2,1)S(1)}, bf16[1024,128]{1,0:T(8,128)(2,1)S(1)}, u32[]{:S(2)}, u32[]{:S(2)}) %collective-permute-start.8) | collective-permute-done | bytes 262176 | tf_op jit(solution)/shard_map/ppermute | solution.py:529
  42.5 2.8 %collective-permute-done.12.refs_13_ = bf16[1024,128]{1,0:T(8,128)(2,1)S(1)} collective-permute-done((bf16[1024,128]{1,0:T(8,128)(2,1)S(1)}, bf16[1024,128]{1,0:T(8,128)(2,1)S(1)}, u32[]{:S(2)}, u32[]{:S(2)}) %collective-permute-start.12) | collective-permute-done | bytes 262176 | tf_op jit(solution)/shard_map/ppermute | solution.py:529
  45.4 1.5 %collective-permute-done.14.refs_15_ = bf16[1024,128]{1,0:T(8,128)(2,1)S(1)} collective-permute-done((bf16[1024,128]{1,0:T(8,128)(2,1)S(1)}, bf16[1024,128]{1,0:T(8,128)(2,1)S(1)}, u32[]{:S(2)}, u32[]{:S(2)}) %collective-permute-start.14) | collective-permute-done | bytes 262176 | tf_op jit(solution)/shard_map/ppermute | solution.py:529
  46.9 11.3 %shard_map.78 = (bf16[32,64,1024]{2,1,0:T(8,128)(2,1)}, bf16[512,128]{1,0:T(8,128)(2,1)S(1)}, bf16[512,128]{1,0:T(8,128)(2,1)S(1)}, bf16[512,128]{1,0:T(8,128)(2,1)S(1)}, bf16[512,128]{1,0:T(8,128)(2,1)S(1)}) custom-call(s32[3]{0:T(128)S(1)} %pad_add_fusion.place, s32[64,1024]{1,0:T(8,128)S(1)} %copy-done.2, f32[8,128]{1,0:T(8,128)S(1)} %broadcast_in_dim.10.turn_cos, ...), custom_call_target="tpu_custom_call" | custom-call | flops 4294967296 | bytes 25165824 | tf_op jit(solution)/shard_map/pallas_call | solution.py:361
  58.2 2.2 %collective-permute-start.15 = (bf16[512,128]{1,0:T(8,128)(2,1)S(1)}, bf16[512,128]{1,0:T(8,128)(2,1)S(1)}, u32[]{:S(2)}, u32[]{:S(2)}) collective-permute-start(bf16[512,128]{1,0:T(8,128)(2,1)S(1)} %get-tuple-element.25), channel_id=1, source_target_pairs={{0,4},{4,0},{8,12},{12,8},{1,5},{5,1},{9,13},{13,9},{2,6},{6,2},{1... | collective-permute-start | bytes 393224 | tf_op jit(solution)/shard_map/ppermute | solution.py:529
  60.4 2.5 %collective-permute-start.16 = (bf16[512,128]{1,0:T(8,128)(2,1)S(1)}, bf16[512,128]{1,0:T(8,128)(2,1)S(1)}, u32[]{:S(2)}, u32[]{:S(2)}) collective-permute-start(bf16[512,128]{1,0:T(8,128)(2,1)S(1)} %get-tuple-element.26), channel_id=1, source_target_pairs={{0,8},{4,12},{8,0},{12,4},{1,9},{5,13},{9,1},{13,5},{2,10},{6,14},... | collective-permute-start | bytes 393224 | tf_op jit(solution)/shard_map/ppermute | solution.py:529
  62.8 14.6 %shard_map.79 = bf16[32,2,256,1024]{3,2,1,0:T(8,128)(2,1)} custom-call(s32[1]{0:T(128)} %bitcast.sub_index, s32[4]{0:T(128)} %counts.3, bf16[32,64,1024]{2,1,0:T(8,128)(2,1)} %get-tuple-element.23.mine.by_id, bf16[32,64,1024]{2,1,0:T(8,128)(2,1)} %get-tuple-element.23.mine.by_id), custom_call_target="tpu_custom_call" | custom-call | flops 2147483648 | bytes 33554432 | tf_op jit(solution)/shard_map/pallas_call | solution.py:436
  77.4 3.7 %shard_map.80 = f32[2752,128]{1,0:T(8,128)} custom-call(f32[12,128]{1,0:T(8,128)S(1)} %bitcast.24, f32[8,128]{1,0:T(8,128)S(1)} %broadcast_in_dim.10.turn_cos, s32[256,256]{1,0:T(8,128)S(1)} %get-tuple-element.28.index, bf16[512,128]{1,0:T(8,128)(2,1)S(1)} %get-tuple-element.24.refs_0_, bf16[512,128]{1,0:T(8,128)(2,1)S(1)} %collective-permute-done.15.refs_1_, ...), custom_call_target="tpu_custom_call" | custom-call | flops 2164260864 | bytes 4194304 | tf_op jit(solution)/shard_map/pallas_call | solution.py:510
  (43 shorter events, 0.5 us)
Async XLA Ops:
  1.2 0.7 copy-start
  1.8 1.4 %copy-start.1 = (bf16[64,2,5504]{2,1,0:T(2,128)(2,1)S(1)}, bf16[64,2,5504]{2,1,0:T(2,128)(2,1)}, u32[]{:S(2)}) copy-start(bf16[64,2,5504]{2,1,0:T(2,128)(2,1)} %param.6) | copy-start | bytes 4227076
  3.2 0.7 copy-start.3
  3.9 12.0 %copy-start.6 = (s32[256,1]{0,1:T(1,128)S(1)}, s32[256,1]{0,1:T(1,128)}, u32[]{:S(2)}) copy-start(s32[256,1]{0,1:T(1,128)} %param.11) | copy-start | bytes 3076
  3.9 12.6 %copy-start.5 = (s32[1024]{0:T(1024)S(1)}, s32[1024]{0:T(1024)}, u32[]{:S(2)}) copy-start(s32[1024]{0:T(1024)} %param.8) | copy-start | bytes 12292
  3.9 43.0 %copy-start.2 = (s32[64,1024]{1,0:T(8,128)S(1)}, s32[64,1024]{1,0:T(8,128)}, u32[]{:S(2)}) copy-start(s32[64,1024]{1,0:T(8,128)} %delays.1) | copy-start | bytes 786436
  8.4 16.9 %collective-permute-start.1 = (bf16[1024,128]{1,0:T(8,128)(2,1)S(1)}, bf16[1024,128]{1,0:T(8,128)(2,1)S(1)}, u32[]{:S(2)}, u32[]{:S(2)}) collective-permute-start(bf16[1024,128]{1,0:T(8,128)(2,1)S(1)} %get-tuple-element.19.refs_0_), channel_id=1, source_target_pairs={{0,2},{1,3},{2,0},{3,1},{4,6},{5,7},{6,4},{7,5},{8,10},{9,11},{10,... | collective-permute-start | bytes 786440 | tf_op jit(solution)/shard_map/ppermute | solution.py:529
  11.5 14.3 %collective-permute-start.2 = (bf16[1024,128]{1,0:T(8,128)(2,1)S(1)}, bf16[1024,128]{1,0:T(8,128)(2,1)S(1)}, u32[]{:S(2)}, u32[]{:S(2)}) collective-permute-start(bf16[1024,128]{1,0:T(8,128)(2,1)S(1)} %get-tuple-element.19.refs_0_), channel_id=1, source_target_pairs={{0,1},{1,0},{2,3},{3,2},{4,5},{5,4},{6,7},{7,6},{8,9},{9,8},{10,11... | collective-permute-start | bytes 786440 | tf_op jit(solution)/shard_map/ppermute | solution.py:529
  11.5 13.9 %collective-permute-start = (bf16[1024,128]{1,0:T(8,128)(2,1)S(1)}, bf16[1024,128]{1,0:T(8,128)(2,1)S(1)}, u32[]{:S(2)}, u32[]{:S(2)}) collective-permute-start(bf16[1024,128]{1,0:T(8,128)(2,1)S(1)} %get-tuple-element.15), channel_id=1, source_target_pairs={{0,4},{4,0},{8,12},{12,8},{1,5},{5,1},{9,13},{13,9},{2,6},{6,2},{1... | collective-permute-start | bytes 786440 | tf_op jit(solution)/shard_map/ppermute | solution.py:529
  13.0 21.3 %collective-permute-start.7 = (bf16[1024,128]{1,0:T(8,128)(2,1)S(1)}, bf16[1024,128]{1,0:T(8,128)(2,1)S(1)}, u32[]{:S(2)}, u32[]{:S(2)}) collective-permute-start(bf16[1024,128]{1,0:T(8,128)(2,1)S(1)} %get-tuple-element.21), channel_id=1, source_target_pairs={{0,8},{4,12},{8,0},{12,4},{1,9},{5,13},{9,1},{13,5},{2,10},{6,14},... | collective-permute-start | bytes 786440 | tf_op jit(solution)/shard_map/ppermute | solution.py:529
  15.6 19.3 %collective-permute-start.11 = (bf16[1024,128]{1,0:T(8,128)(2,1)S(1)}, bf16[1024,128]{1,0:T(8,128)(2,1)S(1)}, u32[]{:S(2)}, u32[]{:S(2)}) collective-permute-start(bf16[1024,128]{1,0:T(8,128)(2,1)S(1)} %get-tuple-element.22), channel_id=1, source_target_pairs={{0,12},{4,8},{8,4},{12,0},{1,13},{5,9},{9,5},{13,1},{2,14},{6,10},... | collective-permute-start | bytes 786440 | tf_op jit(solution)/shard_map/ppermute | solution.py:529
  25.4 11.0 %collective-permute-start.3 = (bf16[1024,128]{1,0:T(8,128)(2,1)S(1)}, bf16[1024,128]{1,0:T(8,128)(2,1)S(1)}, u32[]{:S(2)}, u32[]{:S(2)}) collective-permute-start(bf16[1024,128]{1,0:T(8,128)(2,1)S(1)} %collective-permute-done.1.refs_1_), channel_id=1, source_target_pairs={{0,1},{1,0},{2,3},{3,2},{4,5},{5,4},{6,7},{7,6},{8,9},{9,8},{10,11... | collective-permute-start | bytes 786440 | tf_op jit(solution)/shard_map/ppermute | solution.py:529
  25.4 11.0 %collective-permute-start.4 = (bf16[1024,128]{1,0:T(8,128)(2,1)S(1)}, bf16[1024,128]{1,0:T(8,128)(2,1)S(1)}, u32[]{:S(2)}, u32[]{:S(2)}) collective-permute-start(bf16[1024,128]{1,0:T(8,128)(2,1)S(1)} %collective-permute-done.refs_4_), channel_id=1, source_target_pairs={{0,2},{1,3},{2,0},{3,1},{4,6},{5,7},{6,4},{7,5},{8,10},{9,11},{10,... | collective-permute-start | bytes 786440 | tf_op jit(solution)/shard_map/ppermute | solution.py:529
  25.8 11.1 %collective-permute-start.5 = (bf16[1024,128]{1,0:T(8,128)(2,1)S(1)}, bf16[1024,128]{1,0:T(8,128)(2,1)S(1)}, u32[]{:S(2)}, u32[]{:S(2)}) collective-permute-start(bf16[1024,128]{1,0:T(8,128)(2,1)S(1)} %collective-permute-done.refs_4_), channel_id=1, source_target_pairs={{0,1},{1,0},{2,3},{3,2},{4,5},{5,4},{6,7},{7,6},{8,9},{9,8},{10,11... | collective-permute-start | bytes 786440 | tf_op jit(solution)/shard_map/ppermute | solution.py:529
  34.4 8.2 %collective-permute-start.8 = (bf16[1024,128]{1,0:T(8,128)(2,1)S(1)}, bf16[1024,128]{1,0:T(8,128)(2,1)S(1)}, u32[]{:S(2)}, u32[]{:S(2)}) collective-permute-start(bf16[1024,128]{1,0:T(8,128)(2,1)S(1)} %collective-permute-done.7.refs_8_), channel_id=1, source_target_pairs={{0,2},{1,3},{2,0},{3,1},{4,6},{5,7},{6,4},{7,5},{8,10},{9,11},{10,... | collective-permute-start | bytes 786440 | tf_op jit(solution)/shard_map/ppermute | solution.py:529
  34.9 10.4 %collective-permute-start.12 = (bf16[1024,128]{1,0:T(8,128)(2,1)S(1)}, bf16[1024,128]{1,0:T(8,128)(2,1)S(1)}, u32[]{:S(2)}, u32[]{:S(2)}) collective-permute-start(bf16[1024,128]{1,0:T(8,128)(2,1)S(1)} %collective-permute-done.11.refs_12_), channel_id=1, source_target_pairs={{0,2},{1,3},{2,0},{3,1},{4,6},{5,7},{6,4},{7,5},{8,10},{9,11},{10,... | collective-permute-start | bytes 786440 | tf_op jit(solution)/shard_map/ppermute | solution.py:529
  36.4 9.0 %collective-permute-start.9 = (bf16[1024,128]{1,0:T(8,128)(2,1)S(1)}, bf16[1024,128]{1,0:T(8,128)(2,1)S(1)}, u32[]{:S(2)}, u32[]{:S(2)}) collective-permute-start(bf16[1024,128]{1,0:T(8,128)(2,1)S(1)} %collective-permute-done.7.refs_8_), channel_id=1, source_target_pairs={{0,1},{1,0},{2,3},{3,2},{4,5},{5,4},{6,7},{7,6},{8,9},{9,8},{10,11... | collective-permute-start | bytes 786440 | tf_op jit(solution)/shard_map/ppermute | solution.py:529
  36.4 9.0 %collective-permute-start.13 = (bf16[1024,128]{1,0:T(8,128)(2,1)S(1)}, bf16[1024,128]{1,0:T(8,128)(2,1)S(1)}, u32[]{:S(2)}, u32[]{:S(2)}) collective-permute-start(bf16[1024,128]{1,0:T(8,128)(2,1)S(1)} %collective-permute-done.11.refs_12_), channel_id=1, source_target_pairs={{0,1},{1,0},{2,3},{3,2},{4,5},{5,4},{6,7},{7,6},{8,9},{9,8},{10,11... | collective-permute-start | bytes 786440 | tf_op jit(solution)/shard_map/ppermute | solution.py:529
  36.9 8.5 %collective-permute-start.6 = (bf16[1024,128]{1,0:T(8,128)(2,1)S(1)}, bf16[1024,128]{1,0:T(8,128)(2,1)S(1)}, u32[]{:S(2)}, u32[]{:S(2)}) collective-permute-start(bf16[1024,128]{1,0:T(8,128)(2,1)S(1)} %collective-permute-done.4.refs_5_), channel_id=1, source_target_pairs={{0,1},{1,0},{2,3},{3,2},{4,5},{5,4},{6,7},{7,6},{8,9},{9,8},{10,11... | collective-permute-start | bytes 786440 | tf_op jit(solution)/shard_map/ppermute | solution.py:529
  42.5 2.8 %collective-permute-start.10 = (bf16[1024,128]{1,0:T(8,128)(2,1)S(1)}, bf16[1024,128]{1,0:T(8,128)(2,1)S(1)}, u32[]{:S(2)}, u32[]{:S(2)}) collective-permute-start(bf16[1024,128]{1,0:T(8,128)(2,1)S(1)} %collective-permute-done.8.refs_9_), channel_id=1, source_target_pairs={{0,1},{1,0},{2,3},{3,2},{4,5},{5,4},{6,7},{7,6},{8,9},{9,8},{10,11... | collective-permute-start | bytes 786440 | tf_op jit(solution)/shard_map/ppermute | solution.py:529
  45.3 1.5 %collective-permute-start.14 = (bf16[1024,128]{1,0:T(8,128)(2,1)S(1)}, bf16[1024,128]{1,0:T(8,128)(2,1)S(1)}, u32[]{:S(2)}, u32[]{:S(2)}) collective-permute-start(bf16[1024,128]{1,0:T(8,128)(2,1)S(1)} %collective-permute-done.12.refs_13_), channel_id=1, source_target_pairs={{0,1},{1,0},{2,3},{3,2},{4,5},{5,4},{6,7},{7,6},{8,9},{9,8},{10,11... | collective-permute-start | bytes 786440 | tf_op jit(solution)/shard_map/ppermute | solution.py:529
  58.2 19.2 %collective-permute-start.15 = (bf16[512,128]{1,0:T(8,128)(2,1)S(1)}, bf16[512,128]{1,0:T(8,128)(2,1)S(1)}, u32[]{:S(2)}, u32[]{:S(2)}) collective-permute-start(bf16[512,128]{1,0:T(8,128)(2,1)S(1)} %get-tuple-element.25), channel_id=1, source_target_pairs={{0,4},{4,0},{8,12},{12,8},{1,5},{5,1},{9,13},{13,9},{2,6},{6,2},{1... | collective-permute-start | bytes 393224 | tf_op jit(solution)/shard_map/ppermute | solution.py:529
  60.4 17.1 %collective-permute-start.16 = (bf16[512,128]{1,0:T(8,128)(2,1)S(1)}, bf16[512,128]{1,0:T(8,128)(2,1)S(1)}, u32[]{:S(2)}, u32[]{:S(2)}) collective-permute-start(bf16[512,128]{1,0:T(8,128)(2,1)S(1)} %get-tuple-element.26), channel_id=1, source_target_pairs={{0,8},{4,12},{8,0},{12,4},{1,9},{5,13},{9,1},{13,5},{2,10},{6,14},... | collective-permute-start | bytes 393224 | tf_op jit(solution)/shard_map/ppermute | solution.py:529
  62.8 14.6 %collective-permute-start.17 = (bf16[512,128]{1,0:T(8,128)(2,1)S(1)}, bf16[512,128]{1,0:T(8,128)(2,1)S(1)}, u32[]{:S(2)}, u32[]{:S(2)}) collective-permute-start(bf16[512,128]{1,0:T(8,128)(2,1)S(1)} %get-tuple-element.27), channel_id=1, source_target_pairs={{0,12},{4,8},{8,4},{12,0},{1,13},{5,9},{9,5},{13,1},{2,14},{6,10},... | collective-permute-start | bytes 393224 | tf_op jit(solution)/shard_map/ppermute | solution.py:529
  62.8 14.6 %copy-start.4 = (f32[1536]{0:T(1024)S(1)}, f32[1536]{0:T(1024)}, u32[]{:S(2)}) copy-start(f32[1536]{0:T(1024)} %param.7) | copy-start | bytes 18436

commit v4 on v3

--- a/solution.py
+++ b/solution.py
@@ -152,7 +152,9 @@
 
 
 def filter_kernel(inp, group, spectra_n, pieces, counts, voltages, taps, turn_cos, index, *rest):
-    *flat, table, wide, frames = rest
+    *flat, table, wide, frames, near, sem = rest
+    fetch = pltpu.make_async_copy(voltages, near, sem)
+    fetch.start()
     outs = nested(flat, pieces)
     depth = index.shape[0]
     frames_n = spectra_n + TAPS - 1
@@ -163,7 +165,8 @@
         table[k * depth : (k + 1) * depth, :] = (tall[:, k : k + 1] * base).astype(
             jnp.bfloat16
         )
-    wide[...] = voltages[...].astype(jnp.float32)
+    fetch.wait()
+    wide[...] = near[...].astype(jnp.float32)
     for s in range(frames_n):
         for c in range(2):
             frames[s * inp : (s + 1) * inp, c * NCH : (c + 1) * NCH] = wide[
@@ -209,12 +212,15 @@
             for many in pieces
             for _ in range(many)
         ],
-        in_specs=[SCALARS] + [pl.BlockSpec(memory_space=pltpu.VMEM)] * 4,
+        in_specs=[SCALARS, pl.BlockSpec(memory_space=pltpu.HBM)]
+        + [pl.BlockSpec(memory_space=pltpu.VMEM)] * 3,
         out_specs=[pl.BlockSpec(memory_space=pltpu.VMEM)] * sum(pieces),
         scratch_shapes=[
             pltpu.VMEM((TAPS * depth, columns), jnp.bfloat16),
             pltpu.VMEM(voltages.shape, jnp.float32),
             pltpu.VMEM((voltages.shape[0] // 2, 2 * NCH), jnp.bfloat16),
+            pltpu.VMEM(voltages.shape, jnp.bfloat16),
+            pltpu.SemaphoreType.DMA,
         ],
         compiler_params=pltpu.CompilerParams(vmem_limit_bytes=36 * MIB),
         cost_estimate=pl.CostEstimate(

time: 81.5 us -> 81.9 us (level)
  no operation moved by 1% of the time
where the time goes in v4:
time: 81.9 us; the launch traced here: 81.5 us
  Pallas kernels  34.4 us (42%)
  waiting for transfers between devices  26.9 us (33%)
  starting transfers between devices  15.3 us (19%)
  local copies, waits for them, and re-layouts  3.29 us (4%)
    ppermute x18, waiting for transfers between devices, swap(): return lax.ppermute(x, axis, [(i, i ^ mask) for i in range(size)])  26.9 us
    ppermute x18, starting transfers between devices, swap(): return lax.ppermute(x, axis, [(i, i ^ mask) for i in range(size)])  15.3 us
    pallas_call x1, Pallas kernels, run_visibility(): pl.pallas_call(functools.partial(visibility_kernel, first), out_shape=jax...  14.6 us
    pallas_call x1, Pallas kernels, run_beams(): pl.pallas_call(functools.partial(beam_kernel, (inp, ch_dev, spectra_n, mo...  11.3 us
    pallas_call x1, Pallas kernels, run_filter(): pl.pallas_call(functools.partial(filter_kernel, inp, 4, spectra_n, pieces...  4.93 us
    pallas_call x1, Pallas kernels, run_resynth(): pl.pallas_call(functools.partial(resynth_kernel, most, spectra_n), out_sh...  3.65 us
    unnamed x14, local copies, waits for them, and re-layouts  2.71 us
  transfers between devices with their start and end apart: 18, of which 5 were waited for; matrix products, arithmetic and copies ran while one was open for 1% of the time, Pallas kernels for 18%

profile of v4, /device:TPU:0, one launch (start us, length us, event | category | flops | bytes accessed | tf_op | source)
XLA Modules:
  0.0 81.5 jit_solution(9488492956707819179)
XLA Ops:
  0.7 0.1 sub.34
  0.9 0.1 add.61
  0.9 0.2 add_and_fusion
  1.2 0.6 copy-done
  1.8 1.3 %copy-done.1 = bf16[64,2,5504]{2,1,0:T(2,128)(2,1)S(1)} copy-done((bf16[64,2,5504]{2,1,0:T(2,128)(2,1)S(1)}, bf16[64,2,5504]{2,1,0:T(2,128)(2,1)}, u32[]{:S(2)}) %copy-start.1) | copy-done | bytes 1409048
  3.2 0.7 copy-done.3
  3.9 4.9 %shard_map.77 = (bf16[1024,128]{1,0:T(8,128)(2,1)S(1)}, bf16[1024,128]{1,0:T(8,128)(2,1)S(1)}, bf16[1024,128]{1,0:T(8,128)(2,1)S(1)}, bf16[1024,128]{1,0:T(8,128)(2,1)S(1)}) custom-call(s32[4]{0:T(128)S(1)} %copy-done, bf16[5504,128]{1,0:T(8,128)(2,1)S(1)} %bitcast.22, f32[12,128]{1,0:T(8,128)S(1)} %bitcast.23, f32[8,128]{1,0:T(8,128)S(1)} %broadcast_in_dim.10.turn_cos, ...), custom_call_target="tpu_custom_call" | custom-call | flops 3221225472 | bytes 4194304 | tf_op jit(solution)/shard_map/pallas_call | solution.py:208
  8.8 3.0 %collective-permute-start.1 = (bf16[1024,128]{1,0:T(8,128)(2,1)S(1)}, bf16[1024,128]{1,0:T(8,128)(2,1)S(1)}, u32[]{:S(2)}, u32[]{:S(2)}) collective-permute-start(bf16[1024,128]{1,0:T(8,128)(2,1)S(1)} %get-tuple-element.19.refs_0_), channel_id=1, source_target_pairs={{0,2},{1,3},{2,0},{3,1},{4,6},{5,7},{6,4},{7,5},{8,10},{9,11},{10,... | collective-permute-start | bytes 786440 | tf_op jit(solution)/shard_map/ppermute | solution.py:535
  11.8 1.6 %collective-permute-start = (bf16[1024,128]{1,0:T(8,128)(2,1)S(1)}, bf16[1024,128]{1,0:T(8,128)(2,1)S(1)}, u32[]{:S(2)}, u32[]{:S(2)}) collective-permute-start(bf16[1024,128]{1,0:T(8,128)(2,1)S(1)} %get-tuple-element.15), channel_id=1, source_target_pairs={{0,4},{4,0},{8,12},{12,8},{1,5},{5,1},{9,13},{13,9},{2,6},{6,2},{1... | collective-permute-start | bytes 786440 | tf_op jit(solution)/shard_map/ppermute | solution.py:535
  13.4 2.6 %collective-permute-start.7 = (bf16[1024,128]{1,0:T(8,128)(2,1)S(1)}, bf16[1024,128]{1,0:T(8,128)(2,1)S(1)}, u32[]{:S(2)}, u32[]{:S(2)}) collective-permute-start(bf16[1024,128]{1,0:T(8,128)(2,1)S(1)} %get-tuple-element.21), channel_id=1, source_target_pairs={{0,8},{4,12},{8,0},{12,4},{1,9},{5,13},{9,1},{13,5},{2,10},{6,14},... | collective-permute-start | bytes 786440 | tf_op jit(solution)/shard_map/ppermute | solution.py:535
  16.0 0.2 collective-permute-start.11
  16.3 0.2 convert_reduce_fusion
  16.5 0.1 multiply_add_fusion
  16.6 0.1 pad_add_fusion.place
  16.7 0.1 add.66
  16.8 0.1 add.68
  17.0 0.1 fusion.choose
  17.1 8.7 %collective-permute-done.refs_4_ = bf16[1024,128]{1,0:T(8,128)(2,1)S(1)} collective-permute-done((bf16[1024,128]{1,0:T(8,128)(2,1)S(1)}, bf16[1024,128]{1,0:T(8,128)(2,1)S(1)}, u32[]{:S(2)}, u32[]{:S(2)}) %collective-permute-start) | collective-permute-done | bytes 262176 | tf_op jit(solution)/shard_map/ppermute | solution.py:535
  25.8 0.4 collective-permute-start.4
  26.1 0.2 collective-permute-start.5
  26.4 8.4 %collective-permute-done.7.refs_8_ = bf16[1024,128]{1,0:T(8,128)(2,1)S(1)} collective-permute-done((bf16[1024,128]{1,0:T(8,128)(2,1)S(1)}, bf16[1024,128]{1,0:T(8,128)(2,1)S(1)}, u32[]{:S(2)}, u32[]{:S(2)}) %collective-permute-start.7) | collective-permute-done | bytes 262176 | tf_op jit(solution)/shard_map/ppermute | solution.py:535
  34.7 0.5 collective-permute-start.8
  35.3 1.5 %collective-permute-start.12 = (bf16[1024,128]{1,0:T(8,128)(2,1)S(1)}, bf16[1024,128]{1,0:T(8,128)(2,1)S(1)}, u32[]{:S(2)}, u32[]{:S(2)}) collective-permute-start(bf16[1024,128]{1,0:T(8,128)(2,1)S(1)} %collective-permute-done.11.refs_12_), channel_id=1, source_target_pairs={{0,2},{1,3},{2,0},{3,1},{4,6},{5,7},{6,4},{7,5},{8,10},{9,11},{10,... | collective-permute-start | bytes 786440 | tf_op jit(solution)/shard_map/ppermute | solution.py:535
  36.8 0.5 collective-permute-start.13
  37.4 5.6 %collective-permute-done.8.refs_9_ = bf16[1024,128]{1,0:T(8,128)(2,1)S(1)} collective-permute-done((bf16[1024,128]{1,0:T(8,128)(2,1)S(1)}, bf16[1024,128]{1,0:T(8,128)(2,1)S(1)}, u32[]{:S(2)}, u32[]{:S(2)}) %collective-permute-start.8) | collective-permute-done | bytes 262176 | tf_op jit(solution)/shard_map/ppermute | solution.py:535
  42.9 2.8 %collective-permute-done.12.refs_13_ = bf16[1024,128]{1,0:T(8,128)(2,1)S(1)} collective-permute-done((bf16[1024,128]{1,0:T(8,128)(2,1)S(1)}, bf16[1024,128]{1,0:T(8,128)(2,1)S(1)}, u32[]{:S(2)}, u32[]{:S(2)}) %collective-permute-start.12) | collective-permute-done | bytes 262176 | tf_op jit(solution)/shard_map/ppermute | solution.py:535
  45.7 1.5 %collective-permute-done.14.refs_15_ = bf16[1024,128]{1,0:T(8,128)(2,1)S(1)} collective-permute-done((bf16[1024,128]{1,0:T(8,128)(2,1)S(1)}, bf16[1024,128]{1,0:T(8,128)(2,1)S(1)}, u32[]{:S(2)}, u32[]{:S(2)}) %collective-permute-start.14) | collective-permute-done | bytes 262176 | tf_op jit(solution)/shard_map/ppermute | solution.py:535
  47.3 11.3 %shard_map.78 = (bf16[32,64,1024]{2,1,0:T(8,128)(2,1)}, bf16[512,128]{1,0:T(8,128)(2,1)S(1)}, bf16[512,128]{1,0:T(8,128)(2,1)S(1)}, bf16[512,128]{1,0:T(8,128)(2,1)S(1)}, bf16[512,128]{1,0:T(8,128)(2,1)S(1)}) custom-call(s32[3]{0:T(128)S(1)} %pad_add_fusion.place, s32[64,1024]{1,0:T(8,128)S(1)} %copy-done.2, f32[8,128]{1,0:T(8,128)S(1)} %broadcast_in_dim.10.turn_cos, ...), custom_call_target="tpu_custom_call" | custom-call | flops 4294967296 | bytes 25165824 | tf_op jit(solution)/shard_map/pallas_call | solution.py:367
  58.5 2.2 %collective-permute-start.15 = (bf16[512,128]{1,0:T(8,128)(2,1)S(1)}, bf16[512,128]{1,0:T(8,128)(2,1)S(1)}, u32[]{:S(2)}, u32[]{:S(2)}) collective-permute-start(bf16[512,128]{1,0:T(8,128)(2,1)S(1)} %get-tuple-element.25), channel_id=1, source_target_pairs={{0,4},{4,0},{8,12},{12,8},{1,5},{5,1},{9,13},{13,9},{2,6},{6,2},{1... | collective-permute-start | bytes 393224 | tf_op jit(solution)/shard_map/ppermute | solution.py:535
  60.7 2.5 %collective-permute-start.16 = (bf16[512,128]{1,0:T(8,128)(2,1)S(1)}, bf16[512,128]{1,0:T(8,128)(2,1)S(1)}, u32[]{:S(2)}, u32[]{:S(2)}) collective-permute-start(bf16[512,128]{1,0:T(8,128)(2,1)S(1)} %get-tuple-element.26), channel_id=1, source_target_pairs={{0,8},{4,12},{8,0},{12,4},{1,9},{5,13},{9,1},{13,5},{2,10},{6,14},... | collective-permute-start | bytes 393224 | tf_op jit(solution)/shard_map/ppermute | solution.py:535
  63.2 14.6 %shard_map.79 = bf16[32,2,256,1024]{3,2,1,0:T(8,128)(2,1)} custom-call(s32[1]{0:T(128)} %bitcast.sub_index, s32[4]{0:T(128)} %counts.3, bf16[32,64,1024]{2,1,0:T(8,128)(2,1)} %get-tuple-element.23.mine.by_id, bf16[32,64,1024]{2,1,0:T(8,128)(2,1)} %get-tuple-element.23.mine.by_id), custom_call_target="tpu_custom_call" | custom-call | flops 2147483648 | bytes 33554432 | tf_op jit(solution)/shard_map/pallas_call | solution.py:442
  77.8 3.7 %shard_map.80 = f32[2752,128]{1,0:T(8,128)} custom-call(f32[12,128]{1,0:T(8,128)S(1)} %bitcast.24, f32[8,128]{1,0:T(8,128)S(1)} %broadcast_in_dim.10.turn_cos, s32[256,256]{1,0:T(8,128)S(1)} %get-tuple-element.28.index, bf16[512,128]{1,0:T(8,128)(2,1)S(1)} %get-tuple-element.24.refs_0_, bf16[512,128]{1,0:T(8,128)(2,1)S(1)} %collective-permute-done.15.refs_1_, ...), custom_call_target="tpu_custom_call" | custom-call | flops 2164260864 | bytes 4194304 | tf_op jit(solution)/shard_map/pallas_call | solution.py:516
  (43 shorter events, 0.5 us)
Async XLA Ops:
  1.2 0.7 copy-start
  1.8 1.4 %copy-start.1 = (bf16[64,2,5504]{2,1,0:T(2,128)(2,1)S(1)}, bf16[64,2,5504]{2,1,0:T(2,128)(2,1)}, u32[]{:S(2)}) copy-start(bf16[64,2,5504]{2,1,0:T(2,128)(2,1)} %param.6) | copy-start | bytes 4227076
  3.2 0.7 copy-start.3
  3.9 12.3 %copy-start.6 = (s32[256,1]{0,1:T(1,128)S(1)}, s32[256,1]{0,1:T(1,128)}, u32[]{:S(2)}) copy-start(s32[256,1]{0,1:T(1,128)} %param.11) | copy-start | bytes 3076
  3.9 13.0 %copy-start.5 = (s32[1024]{0:T(1024)S(1)}, s32[1024]{0:T(1024)}, u32[]{:S(2)}) copy-start(s32[1024]{0:T(1024)} %param.8) | copy-start | bytes 12292
  3.9 43.4 %copy-start.2 = (s32[64,1024]{1,0:T(8,128)S(1)}, s32[64,1024]{1,0:T(8,128)}, u32[]{:S(2)}) copy-start(s32[64,1024]{1,0:T(8,128)} %delays.1) | copy-start | bytes 786436
  8.8 16.9 %collective-permute-start.1 = (bf16[1024,128]{1,0:T(8,128)(2,1)S(1)}, bf16[1024,128]{1,0:T(8,128)(2,1)S(1)}, u32[]{:S(2)}, u32[]{:S(2)}) collective-permute-start(bf16[1024,128]{1,0:T(8,128)(2,1)S(1)} %get-tuple-element.19.refs_0_), channel_id=1, source_target_pairs={{0,2},{1,3},{2,0},{3,1},{4,6},{5,7},{6,4},{7,5},{8,10},{9,11},{10,... | collective-permute-start | bytes 786440 | tf_op jit(solution)/shard_map/ppermute | solution.py:535
  11.8 14.3 %collective-permute-start.2 = (bf16[1024,128]{1,0:T(8,128)(2,1)S(1)}, bf16[1024,128]{1,0:T(8,128)(2,1)S(1)}, u32[]{:S(2)}, u32[]{:S(2)}) collective-permute-start(bf16[1024,128]{1,0:T(8,128)(2,1)S(1)} %get-tuple-element.19.refs_0_), channel_id=1, source_target_pairs={{0,1},{1,0},{2,3},{3,2},{4,5},{5,4},{6,7},{7,6},{8,9},{9,8},{10,11... | collective-permute-start | bytes 786440 | tf_op jit(solution)/shard_map/ppermute | solution.py:535
  11.8 13.9 %collective-permute-start = (bf16[1024,128]{1,0:T(8,128)(2,1)S(1)}, bf16[1024,128]{1,0:T(8,128)(2,1)S(1)}, u32[]{:S(2)}, u32[]{:S(2)}) collective-permute-start(bf16[1024,128]{1,0:T(8,128)(2,1)S(1)} %get-tuple-element.15), channel_id=1, source_target_pairs={{0,4},{4,0},{8,12},{12,8},{1,5},{5,1},{9,13},{13,9},{2,6},{6,2},{1... | collective-permute-start | bytes 786440 | tf_op jit(solution)/shard_map/ppermute | solution.py:535
  13.4 21.3 %collective-permute-start.7 = (bf16[1024,128]{1,0:T(8,128)(2,1)S(1)}, bf16[1024,128]{1,0:T(8,128)(2,1)S(1)}, u32[]{:S(2)}, u32[]{:S(2)}) collective-permute-start(bf16[1024,128]{1,0:T(8,128)(2,1)S(1)} %get-tuple-element.21), channel_id=1, source_target_pairs={{0,8},{4,12},{8,0},{12,4},{1,9},{5,13},{9,1},{13,5},{2,10},{6,14},... | collective-permute-start | bytes 786440 | tf_op jit(solution)/shard_map/ppermute | solution.py:535
  16.0 19.3 %collective-permute-start.11 = (bf16[1024,128]{1,0:T(8,128)(2,1)S(1)}, bf16[1024,128]{1,0:T(8,128)(2,1)S(1)}, u32[]{:S(2)}, u32[]{:S(2)}) collective-permute-start(bf16[1024,128]{1,0:T(8,128)(2,1)S(1)} %get-tuple-element.22), channel_id=1, source_target_pairs={{0,12},{4,8},{8,4},{12,0},{1,13},{5,9},{9,5},{13,1},{2,14},{6,10},... | collective-permute-start | bytes 786440 | tf_op jit(solution)/shard_map/ppermute | solution.py:535
  25.8 11.0 %collective-permute-start.3 = (bf16[1024,128]{1,0:T(8,128)(2,1)S(1)}, bf16[1024,128]{1,0:T(8,128)(2,1)S(1)}, u32[]{:S(2)}, u32[]{:S(2)}) collective-permute-start(bf16[1024,128]{1,0:T(8,128)(2,1)S(1)} %collective-permute-done.1.refs_1_), channel_id=1, source_target_pairs={{0,1},{1,0},{2,3},{3,2},{4,5},{5,4},{6,7},{7,6},{8,9},{9,8},{10,11... | collective-permute-start | bytes 786440 | tf_op jit(solution)/shard_map/ppermute | solution.py:535
  25.8 11.0 %collective-permute-start.4 = (bf16[1024,128]{1,0:T(8,128)(2,1)S(1)}, bf16[1024,128]{1,0:T(8,128)(2,1)S(1)}, u32[]{:S(2)}, u32[]{:S(2)}) collective-permute-start(bf16[1024,128]{1,0:T(8,128)(2,1)S(1)} %collective-permute-done.refs_4_), channel_id=1, source_target_pairs={{0,2},{1,3},{2,0},{3,1},{4,6},{5,7},{6,4},{7,5},{8,10},{9,11},{10,... | collective-permute-start | bytes 786440 | tf_op jit(solution)/shard_map/ppermute | solution.py:535
  26.1 11.1 %collective-permute-start.5 = (bf16[1024,128]{1,0:T(8,128)(2,1)S(1)}, bf16[1024,128]{1,0:T(8,128)(2,1)S(1)}, u32[]{:S(2)}, u32[]{:S(2)}) collective-permute-start(bf16[1024,128]{1,0:T(8,128)(2,1)S(1)} %collective-permute-done.refs_4_), channel_id=1, source_target_pairs={{0,1},{1,0},{2,3},{3,2},{4,5},{5,4},{6,7},{7,6},{8,9},{9,8},{10,11... | collective-permute-start | bytes 786440 | tf_op jit(solution)/shard_map/ppermute | solution.py:535
  34.7 8.2 %collective-permute-start.8 = (bf16[1024,128]{1,0:T(8,128)(2,1)S(1)}, bf16[1024,128]{1,0:T(8,128)(2,1)S(1)}, u32[]{:S(2)}, u32[]{:S(2)}) collective-permute-start(bf16[1024,128]{1,0:T(8,128)(2,1)S(1)} %collective-permute-done.7.refs_8_), channel_id=1, source_target_pairs={{0,2},{1,3},{2,0},{3,1},{4,6},{5,7},{6,4},{7,5},{8,10},{9,11},{10,... | collective-permute-start | bytes 786440 | tf_op jit(solution)/shard_map/ppermute | solution.py:535
  35.3 10.4 %collective-permute-start.12 = (bf16[1024,128]{1,0:T(8,128)(2,1)S(1)}, bf16[1024,128]{1,0:T(8,128)(2,1)S(1)}, u32[]{:S(2)}, u32[]{:S(2)}) collective-permute-start(bf16[1024,128]{1,0:T(8,128)(2,1)S(1)} %collective-permute-done.11.refs_12_), channel_id=1, source_target_pairs={{0,2},{1,3},{2,0},{3,1},{4,6},{5,7},{6,4},{7,5},{8,10},{9,11},{10,... | collective-permute-start | bytes 786440 | tf_op jit(solution)/shard_map/ppermute | solution.py:535
  36.8 9.0 %collective-permute-start.9 = (bf16[1024,128]{1,0:T(8,128)(2,1)S(1)}, bf16[1024,128]{1,0:T(8,128)(2,1)S(1)}, u32[]{:S(2)}, u32[]{:S(2)}) collective-permute-start(bf16[1024,128]{1,0:T(8,128)(2,1)S(1)} %collective-permute-done.7.refs_8_), channel_id=1, source_target_pairs={{0,1},{1,0},{2,3},{3,2},{4,5},{5,4},{6,7},{7,6},{8,9},{9,8},{10,11... | collective-permute-start | bytes 786440 | tf_op jit(solution)/shard_map/ppermute | solution.py:535
  36.8 9.0 %collective-permute-start.13 = (bf16[1024,128]{1,0:T(8,128)(2,1)S(1)}, bf16[1024,128]{1,0:T(8,128)(2,1)S(1)}, u32[]{:S(2)}, u32[]{:S(2)}) collective-permute-start(bf16[1024,128]{1,0:T(8,128)(2,1)S(1)} %collective-permute-done.11.refs_12_), channel_id=1, source_target_pairs={{0,1},{1,0},{2,3},{3,2},{4,5},{5,4},{6,7},{7,6},{8,9},{9,8},{10,11... | collective-permute-start | bytes 786440 | tf_op jit(solution)/shard_map/ppermute | solution.py:535
  37.3 8.5 %collective-permute-start.6 = (bf16[1024,128]{1,0:T(8,128)(2,1)S(1)}, bf16[1024,128]{1,0:T(8,128)(2,1)S(1)}, u32[]{:S(2)}, u32[]{:S(2)}) collective-permute-start(bf16[1024,128]{1,0:T(8,128)(2,1)S(1)} %collective-permute-done.4.refs_5_), channel_id=1, source_target_pairs={{0,1},{1,0},{2,3},{3,2},{4,5},{5,4},{6,7},{7,6},{8,9},{9,8},{10,11... | collective-permute-start | bytes 786440 | tf_op jit(solution)/shard_map/ppermute | solution.py:535
  42.9 2.8 %collective-permute-start.10 = (bf16[1024,128]{1,0:T(8,128)(2,1)S(1)}, bf16[1024,128]{1,0:T(8,128)(2,1)S(1)}, u32[]{:S(2)}, u32[]{:S(2)}) collective-permute-start(bf16[1024,128]{1,0:T(8,128)(2,1)S(1)} %collective-permute-done.8.refs_9_), channel_id=1, source_target_pairs={{0,1},{1,0},{2,3},{3,2},{4,5},{5,4},{6,7},{7,6},{8,9},{9,8},{10,11... | collective-permute-start | bytes 786440 | tf_op jit(solution)/shard_map/ppermute | solution.py:535
  45.7 1.5 %collective-permute-start.14 = (bf16[1024,128]{1,0:T(8,128)(2,1)S(1)}, bf16[1024,128]{1,0:T(8,128)(2,1)S(1)}, u32[]{:S(2)}, u32[]{:S(2)}) collective-permute-start(bf16[1024,128]{1,0:T(8,128)(2,1)S(1)} %collective-permute-done.12.refs_13_), channel_id=1, source_target_pairs={{0,1},{1,0},{2,3},{3,2},{4,5},{5,4},{6,7},{7,6},{8,9},{9,8},{10,11... | collective-permute-start | bytes 786440 | tf_op jit(solution)/shard_map/ppermute | solution.py:535
  58.5 19.2 %collective-permute-start.15 = (bf16[512,128]{1,0:T(8,128)(2,1)S(1)}, bf16[512,128]{1,0:T(8,128)(2,1)S(1)}, u32[]{:S(2)}, u32[]{:S(2)}) collective-permute-start(bf16[512,128]{1,0:T(8,128)(2,1)S(1)} %get-tuple-element.25), channel_id=1, source_target_pairs={{0,4},{4,0},{8,12},{12,8},{1,5},{5,1},{9,13},{13,9},{2,6},{6,2},{1... | collective-permute-start | bytes 393224 | tf_op jit(solution)/shard_map/ppermute | solution.py:535
  60.7 17.1 %collective-permute-start.16 = (bf16[512,128]{1,0:T(8,128)(2,1)S(1)}, bf16[512,128]{1,0:T(8,128)(2,1)S(1)}, u32[]{:S(2)}, u32[]{:S(2)}) collective-permute-start(bf16[512,128]{1,0:T(8,128)(2,1)S(1)} %get-tuple-element.26), channel_id=1, source_target_pairs={{0,8},{4,12},{8,0},{12,4},{1,9},{5,13},{9,1},{13,5},{2,10},{6,14},... | collective-permute-start | bytes 393224 | tf_op jit(solution)/shard_map/ppermute | solution.py:535
  63.2 14.6 %collective-permute-start.17 = (bf16[512,128]{1,0:T(8,128)(2,1)S(1)}, bf16[512,128]{1,0:T(8,128)(2,1)S(1)}, u32[]{:S(2)}, u32[]{:S(2)}) collective-permute-start(bf16[512,128]{1,0:T(8,128)(2,1)S(1)} %get-tuple-element.27), channel_id=1, source_target_pairs={{0,12},{4,8},{8,4},{12,0},{1,13},{5,9},{9,5},{13,1},{2,14},{6,10},... | collective-permute-start | bytes 393224 | tf_op jit(solution)/shard_map/ppermute | solution.py:535
  63.2 14.6 %copy-start.4 = (f32[1536]{0:T(1024)S(1)}, f32[1536]{0:T(1024)}, u32[]{:S(2)}) copy-start(f32[1536]{0:T(1024)} %param.7) | copy-start | bytes 18436
